TPU v7x, 32 devices: a whole 2x2x4 slice. The times are simulated.
32 devices in a mesh: row: 4 (over y, x), col: 8 (over z, core).
Axes of the slice: x: 2, y: 2, z: 4, core: 2. Of those that a mesh axis runs over, the one named last changes fastest.
Arguments:
- features: bfloat16 [8, 2048, 128], P('col'), may hold values from -6 to 6
- dst_features: bfloat16 [4096, 128], P(('row', 'col')), may hold values from -6 to 6
- w_self: bfloat16 [128, 256], replicated, may hold values from -0.5 to 0.5
- w_neigh: bfloat16 [128, 256], replicated, may hold values from -0.5 to 0.5
- cotangent: bfloat16 [4096, 256], P(('row', 'col')), may hold values from -6 to 6
- block_values: bfloat16 [4, 8, 32, 128, 128], P('row', 'col'), may hold values from -0.15625 to 0.15625
- block_rows: int32 [4, 8, 32], P('row', 'col'), may hold values from 0 to 7, as said below
- block_cols: int32 [4, 8, 32], P('row', 'col'), may hold values from 0 to 15
- block_counts: int32 [4, 8], P('row', 'col'), may hold values from 4 to 32, as said below
Outputs:
- output: bfloat16 [4096, 256], P(('row', 'col'))
- grad_w_self: float32 [128, 256], replicated
- grad_w_neigh: float32 [128, 256], replicated
- grad_features: float32 [8, 2048, 128], P('col', 'row')
Inputs may be any that keep to these rules, and one draw needn't show every extreme that they name: On one device the slots name distinct pairs of block_rows and block_cols, also in unused slots. `block_counts`: some device uses all 32 slots in every draw.
All inputs are finite; a program needn't handle non-finite values.
Results may differ from a plain program's by a relative error of at most 0.0052.
Values may be sent and summed in bfloat16 or wider, within the bound.
No kernel may reach another device: no remote copies, remote signals or barrier semaphores. Data moves between devices by JAX's collectives and lax.ppermute only.
A program may use at most 64 MiB of HBM per device.

v0:
```python
import math

import jax
import jax.numpy as jnp
from jax import lax
from jax.sharding import PartitionSpec as P


def slot_products(block_vals, source_table, slot_index, einsum_form):
    return jnp.einsum(
        einsum_form, block_vals, source_table[slot_index], preferred_element_type=jnp.float32
    )


def per_device(
    features,
    dst_features,
    w_self,
    w_neigh,
    cotangent,
    block_values,
    block_rows,
    block_cols,
    block_counts,
):
    block_size = block_values.shape[-1]
    feat_width = features.shape[-1]
    local_rows = dst_features.shape[0]
    col_total = lax.axis_size("col")
    slab_blocks = local_rows * col_total // block_size
    source_table = features.reshape(-1, block_size, feat_width)
    source_count = source_table.shape[0]
    block_vals = block_values[0, 0]
    row_ids = block_rows[0, 0]
    col_ids = block_cols[0, 0]
    live_count = block_counts[0, 0]
    slot_total = row_ids.shape[0]
    live_mask = jnp.arange(slot_total, dtype=jnp.int32) < live_count
    row_hits = (
        (row_ids[None, :] == jnp.arange(slab_blocks, dtype=jnp.int32)[:, None]) & live_mask[None, :]
    ).astype(jnp.float32)
    forward_terms = slot_products(block_vals, source_table, col_ids, "sij,sjf->sif")
    summed = jnp.einsum("rs,sif->rif", row_hits, forward_terms, precision=lax.Precision.HIGHEST)
    agg_sum = lax.psum_scatter(
        summed.reshape(local_rows * lax.axis_size("col"), feat_width),
        "col",
        scatter_dimension=0,
        tiled=True,
    )
    aggregate = agg_sum.astype(jnp.bfloat16)
    pre_act = jnp.dot(dst_features, w_self, preferred_element_type=jnp.float32) + jnp.dot(
        aggregate, w_neigh, preferred_element_type=jnp.float32
    )
    sigmoid_pre = jax.nn.sigmoid(pre_act)
    output = (pre_act * sigmoid_pre).astype(jnp.bfloat16)
    grad_pre = (
        cotangent.astype(jnp.float32) * sigmoid_pre * (1.0 + pre_act * (1.0 - sigmoid_pre))
    ).astype(jnp.bfloat16)
    node_total = local_rows * lax.axis_size("row") * col_total
    scale_factor = 1.0 / math.sqrt(node_total)
    self_grad = jnp.einsum("nf,nh->fh", dst_features, grad_pre, preferred_element_type=jnp.float32)
    neigh_grad = jnp.einsum("nf,nh->fh", aggregate, grad_pre, preferred_element_type=jnp.float32)
    self_sum, neigh_sum = lax.psum((self_grad, neigh_grad), ("row", "col"))
    local_grad = jnp.einsum(
        "nh,fh->nf", grad_pre, w_neigh, preferred_element_type=jnp.float32
    ).astype(jnp.bfloat16)
    slab_grad = lax.all_gather(local_grad, "col", axis=0, tiled=True)
    grad_table = slab_grad.reshape(slab_blocks, block_size, feat_width)
    backward_terms = slot_products(block_vals, grad_table, row_ids, "sij,sif->sjf")
    col_hits = (
        (col_ids[None, :] == jnp.arange(source_count, dtype=jnp.int32)[:, None])
        & live_mask[None, :]
    ).astype(jnp.float32)
    source_terms = jnp.einsum(
        "cs,sjf->cjf", col_hits, backward_terms, precision=lax.Precision.HIGHEST
    ).reshape(-1, feat_width)
    source_part = lax.psum_scatter(source_terms, "row", scatter_dimension=0, tiled=True)
    return (
        output,
        self_sum * scale_factor,
        neigh_sum * scale_factor,
        source_part.reshape(1, -1, feat_width),
    )


def solution(mesh):
    placed = (
        P("col", None, None),
        P(("row", "col"), None),
        P(),
        P(),
        P(("row", "col"), None),
        P("row", "col", None, None, None),
        P("row", "col", None),
        P("row", "col", None),
        P("row", "col"),
    )
    return jax.shard_map(
        per_device,
        mesh=mesh,
        in_specs=placed,
        out_specs=(P(("row", "col"), None), P(), P(), P("col", "row", None)),
        check_vma=False,
    )
```

profile of v0, /device:TPU:0, one launch (start us, length us, event | category | flops | bytes accessed | tf_op | source)
XLA Modules:
  0.0 236.0 jit_solution(193083326414582742)
XLA Ops:
  7.2 0.0 copy-start
  7.2 0.0 reduce-scatter.3.cloned.1.call-start
  8.0 0.7 fusion.21
  8.6 2.7 %gather_fusion = bf16[32,128,128]{2,1,0:T(8,128)(2,1)} fusion(bf16[16,128,128]{2,1,0:T(8,128)(2,1)} %bitcast.48, s32[1024]{0:T(1024)S(1)} %pad_clamp_fusion.1), kind=kCustom, calls=%fused_computation | custom fusion | bytes 2097280 | tf_op jit(solution)/shard_map/gather | solution.py:11
  11.3 0.0 copy-done
  11.3 2.1 fusion.6
  13.4 0.0 copy-start.5
  13.4 2.1 copy.21
  15.5 0.0 copy-done.5
  15.5 0.0 copy-start.1
  15.5 0.0 copy-start.2
  15.5 0.0 copy-start.3
  15.5 0.0 copy-start.7
  15.5 2.4 %fusion.2 = f32[8,128,128]{2,0,1:T(8,128)S(1)} fusion(f32[32,128,128]{1,0,2:T(8,128)} %copy.21, s32[32]{0:T(128)S(1)} %bitcast.50, pred[32]{0:T(512)(128)(4,1)S(1)} %iota_compare_fusion.2), kind=kOutput, calls=%fused_computation.4 | convolution fusion | flops 50332160 | bytes 2621600 | tf_op jit(solution)/shard_map/rs,sif->rif/dot_general | solution.py:43
  17.9 0.9 copy.16
  18.8 0.0 reduce-scatter.3.cloned.1.call-update
  18.9 0.0 all-reduce.3.cloned.1.call-start
  18.9 0.0 copy-done.1
  18.9 0.0 copy-done.2
  18.9 0.1 fusion.23
  19.1 33.6 %reduce-scatter.3.cloned.1.call-done = f32[128,128]{1,0:T(8,128)} async-done(((f32[1024,128]{1,0:T(8,128)}), f32[128,128]{1,0:T(8,128)}) %reduce-scatter.3.cloned.1.call-update) | async-done | bytes 65552 | tf_op jit(solution)/shard_map/reduce_scatter | solution.py:44
  52.7 0.0 copy-done.3
  52.7 0.0 copy-done.7
  52.7 1.7 multiply_convert_fusion
  54.3 0.2 convolution_convert_fusion
  54.5 0.9 convolution_bitcast_fusion
  55.3 14.2 %all_gather.3 = bf16[1024,128]{1,0:T(8,128)(2,1)S(1)} all-gather(bf16[128,128]{1,0:T(8,128)(2,1)S(1)} %convolution_convert_fusion), channel_id=1, replica_groups=mesh['row'=4,'col'=8] {'col'}, dimensions={0}, use_global_device_ids=true | all-gather | bytes 294912 | tf_op jit(solution)/shard_map/all_gather | solution.py:67
  69.5 0.7 gather_fusion.1
  70.3 1.9 fusion.4
  72.1 0.0 copy-start.4
  72.1 0.0 copy-start.6
  72.1 2.4 %copy.23 = f32[32,128,128]{1,0,2:T(8,128)S(1)} copy(f32[32,128,128]{2,1,0:T(8,128)} %fusion.4) | data formatting | bytes 4194304 | tf_op jit(solution)/shard_map/sij,sif->sjf/dot_general | solution.py:10
  74.5 0.0 copy-done.4
  74.6 0.9 fusion.8
  75.4 0.0 all-reduce.3.cloned.1.call-update
  75.5 0.0 reduce-scatter.5.cloned.1.call-start
  75.5 0.0 copy-done.6
  75.5 0.8 fusion
  76.4 1.3 copy.18
  77.7 0.0 reduce-scatter.5.cloned.1.call-update
  77.7 121.3 %all-reduce.3.cloned.1.call-done = (f32[128,256]{0,1:T(8,128)}, f32[128,256]{0,1:T(8,128)}) async-done(((f32[128,256]{0,1:T(8,128)}, f32[128,256]{0,1:T(8,128)}), (f32[128,256]{0,1:T(8,128)}, f32[128,256]{0,1:T(8,128)})) %all-reduce.3.cloned.1.call-update) | async-done | bytes 262160 | tf_op jit(solution)/shard_map/psum | solution.py:63
  199.0 1.0 broadcast_multiply_fusion
  200.0 0.8 copy.20
  200.7 0.8 copy.19
  201.5 28.0 %reduce-scatter.5.cloned.1.call-done = f32[512,128]{1,0:T(8,128)} async-done(((f32[2048,128]{1,0:T(8,128)}), f32[512,128]{1,0:T(8,128)}) %reduce-scatter.5.cloned.1.call-update) | async-done | bytes 262160 | tf_op jit(solution)/shard_map/reduce_scatter | solution.py:77
  (4 shorter events, 0.0 us)
Async XLA Ops:
  7.2 4.2 %copy-start = (bf16[1,1,32,128,128]{4,3,2,1,0:T(8,128)(2,1)S(1)}, bf16[1,1,32,128,128]{4,3,2,1,0:T(8,128)(2,1)}, u32[]{:S(2)}) copy-start(bf16[1,1,32,128,128]{4,3,2,1,0:T(8,128)(2,1)} %param.14) | copy-start | bytes 3145732
  7.2 45.5 %reduce-scatter.3.cloned.1.call-start = ((), (), s32[]{:S(2)}) async-start(), calls=%async_computation.2 | async-start | bytes 589824 | tf_op jit(solution)/shard_map/reduce_scatter | solution.py:44
  13.4 2.1 copy-start.5
  15.5 3.4 %copy-start.1 = (bf16[128,128]{1,0:T(8,128)(2,1)S(1)}, bf16[128,128]{1,0:T(8,128)(2,1)}, u32[]{:S(2)}) copy-start(bf16[128,128]{1,0:T(8,128)(2,1)} %param.10) | copy-start | bytes 98308
  15.5 3.4 %copy-start.2 = (bf16[128,256]{1,0:T(8,128)(2,1)S(1)}, bf16[128,256]{1,0:T(8,128)(2,1)}, u32[]{:S(2)}) copy-start(bf16[128,256]{1,0:T(8,128)(2,1)} %param.11) | copy-start | bytes 196612
  15.5 37.2 %copy-start.3 = (bf16[128,256]{1,0:T(8,128)(2,1)S(1)}, bf16[128,256]{1,0:T(8,128)(2,1)}, u32[]{:S(2)}) copy-start(bf16[128,256]{1,0:T(8,128)(2,1)} %param.12) | copy-start | bytes 196612
  15.5 37.2 %copy-start.7 = (bf16[128,256]{1,0:T(8,128)(2,1)S(1)}, bf16[128,256]{1,0:T(8,128)(2,1)}, u32[]{:S(2)}) copy-start(bf16[128,256]{1,0:T(8,128)(2,1)} %param.13) | copy-start | bytes 196612
  18.9 180.1 %all-reduce.3.cloned.1.call-start = ((), (), s32[]{:S(2)}) async-start(), calls=%async_computation.4 | async-start | bytes 524288 | tf_op jit(solution)/shard_map/psum | solution.py:63
  72.1 2.4 %copy-start.4 = (f32[128,128]{1,0:T(8,128)S(1)}, f32[128,128]{1,0:T(8,128)}, u32[]{:S(2)}) copy-start(f32[128,128]{1,0:T(8,128)} %reduce-scatter.3.cloned.1.call-done) | copy-start | bytes 196612
  72.1 3.4 %copy-start.6 = (s32[1,1,32]{2,1,0:T(1,128)S(1)}, s32[1,1,32]{2,1,0:T(1,128)}, u32[]{:S(2)}) copy-start(s32[1,1,32]{2,1,0:T(1,128)} %param.16) | copy-start | bytes 388
  75.5 154.1 %reduce-scatter.5.cloned.1.call-start = ((), (), s32[]{:S(2)}) async-start(), calls=%async_computation.3 | async-start | bytes 1310720 | tf_op jit(solution)/shard_map/reduce_scatter | solution.py:77
Sparse Core Ops, SparseCore 0:
  19.0 33.6 reduce-scatter.2
  75.6 123.3 all-reduce.2
  202.7 26.7 reduce-scatter.4
where the time goes:
time: 236 us
  waiting for transfers between devices  183 us (78%)
  between operations  14.6 us (6%)
  blocking collectives  14.2 us (6%)
  local copies, waits for them, and re-layouts  11.6 us (5%)
  matrix products  10.9 us (5%)
    psum x1, waiting for transfers between devices, per_device(): self_sum, neigh_sum = lax.psum((self_grad, neigh_grad), ('row', 'col'))  121 us
    reduce_scatter x1, waiting for transfers between devices, per_device(): lax.psum_scatter(summed.reshape(local_rows * lax.axis_size('col'), feat_w...  33.6 us
    reduce_scatter x1, waiting for transfers between devices, per_device(): lax.psum_scatter(source_terms, 'row', scatter_dimension=0, tiled=True)  28 us
    all_gather x1, blocking collectives, per_device(): slab_grad = lax.all_gather(local_grad, 'col', axis=0, tiled=True)  14.2 us
  transfers between devices with their start and end apart: 3, of which 3 were waited for; matrix products, arithmetic and copies ran while one was open for 2% of the time, Pallas kernels for 0%

commit v1 on v0

v1 whole, which is shorter than its diff:
```python
import functools
import math

import jax
import jax.numpy as jnp
from jax import lax
from jax.experimental import pallas as pl
from jax.experimental.pallas import tpu as pltpu
from jax.sharding import PartitionSpec as P

F32 = jnp.float32
BF16 = jnp.bfloat16
VMEM = pl.BlockSpec(memory_space=pltpu.VMEM)
SMEM = pl.BlockSpec(memory_space=pltpu.SMEM)


def xor_permute(x, axis, distance):
    total = lax.axis_size(axis)
    return lax.ppermute(x, axis, [(i, i ^ distance) for i in range(total)])


def tree_sum(terms):
    while len(terms) > 1:
        terms = [terms[i] + terms[i + 1] for i in range(0, len(terms), 2)]
    return terms[0]


def forward_kernel(rows, cols, counts, values, table, mine, theirs, acc):
    slots = values.shape[2]
    pairs = mine.shape[0]
    me = lax.axis_index("col")
    acc[...] = jnp.zeros_like(acc)
    live = counts[0, 0]
    for s in range(slots):
        at = rows[0, 0, s] ^ me
        block = values[0, 0, s]
        block = jnp.where(s < live, block, jnp.zeros_like(block))
        acc[at] += jnp.dot(block, table[cols[0, 0, s]], preferred_element_type=F32)
    for p in range(pairs):
        mine[p] = acc[2 * p]
        theirs[p] = acc[2 * p + 1]


def middle_kernel(pairs, *refs):
    sums = refs[:pairs]
    dst, w_self, w_neigh, cot, output = refs[pairs : pairs + 5]
    payloads = refs[pairs + 5 : 2 * pairs + 5]
    weights = refs[2 * pairs + 5]
    z = lax.axis_index("col") // 2
    width = dst.shape[1]
    hidden = w_self.shape[1]
    agg = tree_sum([ref[...] for ref in sums]).astype(BF16)
    own = dst[...]
    pre = jnp.dot(own, w_self[...], preferred_element_type=F32) + jnp.dot(
        agg, w_neigh[...], preferred_element_type=F32
    )
    sig = jax.nn.sigmoid(pre)
    output[...] = (pre * sig).astype(BF16)
    grad_pre = (cot[...].astype(F32) * sig * (1.0 + pre * (1.0 - sig))).astype(BF16)
    grad_t = lax.dot_general(
        w_neigh[...], grad_pre, (((1,), (1,)), ((), ())), preferred_element_type=F32
    ).astype(BF16)
    nodes = (((0,), (0,)), ((), ()))
    share = weights.shape[1]
    w_both = [
        lax.dot_general(own, grad_pre, nodes, preferred_element_type=F32),
        lax.dot_general(agg, grad_pre, nodes, preferred_element_type=F32),
    ]
    for p in range(pairs):
        first = p * share
        weights[p] = w_both[first // width][first % width : first % width + share].astype(BF16)
    halves = hidden // width
    for p in range(pairs):
        payloads[p][:width] = grad_t
        chunk = weights[z ^ p]
        for h in range(halves):
            payloads[p][width + h * share : width + (h + 1) * share] = chunk[
                :, h * width : (h + 1) * width
            ]


def weight_sum_kernel(count, *refs):
    near, far, total = refs[:count], refs[count : 2 * count], refs[2 * count]
    width = total.shape[1]

    def chunk(ref):
        return ref[width:].astype(F32)

    total[...] = tree_sum([chunk(r) for r in near]) + tree_sum([chunk(r) for r in far])


def backward_kernel(pairs, groups, *refs):
    rows, cols, counts, values = refs[:4]
    near = refs[4 : 4 + pairs]
    far = refs[4 + pairs : 4 + 2 * pairs]
    own = refs[4 + 2 * pairs]
    sends = refs[5 + 2 * pairs : 4 + 2 * pairs + groups]
    table, acc = refs[4 + 2 * pairs + groups :]
    width = table.shape[1]
    slots = values.shape[2]
    share = own.shape[0]
    me = lax.axis_index("col")
    group = lax.axis_index("row")
    for p in range(pairs):
        table[2 * p] = near[p][:width]
        table[2 * p + 1] = far[p][:width]
    acc[...] = jnp.zeros_like(acc)
    live = counts[0, 0]
    for s in range(slots):
        block = values[0, 0, s]
        block = jnp.where(s < live, block, jnp.zeros_like(block))
        at = cols[0, 0, s] ^ (group * share)
        acc[at] += jnp.dot(table[rows[0, 0, s] ^ me], block, preferred_element_type=F32)
    own[...] = acc[:share]
    for g in range(1, groups):
        sends[g - 1][...] = acc[g * share : (g + 1) * share].astype(BF16)


def source_sum_kernel(groups, *refs):
    out = refs[groups]
    share, width, block = refs[0].shape
    for b in range(share):
        total = tree_sum([r[b].astype(F32) for r in refs[:groups]])
        out[b * block : (b + 1) * block, :] = total.T


def weight_join_kernel(pairs, *refs):
    chunks = refs[:pairs]
    w_self, w_neigh, table = refs[pairs : pairs + 3]
    z = lax.axis_index("col") // 2
    share = table.shape[1]
    width = chunks[0].shape[1]
    for p in range(pairs):
        for h in range(chunks[0].shape[0] // share):
            table[z ^ p, :, h * width : (h + 1) * width] = chunks[p][h * share : (h + 1) * share]
    half = pairs // 2
    for p in range(half):
        w_self[p * share : (p + 1) * share] = table[p]
        w_neigh[p * share : (p + 1) * share] = table[p + half]


def shaped(shape, dtype):
    return jax.ShapeDtypeStruct(shape, dtype)


def per_device(
    features,
    dst_features,
    w_self,
    w_neigh,
    cotangent,
    block_values,
    block_rows,
    block_cols,
    block_counts,
):
    block = block_values.shape[-1]
    width = features.shape[-1]
    hidden = w_self.shape[-1]
    local = dst_features.shape[0]
    col_total = lax.axis_size("col")
    groups = lax.axis_size("row")
    pairs = col_total // 2
    table = features.reshape(-1, block, width)
    source_blocks = table.shape[0]
    params = pltpu.CompilerParams(vmem_limit_bytes=24 * 1024 * 1024)

    mine, theirs = pl.pallas_call(
        forward_kernel,
        out_shape=[shaped((pairs, block, width), F32)] * 2,
        in_specs=[SMEM, SMEM, SMEM, VMEM, VMEM],
        out_specs=[VMEM, VMEM],
        scratch_shapes=[pltpu.VMEM((col_total, block, width), F32)],
        compiler_params=params,
        name="forward_blocks",
    )(block_rows, block_cols, block_counts, block_values, table)
    chip_sum = mine + xor_permute(theirs, "col", 1)
    sums = [chip_sum[0]] + [xor_permute(chip_sum[p], "col", 2 * p) for p in range(1, pairs)]

    share = 2 * width // pairs
    packed = shaped((width + hidden // width * share, width), BF16)
    output, *payloads = pl.pallas_call(
        functools.partial(middle_kernel, pairs),
        out_shape=[shaped((local, hidden), BF16)] + [packed] * pairs,
        in_specs=[VMEM] * (pairs + 4),
        out_specs=[VMEM] * (pairs + 1),
        scratch_shapes=[pltpu.VMEM((pairs, share, hidden), BF16)],
        compiler_params=params,
        name="dense_layer",
    )(*sums, dst_features, w_self, w_neigh, cotangent)
    near = [payloads[0]] + [xor_permute(payloads[p], "col", 2 * p) for p in range(1, pairs)]
    far = [xor_permute(x, "col", 1) for x in near]

    weight_part = pl.pallas_call(
        functools.partial(weight_sum_kernel, pairs),
        out_shape=shaped((hidden // width * share, width), F32),
        in_specs=[VMEM] * (2 * pairs),
        out_specs=VMEM,
        compiler_params=params,
        name="weight_sum",
    )(*near, *far)
    weight_terms = [weight_part] + [xor_permute(weight_part, "row", g) for g in range(1, groups)]

    source_share = source_blocks // groups
    own, *sends = pl.pallas_call(
        functools.partial(backward_kernel, pairs, groups),
        out_shape=[shaped((source_share, width, block), F32)]
        + [shaped((source_share, width, block), BF16)] * (groups - 1),
        in_specs=[SMEM, SMEM, SMEM] + [VMEM] * (1 + 2 * pairs),
        out_specs=[VMEM] * groups,
        scratch_shapes=[
            pltpu.VMEM((col_total, width, block), BF16),
            pltpu.VMEM((source_blocks, width, block), F32),
        ],
        compiler_params=params,
        name="backward_blocks",
    )(block_rows, block_cols, block_counts, block_values, *near, *far)
    source_terms = [own] + [xor_permute(x, "row", g) for g, x in enumerate(sends, 1)]

    node_total = local * groups * col_total
    weight_chunk = tree_sum(weight_terms) * (1.0 / math.sqrt(node_total))
    chunks = [weight_chunk] + [xor_permute(weight_chunk, "col", 2 * p) for p in range(1, pairs)]
    grad_self, grad_neigh = pl.pallas_call(
        functools.partial(weight_join_kernel, pairs),
        out_shape=[shaped((width, hidden), F32)] * 2,
        in_specs=[VMEM] * pairs,
        out_specs=[VMEM] * 2,
        scratch_shapes=[pltpu.VMEM((pairs, share, hidden), F32)],
        compiler_params=params,
        name="weight_join",
    )(*chunks)

    grad_source = pl.pallas_call(
        functools.partial(source_sum_kernel, groups),
        out_shape=shaped((source_share * block, width), F32),
        in_specs=[VMEM] * groups,
        out_specs=VMEM,
        compiler_params=params,
        name="source_sum",
    )(*source_terms)
    return output, grad_self, grad_neigh, grad_source.reshape(1, -1, width)


def solution(mesh):
    placed = (
        P("col", None, None),
        P(("row", "col"), None),
        P(),
        P(),
        P(("row", "col"), None),
        P("row", "col", None, None, None),
        P("row", "col", None),
        P("row", "col", None),
        P("row", "col"),
    )
    return jax.shard_map(
        per_device,
        mesh=mesh,
        in_specs=placed,
        out_specs=(P(("row", "col"), None), P(), P(), P("col", "row", None)),
        check_vma=False,
    )
```

time: 236 us -> 51.1 us (0.22)
  waiting for transfers between devices: 183 us -> 19.2 us
  starting transfers between devices: 0.12 us -> 22.5 us
  blocking collectives: 14.2 us -> 0 us
  between operations: 14.6 us -> 1.4 us
  matrix products: 10.9 us -> 0 us
  local copies, waits for them, and re-layouts: 11.6 us -> 2.97 us
  Pallas kernels: 0 us -> 4.71 us
    psum x1 -> x0, waiting for transfers between devices: 121 us -> none  [per_device(): self_sum, neigh_sum = lax.psum((self_grad, neigh_grad), ('row', 'col'))]
    reduce_scatter x2 -> x0, waiting for transfers between devices: 61.6 us -> none  [the longest x1 33.6 us: per_device(): lax.psum_scatter(summed.reshape(local_rows * lax.axis_size('col'), feat_w...]
    ppermute x0 -> x20, starting transfers between devices: none -> 22.5 us  [xor_permute(): return lax.ppermute(x, axis, [(i, i ^ distance) for i in range(total)])]
    ppermute x0 -> x20, waiting for transfers between devices: none -> 19.2 us  [xor_permute(): return lax.ppermute(x, axis, [(i, i ^ distance) for i in range(total)])]
    all_gather x1 -> x0, blocking collectives: 14.2 us -> none  [per_device(): slab_grad = lax.all_gather(local_grad, 'col', axis=0, tiled=True)]
    dot_general x9 -> x0, matrix products: 10.9 us -> none  [the longest x2 3.96 us: slot_products(): jnp.einsum(einsum_form, block_vals, source_table[slot_index], preferred_e...]
    dot_general x4 -> x0, local copies, waits for them, and re-layouts: 6.65 us -> none  [the longest x2 4.46 us: slot_products(): jnp.einsum(einsum_form, block_vals, source_table[slot_index], preferred_e...]
    pallas_call x0 -> x6, Pallas kernels: none -> 4.71 us  [the longest x1 1.15 us: per_device(): pl.pallas_call(functools.partial(backward_kernel, pairs, groups), out_sha...]
  transfers between devices with their start and end apart: 3 -> 20, of which waited for: 3 -> 11; matrix products, arithmetic and copies ran while one was open for 2% -> 0% of each run, Pallas kernels for 0% -> 4%
where the time goes in v1:
time: 51.1 us; the launch traced here: 50.9 us
  starting transfers between devices  22.5 us (44%)
  waiting for transfers between devices  19.2 us (38%)
  Pallas kernels  4.71 us (9%)
  local copies, waits for them, and re-layouts  2.97 us (6%)
  between operations  1.4 us (3%)
    ppermute x20, starting transfers between devices, xor_permute(): return lax.ppermute(x, axis, [(i, i ^ distance) for i in range(total)])  22.5 us
    ppermute x20, waiting for transfers between devices, xor_permute(): return lax.ppermute(x, axis, [(i, i ^ distance) for i in range(total)])  19.2 us
    unnamed x18, local copies, waits for them, and re-layouts  2.95 us
    pallas_call x1, Pallas kernels, per_device(): pl.pallas_call(functools.partial(backward_kernel, pairs, groups), out_sha...  1.15 us
    pallas_call x1, Pallas kernels, per_device(): pl.pallas_call(forward_kernel, out_shape=[shaped((pairs, block, width), F...  1.08 us
  transfers between devices with their start and end apart: 20, of which 11 were waited for; matrix products, arithmetic and copies ran while one was open for 0% of the time, Pallas kernels for 4%

profile of v1, /device:TPU:0, one launch (start us, length us, event | category | flops | bytes accessed | tf_op | source)
XLA Modules:
  0.0 50.9 jit_solution(8850867326371741660)
XLA Ops:
  1.3 0.6 %copy-done.7 = s32[1,1,32]{2,1,0:T(1,128)S(1)} copy-done((s32[1,1,32]{2,1,0:T(1,128)S(1)}, s32[1,1,32]{2,1,0:T(1,128)}, u32[]{:S(2)}) %copy-start.7) | copy-done | bytes 152
  1.9 0.0 copy-done.8
  2.0 1.2 %copy-done = bf16[1,1,32,128,128]{4,3,2,1,0:T(8,128)(2,1)S(1)} copy-done((bf16[1,1,32,128,128]{4,3,2,1,0:T(8,128)(2,1)S(1)}, bf16[1,1,32,128,128]{4,3,2,1,0:T(8,128)(2,1)}, u32[]{:S(2)}) %copy-start) | copy-done | bytes 1048600
  3.2 1.0 %copy-done.2 = bf16[1,2048,128]{2,1,0:T(8,128)(2,1)S(1)} copy-done((bf16[1,2048,128]{2,1,0:T(8,128)(2,1)S(1)}, bf16[1,2048,128]{2,1,0:T(8,128)(2,1)}, u32[]{:S(2)}) %copy-start.2) | copy-done | bytes 524312
  4.2 1.1 %forward_blocks.1 = (f32[4,128,128]{2,1,0:T(8,128)S(1)}, f32[4,128,128]{2,1,0:T(8,128)S(1)}) custom-call(s32[1,1,32]{2,1,0:T(1,128)S(1)} %copy-done.7, s32[1,1,32]{2,1,0:T(1,128)S(1)} %copy-done.8, s32[1,1]{1,0:T(1,128)S(6)} %copy.13.counts.refs_2_, bf16[1,1,32,128,128]{4,3,2,1,0:T(8,128)(2,1)S(1)} %copy-done, bf16[16,128,128]{2,1,0:T(8,128)(2,1)S(1)} %bitcast.10), custom_call_target="tpu_custom_call" | custom-call | tf_op jit(solution)/shard_map/forward_blocks/pallas_call | solution.py:168
  5.3 0.5 %collective-permute-start = (f32[4,128,128]{2,1,0:T(8,128)S(1)}, f32[4,128,128]{2,1,0:T(8,128)S(1)}, u32[]{:S(2)}, u32[]{:S(2)}) collective-permute-start(f32[4,128,128]{2,1,0:T(8,128)S(1)} %get-tuple-element.18), channel_id=1, source_target_pairs={{0,1},{1,0},{2,3},{3,2},{4,5},{5,4},{6,7},{7,6},{8,9},{9,8},{10,11... | collective-permute-start | bytes 786440 | tf_op jit(solution)/shard_map/ppermute | solution.py:19
  5.8 1.2 %collective-permute-done = f32[4,128,128]{2,1,0:T(8,128)S(1)} collective-permute-done((f32[4,128,128]{2,1,0:T(8,128)S(1)}, f32[4,128,128]{2,1,0:T(8,128)S(1)}, u32[]{:S(2)}, u32[]{:S(2)}) %collective-permute-start) | collective-permute-done | bytes 262176 | tf_op jit(solution)/shard_map/ppermute | solution.py:19
  7.0 0.0 copy-start.3
  7.0 0.0 copy-start.4
  7.1 0.0 copy-start.5
  7.1 0.0 copy-start.6
  7.1 3.0 %collective-permute-start.1 = (f32[128,128]{1,0:T(8,128)S(1)}, f32[128,128]{1,0:T(8,128)S(1)}, u32[]{:S(2)}, u32[]{:S(2)}) collective-permute-start(f32[128,128]{1,0:T(8,128)S(1)} %get-tuple-element.32), channel_id=1, source_target_pairs={{0,2},{1,3},{2,0},{3,1},{4,6},{5,7},{6,4},{7,5},{8,10},{9,11},{10,... | collective-permute-start | bytes 196616 | tf_op jit(solution)/shard_map/ppermute | solution.py:19
  10.1 2.6 %collective-permute-start.2 = (f32[128,128]{1,0:T(8,128)S(1)}, f32[128,128]{1,0:T(8,128)S(1)}, u32[]{:S(2)}, u32[]{:S(2)}) collective-permute-start(f32[128,128]{1,0:T(8,128)S(1)} %get-tuple-element.31), channel_id=1, source_target_pairs={{0,4},{1,5},{2,6},{3,7},{4,0},{5,1},{6,2},{7,3},{8,12},{9,13},{10,... | collective-permute-start | bytes 196616 | tf_op jit(solution)/shard_map/ppermute | solution.py:19
  12.7 0.0 collective-permute-start.3
  12.7 0.0 collective-permute-done.1.refs_1_
  12.7 4.9 %collective-permute-done.2.refs_2_ = f32[128,128]{1,0:T(8,128)S(1)} collective-permute-done((f32[128,128]{1,0:T(8,128)S(1)}, f32[128,128]{1,0:T(8,128)S(1)}, u32[]{:S(2)}, u32[]{:S(2)}) %collective-permute-start.2) | collective-permute-done | bytes 65568 | tf_op jit(solution)/shard_map/ppermute | solution.py:19
  17.7 1.2 %collective-permute-done.3.refs_3_ = f32[128,128]{1,0:T(8,128)S(1)} collective-permute-done((f32[128,128]{1,0:T(8,128)S(1)}, f32[128,128]{1,0:T(8,128)S(1)}, u32[]{:S(2)}, u32[]{:S(2)}) %collective-permute-start.3) | collective-permute-done | bytes 65568 | tf_op jit(solution)/shard_map/ppermute | solution.py:19
  18.9 0.8 %dense_layer.1 = (bf16[128,256]{1,0:T(8,128)(2,1)}, bf16[256,128]{1,0:T(8,128)(2,1)S(1)}, bf16[256,128]{1,0:T(8,128)(2,1)S(1)}, bf16[256,128]{1,0:T(8,128)(2,1)S(1)}, bf16[256,128]{1,0:T(8,128)(2,1)S(1)}) custom-call(f32[128,128]{1,0:T(8,128)S(1)} %get-tuple-element.33.refs_0_, f32[128,128]{1,0:T(8,128)S(1)} %collective-permute-done.1.refs_1_, ...), custom_call_target="tpu_custom_call" | custom-call | tf_op jit(solution)/shard_map/dense_layer/pallas_call | solution.py:182
  19.7 2.0 %collective-permute-start.6 = (bf16[256,128]{1,0:T(8,128)(2,1)S(1)}, bf16[256,128]{1,0:T(8,128)(2,1)S(1)}, u32[]{:S(2)}, u32[]{:S(2)}) collective-permute-start(bf16[256,128]{1,0:T(8,128)(2,1)S(1)} %get-tuple-element.23), channel_id=1, source_target_pairs={{0,6},{1,7},{2,4},{3,5},{4,2},{5,3},{6,0},{7,1},{8,14},{9,15},{10,... | collective-permute-start | bytes 196616 | tf_op jit(solution)/shard_map/ppermute | solution.py:19
  21.7 0.4 collective-permute-start.4
  22.1 2.0 %collective-permute-start.5 = (bf16[256,128]{1,0:T(8,128)(2,1)S(1)}, bf16[256,128]{1,0:T(8,128)(2,1)S(1)}, u32[]{:S(2)}, u32[]{:S(2)}) collective-permute-start(bf16[256,128]{1,0:T(8,128)(2,1)S(1)} %get-tuple-element.22), channel_id=1, source_target_pairs={{0,4},{1,5},{2,6},{3,7},{4,0},{5,1},{6,2},{7,3},{8,12},{9,13},{10,... | collective-permute-start | bytes 196616 | tf_op jit(solution)/shard_map/ppermute | solution.py:19
  24.1 0.0 collective-permute-start.7
  24.1 1.7 %collective-permute-done.6.refs_3_.refs_7_ = bf16[256,128]{1,0:T(8,128)(2,1)S(1)} collective-permute-done((bf16[256,128]{1,0:T(8,128)(2,1)S(1)}, bf16[256,128]{1,0:T(8,128)(2,1)S(1)}, u32[]{:S(2)}, u32[]{:S(2)}) %collective-permute-start.6) | collective-permute-done | bytes 65568 | tf_op jit(solution)/shard_map/ppermute | solution.py:19
  25.9 0.0 collective-permute-start.10
  25.9 1.7 %collective-permute-done.4.refs_1_.refs_5_ = bf16[256,128]{1,0:T(8,128)(2,1)S(1)} collective-permute-done((bf16[256,128]{1,0:T(8,128)(2,1)S(1)}, bf16[256,128]{1,0:T(8,128)(2,1)S(1)}, u32[]{:S(2)}, u32[]{:S(2)}) %collective-permute-start.4) | collective-permute-done | bytes 65568 | tf_op jit(solution)/shard_map/ppermute | solution.py:19
  27.6 0.0 collective-permute-start.8
  27.6 0.5 collective-permute-start.9
  28.1 0.0 collective-permute-done.10.refs_7_.refs_11_
  28.1 0.7 %collective-permute-done.8.refs_5_.refs_9_ = bf16[256,128]{1,0:T(8,128)(2,1)S(1)} collective-permute-done((bf16[256,128]{1,0:T(8,128)(2,1)S(1)}, bf16[256,128]{1,0:T(8,128)(2,1)S(1)}, u32[]{:S(2)}, u32[]{:S(2)}) %collective-permute-start.8) | collective-permute-done | bytes 65568 | tf_op jit(solution)/shard_map/ppermute | solution.py:19
  28.8 0.2 collective-permute-done.9.refs_6_.refs_10_
  29.0 1.6 %collective-permute-start.11 = (f32[128,128]{1,0:T(8,128)S(1)}, f32[128,128]{1,0:T(8,128)S(1)}, u32[]{:S(2)}, u32[]{:S(2)}) collective-permute-start(f32[128,128]{1,0:T(8,128)S(1)} %weight_sum.1), channel_id=1, source_target_pairs={{0,8},{8,0},{16,24},{24,16},{1,9},{9,1},{17,25},{25,17},{2,10},{10... | collective-permute-start | bytes 196616 | tf_op jit(solution)/shard_map/ppermute | solution.py:19
  30.6 1.5 %collective-permute-start.12 = (f32[128,128]{1,0:T(8,128)S(1)}, f32[128,128]{1,0:T(8,128)S(1)}, u32[]{:S(2)}, u32[]{:S(2)}) collective-permute-start(f32[128,128]{1,0:T(8,128)S(1)} %weight_sum.1), channel_id=1, source_target_pairs={{0,16},{8,24},{16,0},{24,8},{1,17},{9,25},{17,1},{25,9},{2,18},{10... | collective-permute-start | bytes 196616 | tf_op jit(solution)/shard_map/ppermute | solution.py:19
  32.1 0.5 collective-permute-start.13
  32.6 1.2 %backward_blocks.1 = (f32[4,128,128]{2,1,0:T(8,128)S(1)}, bf16[4,128,128]{2,1,0:T(8,128)(2,1)S(1)}, bf16[4,128,128]{2,1,0:T(8,128)(2,1)S(1)}, bf16[4,128,128]{2,1,0:T(8,128)(2,1)S(1)}) custom-call(s32[1,1,32]{2,1,0:T(1,128)S(1)} %copy-done.7, s32[1,1,32]{2,1,0:T(1,128)S(1)} %copy-done.8, s32[1,1]{1,0:T(1,128)S(6)} %copy.13.counts.refs_2_, ...), custom_call_target="tpu_custom_call" | custom-call | tf_op jit(solution)/shard_map/backward_blocks/pallas_call | solution.py:205
  33.8 0.0 collective-permute-done.11
  33.8 1.1 %collective-permute-done.12 = f32[128,128]{1,0:T(8,128)S(1)} collective-permute-done((f32[128,128]{1,0:T(8,128)S(1)}, f32[128,128]{1,0:T(8,128)S(1)}, u32[]{:S(2)}, u32[]{:S(2)}) %collective-permute-start.12) | collective-permute-done | bytes 65568 | tf_op jit(solution)/shard_map/ppermute | solution.py:19
  34.9 2.4 %collective-permute-done.13 = f32[128,128]{1,0:T(8,128)S(1)} collective-permute-done((f32[128,128]{1,0:T(8,128)S(1)}, f32[128,128]{1,0:T(8,128)S(1)}, u32[]{:S(2)}, u32[]{:S(2)}) %collective-permute-start.13) | collective-permute-done | bytes 65568 | tf_op jit(solution)/shard_map/ppermute | solution.py:19
  37.3 1.3 %collective-permute-start.14 = (f32[128,128]{1,0:T(8,128)S(1)}, f32[128,128]{1,0:T(8,128)S(1)}, u32[]{:S(2)}, u32[]{:S(2)}) collective-permute-start(f32[128,128]{1,0:T(8,128)S(1)} %add_multiply_fusion.refs_0_), channel_id=1, source_target_pairs={{0,2},{1,3},{2,0},{3,1},{4,6},{5,7},{6,4},{7,5},{8,10},{9,11},{10,... | collective-permute-start | bytes 196616 | tf_op jit(solution)/shard_map/ppermute | solution.py:19
  38.5 0.5 %collective-permute-start.17 = (bf16[4,128,128]{2,1,0:T(8,128)(2,1)S(1)}, bf16[4,128,128]{2,1,0:T(8,128)(2,1)S(1)}, u32[]{:S(2)}, u32[]{:S(2)}) collective-permute-start(bf16[4,128,128]{2,1,0:T(8,128)(2,1)S(1)} %get-tuple-element.27), channel_id=1, source_target_pairs={{0,8},{8,0},{16,24},{24,16},{1,9},{9,1},{17,25},{25,17},{2,10},{10... | collective-permute-start | bytes 393224 | tf_op jit(solution)/shard_map/ppermute | solution.py:19
  39.1 0.5 collective-permute-start.18
  39.6 2.4 %collective-permute-start.19 = (bf16[4,128,128]{2,1,0:T(8,128)(2,1)S(1)}, bf16[4,128,128]{2,1,0:T(8,128)(2,1)S(1)}, u32[]{:S(2)}, u32[]{:S(2)}) collective-permute-start(bf16[4,128,128]{2,1,0:T(8,128)(2,1)S(1)} %get-tuple-element.29), channel_id=1, source_target_pairs={{0,24},{8,16},{16,8},{24,0},{1,25},{9,17},{17,9},{25,1},{2,26},{10... | collective-permute-start | bytes 393224 | tf_op jit(solution)/shard_map/ppermute | solution.py:19
  42.0 1.0 %collective-permute-start.15 = (f32[128,128]{1,0:T(8,128)S(1)}, f32[128,128]{1,0:T(8,128)S(1)}, u32[]{:S(2)}, u32[]{:S(2)}) collective-permute-start(f32[128,128]{1,0:T(8,128)S(1)} %add_multiply_fusion.refs_0_), channel_id=1, source_target_pairs={{0,4},{1,5},{2,6},{3,7},{4,0},{5,1},{6,2},{7,3},{8,12},{9,13},{10,... | collective-permute-start | bytes 196616 | tf_op jit(solution)/shard_map/ppermute | solution.py:19
  43.1 2.2 %collective-permute-start.16 = (f32[128,128]{1,0:T(8,128)S(1)}, f32[128,128]{1,0:T(8,128)S(1)}, u32[]{:S(2)}, u32[]{:S(2)}) collective-permute-start(f32[128,128]{1,0:T(8,128)S(1)} %add_multiply_fusion.refs_0_), channel_id=1, source_target_pairs={{0,6},{1,7},{2,4},{3,5},{4,2},{5,3},{6,0},{7,1},{8,14},{9,15},{10,... | collective-permute-start | bytes 196616 | tf_op jit(solution)/shard_map/ppermute | solution.py:19
  45.2 2.7 %collective-permute-done.15.refs_2_ = f32[128,128]{1,0:T(8,128)S(1)} collective-permute-done((f32[128,128]{1,0:T(8,128)S(1)}, f32[128,128]{1,0:T(8,128)S(1)}, u32[]{:S(2)}, u32[]{:S(2)}) %collective-permute-start.15) | collective-permute-done | bytes 65568 | tf_op jit(solution)/shard_map/ppermute | solution.py:19
  47.9 1.3 %collective-permute-done.16.refs_3_ = f32[128,128]{1,0:T(8,128)S(1)} collective-permute-done((f32[128,128]{1,0:T(8,128)S(1)}, f32[128,128]{1,0:T(8,128)S(1)}, u32[]{:S(2)}, u32[]{:S(2)}) %collective-permute-start.16) | collective-permute-done | bytes 65568 | tf_op jit(solution)/shard_map/ppermute | solution.py:19
  49.3 0.7 %weight_join.1 = (f32[128,256]{1,0:T(8,128)}, f32[128,256]{1,0:T(8,128)}) custom-call(f32[128,128]{1,0:T(8,128)S(1)} %add_multiply_fusion.refs_0_, f32[128,128]{1,0:T(8,128)S(1)} %collective-permute-done.14.refs_1_, f32[128,128]{1,0:T(8,128)S(1)} %collective-permute-done.15.refs_2_, f32[128,128]{1,0:T(8,128)S(1)} %collective-permute-done.16.refs_3_), custom_call_target="tpu_custom_call" | custom-call | tf_op jit(solution)/shard_map/weight_join/pallas_call | solution.py:223
  50.0 0.0 collective-permute-done.17.refs_1_
  50.0 0.9 %source_sum.1 = f32[512,128]{1,0:T(8,128)} custom-call(f32[4,128,128]{2,1,0:T(8,128)S(1)} %get-tuple-element.26.refs_0_, bf16[4,128,128]{2,1,0:T(8,128)(2,1)S(1)} %collective-permute-done.17.refs_1_, bf16[4,128,128]{2,1,0:T(8,128)(2,1)S(1)} %collective-permute-done.18.refs_2_, bf16[4,128,128]{2,1,0:T(8,128)(2,1)S(1)} %collective-permute-done.19.refs_3_), custom_call_target="tpu_custom_call" | custom-call | tf_op jit(solution)/shard_map/source_sum/pallas_call | solution.py:233
  (19 shorter events, 0.1 us)
Async XLA Ops:
  1.3 0.7 %copy-start.7 = (s32[1,1,32]{2,1,0:T(1,128)S(1)}, s32[1,1,32]{2,1,0:T(1,128)}, u32[]{:S(2)}) copy-start(s32[1,1,32]{2,1,0:T(1,128)} %refs_0_.1) | copy-start | bytes 388
  1.3 0.7 %copy-start.8 = (s32[1,1,32]{2,1,0:T(1,128)S(1)}, s32[1,1,32]{2,1,0:T(1,128)}, u32[]{:S(2)}) copy-start(s32[1,1,32]{2,1,0:T(1,128)} %refs_1_.1) | copy-start | bytes 388
  2.0 1.2 %copy-start = (bf16[1,1,32,128,128]{4,3,2,1,0:T(8,128)(2,1)S(1)}, bf16[1,1,32,128,128]{4,3,2,1,0:T(8,128)(2,1)}, u32[]{:S(2)}) copy-start(bf16[1,1,32,128,128]{4,3,2,1,0:T(8,128)(2,1)} %refs_3_.1) | copy-start | bytes 3145732
  3.2 1.0 %copy-start.2 = (bf16[1,2048,128]{2,1,0:T(8,128)(2,1)S(1)}, bf16[1,2048,128]{2,1,0:T(8,128)(2,1)}, u32[]{:S(2)}) copy-start(bf16[1,2048,128]{2,1,0:T(8,128)(2,1)} %param.9) | copy-start | bytes 1572868
  5.3 1.7 %collective-permute-start = (f32[4,128,128]{2,1,0:T(8,128)S(1)}, f32[4,128,128]{2,1,0:T(8,128)S(1)}, u32[]{:S(2)}, u32[]{:S(2)}) collective-permute-start(f32[4,128,128]{2,1,0:T(8,128)S(1)} %get-tuple-element.18), channel_id=1, source_target_pairs={{0,1},{1,0},{2,3},{3,2},{4,5},{5,4},{6,7},{7,6},{8,9},{9,8},{10,11... | collective-permute-start | bytes 786440 | tf_op jit(solution)/shard_map/ppermute | solution.py:19
  7.0 25.6 %copy-start.1 = (bf16[1,1,32,128,128]{4,3,2,1,0:T(8,128)(2,1)S(1)}, bf16[1,1,32,128,128]{4,3,2,1,0:T(8,128)(2,1)}, u32[]{:S(2)}) copy-start(bf16[1,1,32,128,128]{4,3,2,1,0:T(8,128)(2,1)} %refs_3_.1) | copy-start | bytes 3145732
  7.0 11.9 %copy-start.3 = (bf16[128,256]{1,0:T(8,128)(2,1)S(1)}, bf16[128,256]{1,0:T(8,128)(2,1)}, u32[]{:S(2)}) copy-start(bf16[128,256]{1,0:T(8,128)(2,1)} %refs_5_.1) | copy-start | bytes 196612
  7.0 11.8 %copy-start.4 = (bf16[128,256]{1,0:T(8,128)(2,1)S(1)}, bf16[128,256]{1,0:T(8,128)(2,1)}, u32[]{:S(2)}) copy-start(bf16[128,256]{1,0:T(8,128)(2,1)} %refs_6_.1) | copy-start | bytes 196612
  7.1 11.8 %copy-start.5 = (bf16[128,256]{1,0:T(8,128)(2,1)S(1)}, bf16[128,256]{1,0:T(8,128)(2,1)}, u32[]{:S(2)}) copy-start(bf16[128,256]{1,0:T(8,128)(2,1)} %refs_7_.1) | copy-start | bytes 196612
  7.1 11.8 %copy-start.6 = (bf16[128,128]{1,0:T(8,128)(2,1)S(1)}, bf16[128,128]{1,0:T(8,128)(2,1)}, u32[]{:S(2)}) copy-start(bf16[128,128]{1,0:T(8,128)(2,1)} %refs_4_.1) | copy-start | bytes 98308
  7.1 5.6 %collective-permute-start.1 = (f32[128,128]{1,0:T(8,128)S(1)}, f32[128,128]{1,0:T(8,128)S(1)}, u32[]{:S(2)}, u32[]{:S(2)}) collective-permute-start(f32[128,128]{1,0:T(8,128)S(1)} %get-tuple-element.32), channel_id=1, source_target_pairs={{0,2},{1,3},{2,0},{3,1},{4,6},{5,7},{6,4},{7,5},{8,10},{9,11},{10,... | collective-permute-start | bytes 196616 | tf_op jit(solution)/shard_map/ppermute | solution.py:19
  10.1 7.5 %collective-permute-start.2 = (f32[128,128]{1,0:T(8,128)S(1)}, f32[128,128]{1,0:T(8,128)S(1)}, u32[]{:S(2)}, u32[]{:S(2)}) collective-permute-start(f32[128,128]{1,0:T(8,128)S(1)} %get-tuple-element.31), channel_id=1, source_target_pairs={{0,4},{1,5},{2,6},{3,7},{4,0},{5,1},{6,2},{7,3},{8,12},{9,13},{10,... | collective-permute-start | bytes 196616 | tf_op jit(solution)/shard_map/ppermute | solution.py:19
  12.7 6.2 %collective-permute-start.3 = (f32[128,128]{1,0:T(8,128)S(1)}, f32[128,128]{1,0:T(8,128)S(1)}, u32[]{:S(2)}, u32[]{:S(2)}) collective-permute-start(f32[128,128]{1,0:T(8,128)S(1)} %get-tuple-element.30), channel_id=1, source_target_pairs={{0,6},{1,7},{2,4},{3,5},{4,2},{5,3},{6,0},{7,1},{8,14},{9,15},{10,... | collective-permute-start | bytes 196616 | tf_op jit(solution)/shard_map/ppermute | solution.py:19
  19.7 6.1 %collective-permute-start.6 = (bf16[256,128]{1,0:T(8,128)(2,1)S(1)}, bf16[256,128]{1,0:T(8,128)(2,1)S(1)}, u32[]{:S(2)}, u32[]{:S(2)}) collective-permute-start(bf16[256,128]{1,0:T(8,128)(2,1)S(1)} %get-tuple-element.23), channel_id=1, source_target_pairs={{0,6},{1,7},{2,4},{3,5},{4,2},{5,3},{6,0},{7,1},{8,14},{9,15},{10,... | collective-permute-start | bytes 196616 | tf_op jit(solution)/shard_map/ppermute | solution.py:19
  21.7 5.8 %collective-permute-start.4 = (bf16[256,128]{1,0:T(8,128)(2,1)S(1)}, bf16[256,128]{1,0:T(8,128)(2,1)S(1)}, u32[]{:S(2)}, u32[]{:S(2)}) collective-permute-start(bf16[256,128]{1,0:T(8,128)(2,1)S(1)} %get-tuple-element.21), channel_id=1, source_target_pairs={{0,2},{1,3},{2,0},{3,1},{4,6},{5,7},{6,4},{7,5},{8,10},{9,11},{10,... | collective-permute-start | bytes 196616 | tf_op jit(solution)/shard_map/ppermute | solution.py:19
  22.1 5.5 %collective-permute-start.5 = (bf16[256,128]{1,0:T(8,128)(2,1)S(1)}, bf16[256,128]{1,0:T(8,128)(2,1)S(1)}, u32[]{:S(2)}, u32[]{:S(2)}) collective-permute-start(bf16[256,128]{1,0:T(8,128)(2,1)S(1)} %get-tuple-element.22), channel_id=1, source_target_pairs={{0,4},{1,5},{2,6},{3,7},{4,0},{5,1},{6,2},{7,3},{8,12},{9,13},{10,... | collective-permute-start | bytes 196616 | tf_op jit(solution)/shard_map/ppermute | solution.py:19
  24.1 4.0 %collective-permute-start.7 = (bf16[256,128]{1,0:T(8,128)(2,1)S(1)}, bf16[256,128]{1,0:T(8,128)(2,1)S(1)}, u32[]{:S(2)}, u32[]{:S(2)}) collective-permute-start(bf16[256,128]{1,0:T(8,128)(2,1)S(1)} %get-tuple-element.20.refs_0_.refs_4_), channel_id=1, source_target_pairs={{0,1},{1,0},{2,3},{3,2},{4,5},{5,4},{6,7},{7,6},{8,9},{9,8},{10,11... | collective-permute-start | bytes 196616 | tf_op jit(solution)/shard_map/ppermute | solution.py:19
  25.9 2.2 %collective-permute-start.10 = (bf16[256,128]{1,0:T(8,128)(2,1)S(1)}, bf16[256,128]{1,0:T(8,128)(2,1)S(1)}, u32[]{:S(2)}, u32[]{:S(2)}) collective-permute-start(bf16[256,128]{1,0:T(8,128)(2,1)S(1)} %collective-permute-done.6.refs_3_.refs_7_), channel_id=1, source_target_pairs={{0,1},{1,0},{2,3},{3,2},{4,5},{5,4},{6,7},{7,6},{8,9},{9,8},{10,11... | collective-permute-start | bytes 196616 | tf_op jit(solution)/shard_map/ppermute | solution.py:19
  27.6 1.3 %collective-permute-start.8 = (bf16[256,128]{1,0:T(8,128)(2,1)S(1)}, bf16[256,128]{1,0:T(8,128)(2,1)S(1)}, u32[]{:S(2)}, u32[]{:S(2)}) collective-permute-start(bf16[256,128]{1,0:T(8,128)(2,1)S(1)} %collective-permute-done.4.refs_1_.refs_5_), channel_id=1, source_target_pairs={{0,1},{1,0},{2,3},{3,2},{4,5},{5,4},{6,7},{7,6},{8,9},{9,8},{10,11... | collective-permute-start | bytes 196616 | tf_op jit(solution)/shard_map/ppermute | solution.py:19
  27.6 1.4 %collective-permute-start.9 = (bf16[256,128]{1,0:T(8,128)(2,1)S(1)}, bf16[256,128]{1,0:T(8,128)(2,1)S(1)}, u32[]{:S(2)}, u32[]{:S(2)}) collective-permute-start(bf16[256,128]{1,0:T(8,128)(2,1)S(1)} %collective-permute-done.5.refs_2_.refs_6_), channel_id=1, source_target_pairs={{0,1},{1,0},{2,3},{3,2},{4,5},{5,4},{6,7},{7,6},{8,9},{9,8},{10,11... | collective-permute-start | bytes 196616 | tf_op jit(solution)/shard_map/ppermute | solution.py:19
  29.0 4.7 %collective-permute-start.11 = (f32[128,128]{1,0:T(8,128)S(1)}, f32[128,128]{1,0:T(8,128)S(1)}, u32[]{:S(2)}, u32[]{:S(2)}) collective-permute-start(f32[128,128]{1,0:T(8,128)S(1)} %weight_sum.1), channel_id=1, source_target_pairs={{0,8},{8,0},{16,24},{24,16},{1,9},{9,1},{17,25},{25,17},{2,10},{10... | collective-permute-start | bytes 196616 | tf_op jit(solution)/shard_map/ppermute | solution.py:19
  30.6 4.3 %collective-permute-start.12 = (f32[128,128]{1,0:T(8,128)S(1)}, f32[128,128]{1,0:T(8,128)S(1)}, u32[]{:S(2)}, u32[]{:S(2)}) collective-permute-start(f32[128,128]{1,0:T(8,128)S(1)} %weight_sum.1), channel_id=1, source_target_pairs={{0,16},{8,24},{16,0},{24,8},{1,17},{9,25},{17,1},{25,9},{2,18},{10... | collective-permute-start | bytes 196616 | tf_op jit(solution)/shard_map/ppermute | solution.py:19
  32.1 5.2 %collective-permute-start.13 = (f32[128,128]{1,0:T(8,128)S(1)}, f32[128,128]{1,0:T(8,128)S(1)}, u32[]{:S(2)}, u32[]{:S(2)}) collective-permute-start(f32[128,128]{1,0:T(8,128)S(1)} %weight_sum.1), channel_id=1, source_target_pairs={{0,24},{8,16},{16,8},{24,0},{1,25},{9,17},{17,9},{25,1},{2,26},{10... | collective-permute-start | bytes 196616 | tf_op jit(solution)/shard_map/ppermute | solution.py:19
  37.3 5.8 %collective-permute-start.14 = (f32[128,128]{1,0:T(8,128)S(1)}, f32[128,128]{1,0:T(8,128)S(1)}, u32[]{:S(2)}, u32[]{:S(2)}) collective-permute-start(f32[128,128]{1,0:T(8,128)S(1)} %add_multiply_fusion.refs_0_), channel_id=1, source_target_pairs={{0,2},{1,3},{2,0},{3,1},{4,6},{5,7},{6,4},{7,5},{8,10},{9,11},{10,... | collective-permute-start | bytes 196616 | tf_op jit(solution)/shard_map/ppermute | solution.py:19
  38.5 11.4 %collective-permute-start.17 = (bf16[4,128,128]{2,1,0:T(8,128)(2,1)S(1)}, bf16[4,128,128]{2,1,0:T(8,128)(2,1)S(1)}, u32[]{:S(2)}, u32[]{:S(2)}) collective-permute-start(bf16[4,128,128]{2,1,0:T(8,128)(2,1)S(1)} %get-tuple-element.27), channel_id=1, source_target_pairs={{0,8},{8,0},{16,24},{24,16},{1,9},{9,1},{17,25},{25,17},{2,10},{10... | collective-permute-start | bytes 393224 | tf_op jit(solution)/shard_map/ppermute | solution.py:19
  39.1 10.9 %collective-permute-start.18 = (bf16[4,128,128]{2,1,0:T(8,128)(2,1)S(1)}, bf16[4,128,128]{2,1,0:T(8,128)(2,1)S(1)}, u32[]{:S(2)}, u32[]{:S(2)}) collective-permute-start(bf16[4,128,128]{2,1,0:T(8,128)(2,1)S(1)} %get-tuple-element.28), channel_id=1, source_target_pairs={{0,16},{8,24},{16,0},{24,8},{1,17},{9,25},{17,1},{25,9},{2,18},{10... | collective-permute-start | bytes 393224 | tf_op jit(solution)/shard_map/ppermute | solution.py:19
  39.6 10.4 %collective-permute-start.19 = (bf16[4,128,128]{2,1,0:T(8,128)(2,1)S(1)}, bf16[4,128,128]{2,1,0:T(8,128)(2,1)S(1)}, u32[]{:S(2)}, u32[]{:S(2)}) collective-permute-start(bf16[4,128,128]{2,1,0:T(8,128)(2,1)S(1)} %get-tuple-element.29), channel_id=1, source_target_pairs={{0,24},{8,16},{16,8},{24,0},{1,25},{9,17},{17,9},{25,1},{2,26},{10... | collective-permute-start | bytes 393224 | tf_op jit(solution)/shard_map/ppermute | solution.py:19
  42.0 5.9 %collective-permute-start.15 = (f32[128,128]{1,0:T(8,128)S(1)}, f32[128,128]{1,0:T(8,128)S(1)}, u32[]{:S(2)}, u32[]{:S(2)}) collective-permute-start(f32[128,128]{1,0:T(8,128)S(1)} %add_multiply_fusion.refs_0_), channel_id=1, source_target_pairs={{0,4},{1,5},{2,6},{3,7},{4,0},{5,1},{6,2},{7,3},{8,12},{9,13},{10,... | collective-permute-start | bytes 196616 | tf_op jit(solution)/shard_map/ppermute | solution.py:19
  43.1 6.2 %collective-permute-start.16 = (f32[128,128]{1,0:T(8,128)S(1)}, f32[128,128]{1,0:T(8,128)S(1)}, u32[]{:S(2)}, u32[]{:S(2)}) collective-permute-start(f32[128,128]{1,0:T(8,128)S(1)} %add_multiply_fusion.refs_0_), channel_id=1, source_target_pairs={{0,6},{1,7},{2,4},{3,5},{4,2},{5,3},{6,0},{7,1},{8,14},{9,15},{10,... | collective-permute-start | bytes 196616 | tf_op jit(solution)/shard_map/ppermute | solution.py:19

commit v2 on v1

--- a/solution.py
+++ b/solution.py
@@ -12,6 +12,7 @@
 BF16 = jnp.bfloat16
 VMEM = pl.BlockSpec(memory_space=pltpu.VMEM)
 SMEM = pl.BlockSpec(memory_space=pltpu.SMEM)
+HBM = pl.BlockSpec(memory_space=pltpu.HBM)
 
 
 def xor_permute(x, axis, distance):
@@ -25,13 +26,29 @@
     return terms[0]
 
 
-def forward_kernel(rows, cols, counts, values, table, mine, theirs, acc):
+def forward_kernel(
+    rows_in, cols_in, counts, values_in, table_in, mine, theirs, rows_out, cols_out, values, rows, cols, table, acc, sems
+):
     slots = values.shape[2]
     pairs = mine.shape[0]
+    parts = sems.shape[0] - 5
+    step = slots // parts
     me = lax.axis_index("col")
+    wanted = [(rows_in, rows), (cols_in, cols), (table_in, table)]
+    passed = [(rows_in, rows_out), (cols_in, cols_out)]
+    for i in range(parts):
+        piece = pl.ds(i * step, step)
+        wanted.append((values_in.at[0, 0, piece], values.at[0, 0, piece]))
+    copies = [pltpu.make_async_copy(a, b, sems.at[i]) for i, (a, b) in enumerate(wanted + passed)]
+    for copy in copies:
+        copy.start()
     acc[...] = jnp.zeros_like(acc)
+    for copy in copies[:3]:
+        copy.wait()
     live = counts[0, 0]
     for s in range(slots):
+        if s % step == 0:
+            copies[3 + s // step].wait()
         at = rows[0, 0, s] ^ me
         block = values[0, 0, s]
         block = jnp.where(s < live, block, jnp.zeros_like(block))
@@ -39,6 +56,8 @@
     for p in range(pairs):
         mine[p] = acc[2 * p]
         theirs[p] = acc[2 * p + 1]
+    for copy in copies[3 + parts :]:
+        copy.wait()
 
 
 def middle_kernel(pairs, *refs):
@@ -116,17 +135,11 @@
         sends[g - 1][...] = acc[g * share : (g + 1) * share].astype(BF16)
 
 
-def source_sum_kernel(groups, *refs):
-    out = refs[groups]
-    share, width, block = refs[0].shape
-    for b in range(share):
-        total = tree_sum([r[b].astype(F32) for r in refs[:groups]])
-        out[b * block : (b + 1) * block, :] = total.T
-
-
-def weight_join_kernel(pairs, *refs):
+def final_kernel(pairs, groups, *refs):
     chunks = refs[:pairs]
-    w_self, w_neigh, table = refs[pairs : pairs + 3]
+    terms = refs[pairs : pairs + groups]
+    held, output, w_self, w_neigh, out, table = refs[pairs + groups :]
+    output[...] = held[...]
     z = lax.axis_index("col") // 2
     share = table.shape[1]
     width = chunks[0].shape[1]
@@ -137,6 +150,14 @@
     for p in range(half):
         w_self[p * share : (p + 1) * share] = table[p]
         w_neigh[p * share : (p + 1) * share] = table[p + half]
+    blocks, _, block = terms[0].shape
+    for b in range(blocks):
+        total = tree_sum([r[b].astype(F32) for r in terms])
+        out[b * block : (b + 1) * block, :] = total.T
+
+
+def weight_total_kernel(scale, *refs):
+    refs[-1][...] = tree_sum([r[...] for r in refs[:-1]]) * scale
 
 
 def shaped(shape, dtype):
@@ -165,21 +186,33 @@
     source_blocks = table.shape[0]
     params = pltpu.CompilerParams(vmem_limit_bytes=24 * 1024 * 1024)
 
-    mine, theirs = pl.pallas_call(
+    inputs = (block_rows, block_cols, block_values, table)
+    mine, theirs, rows, cols, values = pl.pallas_call(
         forward_kernel,
-        out_shape=[shaped((pairs, block, width), F32)] * 2,
-        in_specs=[SMEM, SMEM, SMEM, VMEM, VMEM],
-        out_specs=[VMEM, VMEM],
-        scratch_shapes=[pltpu.VMEM((col_total, block, width), F32)],
+        out_shape=[shaped((pairs, block, width), F32)] * 2
+        + [shaped(x.shape, x.dtype) for x in (block_rows, block_cols, block_values)],
+        in_specs=[HBM, HBM, SMEM, HBM, HBM],
+        out_specs=[VMEM] * 5,
+        scratch_shapes=[
+            pltpu.SMEM(block_rows.shape, jnp.int32),
+            pltpu.SMEM(block_cols.shape, jnp.int32),
+            pltpu.VMEM(table.shape, BF16),
+            pltpu.VMEM((col_total, block, width), F32),
+            pltpu.SemaphoreType.DMA((9,)),
+        ],
         compiler_params=params,
         name="forward_blocks",
-    )(block_rows, block_cols, block_counts, block_values, table)
+    )(
+        *[pltpu.with_memory_space_constraint(x, pltpu.HBM) for x in inputs[:2]],
+        block_counts,
+        *[pltpu.with_memory_space_constraint(x, pltpu.HBM) for x in inputs[2:]],
+    )
     chip_sum = mine + xor_permute(theirs, "col", 1)
     sums = [chip_sum[0]] + [xor_permute(chip_sum[p], "col", 2 * p) for p in range(1, pairs)]
 
     share = 2 * width // pairs
     packed = shaped((width + hidden // width * share, width), BF16)
-    output, *payloads = pl.pallas_call(
+    held, *payloads = pl.pallas_call(
         functools.partial(middle_kernel, pairs),
         out_shape=[shaped((local, hidden), BF16)] + [packed] * pairs,
         in_specs=[VMEM] * (pairs + 4),
@@ -214,30 +247,34 @@
         ],
         compiler_params=params,
         name="backward_blocks",
-    )(block_rows, block_cols, block_counts, block_values, *near, *far)
+    )(rows, cols, block_counts, values, *near, *far)
     source_terms = [own] + [xor_permute(x, "row", g) for g, x in enumerate(sends, 1)]
 
     node_total = local * groups * col_total
-    weight_chunk = tree_sum(weight_terms) * (1.0 / math.sqrt(node_total))
-    chunks = [weight_chunk] + [xor_permute(weight_chunk, "col", 2 * p) for p in range(1, pairs)]
-    grad_self, grad_neigh = pl.pallas_call(
-        functools.partial(weight_join_kernel, pairs),
-        out_shape=[shaped((width, hidden), F32)] * 2,
-        in_specs=[VMEM] * pairs,
-        out_specs=[VMEM] * 2,
-        scratch_shapes=[pltpu.VMEM((pairs, share, hidden), F32)],
-        compiler_params=params,
-        name="weight_join",
-    )(*chunks)
-
-    grad_source = pl.pallas_call(
-        functools.partial(source_sum_kernel, groups),
-        out_shape=shaped((source_share * block, width), F32),
+    weight_chunk = pl.pallas_call(
+        functools.partial(weight_total_kernel, 1.0 / math.sqrt(node_total)),
+        out_shape=shaped(weight_part.shape, F32),
         in_specs=[VMEM] * groups,
         out_specs=VMEM,
         compiler_params=params,
-        name="source_sum",
-    )(*source_terms)
+        cost_estimate=pl.CostEstimate(flops=0, bytes_accessed=16 * 1024 * 1024, transcendentals=0),
+        name="weight_total",
+    )(*weight_terms)
+    chunks = [weight_chunk] + [xor_permute(weight_chunk, "col", 2 * p) for p in range(1, pairs)]
+    output, grad_self, grad_neigh, grad_source = pl.pallas_call(
+        functools.partial(final_kernel, pairs, groups),
+        out_shape=[
+            shaped((local, hidden), BF16),
+            shaped((width, hidden), F32),
+            shaped((width, hidden), F32),
+            shaped((source_share * block, width), F32),
+        ],
+        in_specs=[VMEM] * (pairs + groups + 1),
+        out_specs=[VMEM] * 4,
+        scratch_shapes=[pltpu.VMEM((pairs, share, hidden), F32)],
+        compiler_params=params,
+        name="join_outputs",
+    )(*chunks, *source_terms, held)
     return output, grad_self, grad_neigh, grad_source.reshape(1, -1, width)
 
 

time: 51.1 us -> 47.3 us (0.926)
  starting transfers between devices: 22.5 us -> 19 us
  local copies, waits for them, and re-layouts: 2.97 us -> 0.05 us
  waiting for transfers between devices: 19.2 us -> 21.9 us
    ppermute x20, starting transfers between devices: 22.5 us -> 19 us  [xor_permute(): return lax.ppermute(x, axis, [(i, i ^ distance) for i in range(total)])]
    unnamed x18 -> x8, local copies, waits for them, and re-layouts: 2.95 us -> 0.03 us
    ppermute x20, waiting for transfers between devices: 19.2 us -> 21.9 us  [xor_permute(): return lax.ppermute(x, axis, [(i, i ^ distance) for i in range(total)])]
    pallas_call x1, Pallas kernels: 1.08 us -> 2.21 us  [per_device(): pl.pallas_call(forward_kernel, out_shape=[shaped((pairs, block, width), F...]
    pallas_call x2, Pallas kernels: 1.6 us -> 0.91 us  [the longest x1 0.9 us: per_device(): pl.pallas_call(functools.partial(final_kernel, pairs, groups), out_shape=...]
  transfers between devices with their start and end apart: 20 -> 20, of which waited for: 11 -> 12; matrix products, arithmetic and copies ran while one was open for 0% -> 0% of each run, Pallas kernels for 4% -> 2%
where the time goes in v2:
time: 47.3 us; the launch traced here: 47.2 us
  waiting for transfers between devices  21.9 us (46%)
  starting transfers between devices  19 us (40%)
  Pallas kernels  4.76 us (10%)
  between operations  1.4 us (3%)
    ppermute x20, waiting for transfers between devices, xor_permute(): return lax.ppermute(x, axis, [(i, i ^ distance) for i in range(total)])  21.9 us
    ppermute x20, starting transfers between devices, xor_permute(): return lax.ppermute(x, axis, [(i, i ^ distance) for i in range(total)])  19 us
    pallas_call x1, Pallas kernels, per_device(): pl.pallas_call(forward_kernel, out_shape=[shaped((pairs, block, width), F...  2.21 us
    pallas_call x1, Pallas kernels, per_device(): pl.pallas_call(functools.partial(backward_kernel, pairs, groups), out_sha...  1.15 us
  transfers between devices with their start and end apart: 20, of which 12 were waited for; matrix products, arithmetic and copies ran while one was open for 0% of the time, Pallas kernels for 2%

profile of v2, /device:TPU:0, one launch (start us, length us, event | category | flops | bytes accessed | tf_op | source)
XLA Modules:
  0.0 47.2 jit_solution(13161581954445104611)
XLA Ops:
  1.3 2.2 %forward_blocks.1 = (f32[4,128,128]{2,1,0:T(8,128)S(1)}, f32[4,128,128]{2,1,0:T(8,128)S(1)}, s32[1,1,32]{2,1,0:T(1,128)S(1)}, s32[1,1,32]{2,1,0:T(1,128)S(1)}, bf16[1,1,32,128,128]{4,3,2,1,0:T(8,128)(2,1)S(1)}) custom-call(s32[1,1,32]{2,1,0:T(1,128)} %rows_in.1, s32[1,1,32]{2,1,0:T(1,128)} %cols_in.1, s32[1,1]{1,0:T(1,128)S(6)} %copy.13.counts.refs_2_, ...), custom_call_target="tpu_custom_call" | custom-call | tf_op jit(solution)/shard_map/forward_blocks/pallas_call | solution.py:190
  3.5 0.5 %collective-permute-start = (f32[4,128,128]{2,1,0:T(8,128)S(1)}, f32[4,128,128]{2,1,0:T(8,128)S(1)}, u32[]{:S(2)}, u32[]{:S(2)}) collective-permute-start(f32[4,128,128]{2,1,0:T(8,128)S(1)} %get-tuple-element.23), channel_id=1, source_target_pairs={{0,1},{1,0},{2,3},{3,2},{4,5},{5,4},{6,7},{7,6},{8,9},{9,8},{10,11... | collective-permute-start | bytes 786440 | tf_op jit(solution)/shard_map/ppermute | solution.py:20
  4.0 1.2 %collective-permute-done = f32[4,128,128]{2,1,0:T(8,128)S(1)} collective-permute-done((f32[4,128,128]{2,1,0:T(8,128)S(1)}, f32[4,128,128]{2,1,0:T(8,128)S(1)}, u32[]{:S(2)}, u32[]{:S(2)}) %collective-permute-start) | collective-permute-done | bytes 262176 | tf_op jit(solution)/shard_map/ppermute | solution.py:20
  5.2 0.0 copy-start
  5.2 0.0 copy-start.1
  5.2 0.0 copy-start.2
  5.3 0.0 copy-start.3
  5.3 5.0 %collective-permute-start.3 = (f32[128,128]{1,0:T(8,128)S(1)}, f32[128,128]{1,0:T(8,128)S(1)}, u32[]{:S(2)}, u32[]{:S(2)}) collective-permute-start(f32[128,128]{1,0:T(8,128)S(1)} %get-tuple-element.40), channel_id=1, source_target_pairs={{0,6},{1,7},{2,4},{3,5},{4,2},{5,3},{6,0},{7,1},{8,14},{9,15},{10,... | collective-permute-start | bytes 196616 | tf_op jit(solution)/shard_map/ppermute | solution.py:20
  10.3 0.0 collective-permute-start.2
  10.3 0.6 %collective-permute-start.1 = (f32[128,128]{1,0:T(8,128)S(1)}, f32[128,128]{1,0:T(8,128)S(1)}, u32[]{:S(2)}, u32[]{:S(2)}) collective-permute-start(f32[128,128]{1,0:T(8,128)S(1)} %get-tuple-element.42), channel_id=1, source_target_pairs={{0,2},{1,3},{2,0},{3,1},{4,6},{5,7},{6,4},{7,5},{8,10},{9,11},{10,... | collective-permute-start | bytes 196616 | tf_op jit(solution)/shard_map/ppermute | solution.py:20
  11.0 2.0 %collective-permute-done.3.refs_3_ = f32[128,128]{1,0:T(8,128)S(1)} collective-permute-done((f32[128,128]{1,0:T(8,128)S(1)}, f32[128,128]{1,0:T(8,128)S(1)}, u32[]{:S(2)}, u32[]{:S(2)}) %collective-permute-start.3) | collective-permute-done | bytes 65568 | tf_op jit(solution)/shard_map/ppermute | solution.py:20
  13.0 3.3 %collective-permute-done.2.refs_2_ = f32[128,128]{1,0:T(8,128)S(1)} collective-permute-done((f32[128,128]{1,0:T(8,128)S(1)}, f32[128,128]{1,0:T(8,128)S(1)}, u32[]{:S(2)}, u32[]{:S(2)}) %collective-permute-start.2) | collective-permute-done | bytes 65568 | tf_op jit(solution)/shard_map/ppermute | solution.py:20
  16.2 0.0 collective-permute-done.1.refs_1_
  16.3 0.4 dense_layer.1
  16.7 1.1 %collective-permute-start.4 = (bf16[256,128]{1,0:T(8,128)(2,1)S(1)}, bf16[256,128]{1,0:T(8,128)(2,1)S(1)}, u32[]{:S(2)}, u32[]{:S(2)}) collective-permute-start(bf16[256,128]{1,0:T(8,128)(2,1)S(1)} %get-tuple-element.25), channel_id=1, source_target_pairs={{0,2},{1,3},{2,0},{3,1},{4,6},{5,7},{6,4},{7,5},{8,10},{9,11},{10,... | collective-permute-start | bytes 196616 | tf_op jit(solution)/shard_map/ppermute | solution.py:20
  17.9 2.0 %collective-permute-start.5 = (bf16[256,128]{1,0:T(8,128)(2,1)S(1)}, bf16[256,128]{1,0:T(8,128)(2,1)S(1)}, u32[]{:S(2)}, u32[]{:S(2)}) collective-permute-start(bf16[256,128]{1,0:T(8,128)(2,1)S(1)} %get-tuple-element.26), channel_id=1, source_target_pairs={{0,4},{1,5},{2,6},{3,7},{4,0},{5,1},{6,2},{7,3},{8,12},{9,13},{10,... | collective-permute-start | bytes 196616 | tf_op jit(solution)/shard_map/ppermute | solution.py:20
  19.8 1.4 %collective-permute-start.6 = (bf16[256,128]{1,0:T(8,128)(2,1)S(1)}, bf16[256,128]{1,0:T(8,128)(2,1)S(1)}, u32[]{:S(2)}, u32[]{:S(2)}) collective-permute-start(bf16[256,128]{1,0:T(8,128)(2,1)S(1)} %get-tuple-element.27), channel_id=1, source_target_pairs={{0,6},{1,7},{2,4},{3,5},{4,2},{5,3},{6,0},{7,1},{8,14},{9,15},{10,... | collective-permute-start | bytes 196616 | tf_op jit(solution)/shard_map/ppermute | solution.py:20
  21.2 0.0 collective-permute-start.7
  21.2 0.3 collective-permute-done.4.refs_1_.refs_5_
  21.5 0.2 collective-permute-start.8
  21.7 2.9 %collective-permute-done.5.refs_2_.refs_6_ = bf16[256,128]{1,0:T(8,128)(2,1)S(1)} collective-permute-done((bf16[256,128]{1,0:T(8,128)(2,1)S(1)}, bf16[256,128]{1,0:T(8,128)(2,1)S(1)}, u32[]{:S(2)}, u32[]{:S(2)}) %collective-permute-start.5) | collective-permute-done | bytes 65568 | tf_op jit(solution)/shard_map/ppermute | solution.py:20
  24.5 0.0 collective-permute-start.9
  24.6 1.4 %collective-permute-done.6.refs_3_.refs_7_ = bf16[256,128]{1,0:T(8,128)(2,1)S(1)} collective-permute-done((bf16[256,128]{1,0:T(8,128)(2,1)S(1)}, bf16[256,128]{1,0:T(8,128)(2,1)S(1)}, u32[]{:S(2)}, u32[]{:S(2)}) %collective-permute-start.6) | collective-permute-done | bytes 65568 | tf_op jit(solution)/shard_map/ppermute | solution.py:20
  26.0 0.0 collective-permute-start.10
  26.0 0.0 collective-permute-done.7.refs_4_.refs_8_
  26.0 0.0 collective-permute-done.8.refs_5_.refs_9_
  26.0 0.0 collective-permute-done.9.refs_6_.refs_10_
  26.0 1.2 %collective-permute-done.10.refs_7_.refs_11_ = bf16[256,128]{1,0:T(8,128)(2,1)S(1)} collective-permute-done((bf16[256,128]{1,0:T(8,128)(2,1)S(1)}, bf16[256,128]{1,0:T(8,128)(2,1)S(1)}, u32[]{:S(2)}, u32[]{:S(2)}) %collective-permute-start.10) | collective-permute-done | bytes 65568 | tf_op jit(solution)/shard_map/ppermute | solution.py:20
  27.2 2.5 %collective-permute-start.13 = (f32[128,128]{1,0:T(8,128)S(1)}, f32[128,128]{1,0:T(8,128)S(1)}, u32[]{:S(2)}, u32[]{:S(2)}) collective-permute-start(f32[128,128]{1,0:T(8,128)S(1)} %weight_sum.1.refs_0_), channel_id=1, source_target_pairs={{0,24},{8,16},{16,8},{24,0},{1,25},{9,17},{17,9},{25,1},{2,26},{10... | collective-permute-start | bytes 196616 | tf_op jit(solution)/shard_map/ppermute | solution.py:20
  29.7 0.5 %collective-permute-start.12 = (f32[128,128]{1,0:T(8,128)S(1)}, f32[128,128]{1,0:T(8,128)S(1)}, u32[]{:S(2)}, u32[]{:S(2)}) collective-permute-start(f32[128,128]{1,0:T(8,128)S(1)} %weight_sum.1.refs_0_), channel_id=1, source_target_pairs={{0,16},{8,24},{16,0},{24,8},{1,17},{9,25},{17,1},{25,9},{2,18},{10... | collective-permute-start | bytes 196616 | tf_op jit(solution)/shard_map/ppermute | solution.py:20
  30.2 0.6 %collective-permute-start.11 = (f32[128,128]{1,0:T(8,128)S(1)}, f32[128,128]{1,0:T(8,128)S(1)}, u32[]{:S(2)}, u32[]{:S(2)}) collective-permute-start(f32[128,128]{1,0:T(8,128)S(1)} %weight_sum.1.refs_0_), channel_id=1, source_target_pairs={{0,8},{8,0},{16,24},{24,16},{1,9},{9,1},{17,25},{25,17},{2,10},{10... | collective-permute-start | bytes 196616 | tf_op jit(solution)/shard_map/ppermute | solution.py:20
  30.8 1.2 %backward_blocks.1 = (f32[4,128,128]{2,1,0:T(8,128)S(1)}, bf16[4,128,128]{2,1,0:T(8,128)(2,1)S(1)}, bf16[4,128,128]{2,1,0:T(8,128)(2,1)S(1)}, bf16[4,128,128]{2,1,0:T(8,128)(2,1)S(1)}) custom-call(s32[1,1,32]{2,1,0:T(1,128)S(1)} %get-tuple-element.28.refs_0_, s32[1,1,32]{2,1,0:T(1,128)S(1)} %get-tuple-element.29.refs_1_, s32[1,1]{1,0:T(1,128)S(6)} %copy.13.counts.refs_2_, ...), custom_call_target="tpu_custom_call" | custom-call | tf_op jit(solution)/shard_map/backward_blocks/pallas_call | solution.py:238
  32.0 1.5 %collective-permute-start.17 = (bf16[4,128,128]{2,1,0:T(8,128)(2,1)S(1)}, bf16[4,128,128]{2,1,0:T(8,128)(2,1)S(1)}, u32[]{:S(2)}, u32[]{:S(2)}) collective-permute-start(bf16[4,128,128]{2,1,0:T(8,128)(2,1)S(1)} %get-tuple-element.32), channel_id=1, source_target_pairs={{0,8},{8,0},{16,24},{24,16},{1,9},{9,1},{17,25},{25,17},{2,10},{10... | collective-permute-start | bytes 393224 | tf_op jit(solution)/shard_map/ppermute | solution.py:20
  33.5 0.0 collective-permute-done.13.refs_3_
  33.5 0.5 %collective-permute-done.12.refs_2_ = f32[128,128]{1,0:T(8,128)S(1)} collective-permute-done((f32[128,128]{1,0:T(8,128)S(1)}, f32[128,128]{1,0:T(8,128)S(1)}, u32[]{:S(2)}, u32[]{:S(2)}) %collective-permute-start.12) | collective-permute-done | bytes 65568 | tf_op jit(solution)/shard_map/ppermute | solution.py:20
  34.0 1.1 %collective-permute-done.11.refs_1_ = f32[128,128]{1,0:T(8,128)S(1)} collective-permute-done((f32[128,128]{1,0:T(8,128)S(1)}, f32[128,128]{1,0:T(8,128)S(1)}, u32[]{:S(2)}, u32[]{:S(2)}) %collective-permute-start.11) | collective-permute-done | bytes 65568 | tf_op jit(solution)/shard_map/ppermute | solution.py:20
  35.1 1.4 %collective-permute-start.16 = (f32[128,128]{1,0:T(8,128)S(1)}, f32[128,128]{1,0:T(8,128)S(1)}, u32[]{:S(2)}, u32[]{:S(2)}) collective-permute-start(f32[128,128]{1,0:T(8,128)S(1)} %weight_total.1.refs_0_), channel_id=1, source_target_pairs={{0,6},{1,7},{2,4},{3,5},{4,2},{5,3},{6,0},{7,1},{8,14},{9,15},{10,... | collective-permute-start | bytes 196616 | tf_op jit(solution)/shard_map/ppermute | solution.py:20
  36.5 1.5 %collective-permute-start.18 = (bf16[4,128,128]{2,1,0:T(8,128)(2,1)S(1)}, bf16[4,128,128]{2,1,0:T(8,128)(2,1)S(1)}, u32[]{:S(2)}, u32[]{:S(2)}) collective-permute-start(bf16[4,128,128]{2,1,0:T(8,128)(2,1)S(1)} %get-tuple-element.33), channel_id=1, source_target_pairs={{0,16},{8,24},{16,0},{24,8},{1,17},{9,25},{17,1},{25,9},{2,18},{10... | collective-permute-start | bytes 393224 | tf_op jit(solution)/shard_map/ppermute | solution.py:20
  38.0 0.1 collective-permute-start.19
  38.2 0.0 collective-permute-start.15
  38.2 3.8 %collective-permute-done.16.refs_3_ = f32[128,128]{1,0:T(8,128)S(1)} collective-permute-done((f32[128,128]{1,0:T(8,128)S(1)}, f32[128,128]{1,0:T(8,128)S(1)}, u32[]{:S(2)}, u32[]{:S(2)}) %collective-permute-start.16) | collective-permute-done | bytes 65568 | tf_op jit(solution)/shard_map/ppermute | solution.py:20
  42.0 0.0 collective-permute-start.14
  42.0 2.1 %collective-permute-done.15.refs_2_ = f32[128,128]{1,0:T(8,128)S(1)} collective-permute-done((f32[128,128]{1,0:T(8,128)S(1)}, f32[128,128]{1,0:T(8,128)S(1)}, u32[]{:S(2)}, u32[]{:S(2)}) %collective-permute-start.15) | collective-permute-done | bytes 65568 | tf_op jit(solution)/shard_map/ppermute | solution.py:20
  44.0 2.2 %collective-permute-done.14.refs_1_ = f32[128,128]{1,0:T(8,128)S(1)} collective-permute-done((f32[128,128]{1,0:T(8,128)S(1)}, f32[128,128]{1,0:T(8,128)S(1)}, u32[]{:S(2)}, u32[]{:S(2)}) %collective-permute-start.14) | collective-permute-done | bytes 65568 | tf_op jit(solution)/shard_map/ppermute | solution.py:20
  46.2 0.0 collective-permute-done.17.refs_5_
  46.2 0.0 collective-permute-done.18.refs_6_
  46.3 0.0 collective-permute-done.19.refs_7_
  46.3 0.9 %join_outputs.1 = (bf16[128,256]{1,0:T(8,128)(2,1)}, f32[128,256]{1,0:T(8,128)}, f32[128,256]{1,0:T(8,128)}, f32[512,128]{1,0:T(8,128)}) custom-call(f32[128,128]{1,0:T(8,128)S(1)} %weight_total.1.refs_0_, f32[128,128]{1,0:T(8,128)S(1)} %collective-permute-done.14.refs_1_, f32[128,128]{1,0:T(8,128)S(1)} %collective-permute-done.15.refs_2_, ...), custom_call_target="tpu_custom_call" | custom-call | tf_op jit(solution)/shard_map/join_outputs/pallas_call | solution.py:264
  (8 shorter events, 0.1 us)
Async XLA Ops:
  3.5 1.7 %collective-permute-start = (f32[4,128,128]{2,1,0:T(8,128)S(1)}, f32[4,128,128]{2,1,0:T(8,128)S(1)}, u32[]{:S(2)}, u32[]{:S(2)}) collective-permute-start(f32[4,128,128]{2,1,0:T(8,128)S(1)} %get-tuple-element.23), channel_id=1, source_target_pairs={{0,1},{1,0},{2,3},{3,2},{4,5},{5,4},{6,7},{7,6},{8,9},{9,8},{10,11... | collective-permute-start | bytes 786440 | tf_op jit(solution)/shard_map/ppermute | solution.py:20
  5.2 11.0 %copy-start = (bf16[128,256]{1,0:T(8,128)(2,1)S(1)}, bf16[128,256]{1,0:T(8,128)(2,1)}, u32[]{:S(2)}) copy-start(bf16[128,256]{1,0:T(8,128)(2,1)} %refs_5_.1) | copy-start | bytes 196612
  5.2 11.0 %copy-start.1 = (bf16[128,256]{1,0:T(8,128)(2,1)S(1)}, bf16[128,256]{1,0:T(8,128)(2,1)}, u32[]{:S(2)}) copy-start(bf16[128,256]{1,0:T(8,128)(2,1)} %refs_6_.1) | copy-start | bytes 196612
  5.2 11.0 %copy-start.2 = (bf16[128,256]{1,0:T(8,128)(2,1)S(1)}, bf16[128,256]{1,0:T(8,128)(2,1)}, u32[]{:S(2)}) copy-start(bf16[128,256]{1,0:T(8,128)(2,1)} %refs_7_.1) | copy-start | bytes 196612
  5.3 11.0 %copy-start.3 = (bf16[128,128]{1,0:T(8,128)(2,1)S(1)}, bf16[128,128]{1,0:T(8,128)(2,1)}, u32[]{:S(2)}) copy-start(bf16[128,128]{1,0:T(8,128)(2,1)} %refs_4_.1) | copy-start | bytes 98308
  5.3 7.7 %collective-permute-start.3 = (f32[128,128]{1,0:T(8,128)S(1)}, f32[128,128]{1,0:T(8,128)S(1)}, u32[]{:S(2)}, u32[]{:S(2)}) collective-permute-start(f32[128,128]{1,0:T(8,128)S(1)} %get-tuple-element.40), channel_id=1, source_target_pairs={{0,6},{1,7},{2,4},{3,5},{4,2},{5,3},{6,0},{7,1},{8,14},{9,15},{10,... | collective-permute-start | bytes 196616 | tf_op jit(solution)/shard_map/ppermute | solution.py:20
  10.3 5.9 %collective-permute-start.2 = (f32[128,128]{1,0:T(8,128)S(1)}, f32[128,128]{1,0:T(8,128)S(1)}, u32[]{:S(2)}, u32[]{:S(2)}) collective-permute-start(f32[128,128]{1,0:T(8,128)S(1)} %get-tuple-element.41), channel_id=1, source_target_pairs={{0,4},{1,5},{2,6},{3,7},{4,0},{5,1},{6,2},{7,3},{8,12},{9,13},{10,... | collective-permute-start | bytes 196616 | tf_op jit(solution)/shard_map/ppermute | solution.py:20
  10.3 5.9 %collective-permute-start.1 = (f32[128,128]{1,0:T(8,128)S(1)}, f32[128,128]{1,0:T(8,128)S(1)}, u32[]{:S(2)}, u32[]{:S(2)}) collective-permute-start(f32[128,128]{1,0:T(8,128)S(1)} %get-tuple-element.42), channel_id=1, source_target_pairs={{0,2},{1,3},{2,0},{3,1},{4,6},{5,7},{6,4},{7,5},{8,10},{9,11},{10,... | collective-permute-start | bytes 196616 | tf_op jit(solution)/shard_map/ppermute | solution.py:20
  16.7 4.8 %collective-permute-start.4 = (bf16[256,128]{1,0:T(8,128)(2,1)S(1)}, bf16[256,128]{1,0:T(8,128)(2,1)S(1)}, u32[]{:S(2)}, u32[]{:S(2)}) collective-permute-start(bf16[256,128]{1,0:T(8,128)(2,1)S(1)} %get-tuple-element.25), channel_id=1, source_target_pairs={{0,2},{1,3},{2,0},{3,1},{4,6},{5,7},{6,4},{7,5},{8,10},{9,11},{10,... | collective-permute-start | bytes 196616 | tf_op jit(solution)/shard_map/ppermute | solution.py:20
  17.9 6.7 %collective-permute-start.5 = (bf16[256,128]{1,0:T(8,128)(2,1)S(1)}, bf16[256,128]{1,0:T(8,128)(2,1)S(1)}, u32[]{:S(2)}, u32[]{:S(2)}) collective-permute-start(bf16[256,128]{1,0:T(8,128)(2,1)S(1)} %get-tuple-element.26), channel_id=1, source_target_pairs={{0,4},{1,5},{2,6},{3,7},{4,0},{5,1},{6,2},{7,3},{8,12},{9,13},{10,... | collective-permute-start | bytes 196616 | tf_op jit(solution)/shard_map/ppermute | solution.py:20
  19.8 6.1 %collective-permute-start.6 = (bf16[256,128]{1,0:T(8,128)(2,1)S(1)}, bf16[256,128]{1,0:T(8,128)(2,1)S(1)}, u32[]{:S(2)}, u32[]{:S(2)}) collective-permute-start(bf16[256,128]{1,0:T(8,128)(2,1)S(1)} %get-tuple-element.27), channel_id=1, source_target_pairs={{0,6},{1,7},{2,4},{3,5},{4,2},{5,3},{6,0},{7,1},{8,14},{9,15},{10,... | collective-permute-start | bytes 196616 | tf_op jit(solution)/shard_map/ppermute | solution.py:20
  21.2 4.8 %collective-permute-start.7 = (bf16[256,128]{1,0:T(8,128)(2,1)S(1)}, bf16[256,128]{1,0:T(8,128)(2,1)S(1)}, u32[]{:S(2)}, u32[]{:S(2)}) collective-permute-start(bf16[256,128]{1,0:T(8,128)(2,1)S(1)} %get-tuple-element.24.refs_0_.refs_4_), channel_id=1, source_target_pairs={{0,1},{1,0},{2,3},{3,2},{4,5},{5,4},{6,7},{7,6},{8,9},{9,8},{10,11... | collective-permute-start | bytes 196616 | tf_op jit(solution)/shard_map/ppermute | solution.py:20
  21.5 4.5 %collective-permute-start.8 = (bf16[256,128]{1,0:T(8,128)(2,1)S(1)}, bf16[256,128]{1,0:T(8,128)(2,1)S(1)}, u32[]{:S(2)}, u32[]{:S(2)}) collective-permute-start(bf16[256,128]{1,0:T(8,128)(2,1)S(1)} %collective-permute-done.4.refs_1_.refs_5_), channel_id=1, source_target_pairs={{0,1},{1,0},{2,3},{3,2},{4,5},{5,4},{6,7},{7,6},{8,9},{9,8},{10,11... | collective-permute-start | bytes 196616 | tf_op jit(solution)/shard_map/ppermute | solution.py:20
  24.5 1.4 %collective-permute-start.9 = (bf16[256,128]{1,0:T(8,128)(2,1)S(1)}, bf16[256,128]{1,0:T(8,128)(2,1)S(1)}, u32[]{:S(2)}, u32[]{:S(2)}) collective-permute-start(bf16[256,128]{1,0:T(8,128)(2,1)S(1)} %collective-permute-done.5.refs_2_.refs_6_), channel_id=1, source_target_pairs={{0,1},{1,0},{2,3},{3,2},{4,5},{5,4},{6,7},{7,6},{8,9},{9,8},{10,11... | collective-permute-start | bytes 196616 | tf_op jit(solution)/shard_map/ppermute | solution.py:20
  26.0 1.3 %collective-permute-start.10 = (bf16[256,128]{1,0:T(8,128)(2,1)S(1)}, bf16[256,128]{1,0:T(8,128)(2,1)S(1)}, u32[]{:S(2)}, u32[]{:S(2)}) collective-permute-start(bf16[256,128]{1,0:T(8,128)(2,1)S(1)} %collective-permute-done.6.refs_3_.refs_7_), channel_id=1, source_target_pairs={{0,1},{1,0},{2,3},{3,2},{4,5},{5,4},{6,7},{7,6},{8,9},{9,8},{10,11... | collective-permute-start | bytes 196616 | tf_op jit(solution)/shard_map/ppermute | solution.py:20
  27.2 6.3 %collective-permute-start.13 = (f32[128,128]{1,0:T(8,128)S(1)}, f32[128,128]{1,0:T(8,128)S(1)}, u32[]{:S(2)}, u32[]{:S(2)}) collective-permute-start(f32[128,128]{1,0:T(8,128)S(1)} %weight_sum.1.refs_0_), channel_id=1, source_target_pairs={{0,24},{8,16},{16,8},{24,0},{1,25},{9,17},{17,9},{25,1},{2,26},{10... | collective-permute-start | bytes 196616 | tf_op jit(solution)/shard_map/ppermute | solution.py:20
  29.7 4.3 %collective-permute-start.12 = (f32[128,128]{1,0:T(8,128)S(1)}, f32[128,128]{1,0:T(8,128)S(1)}, u32[]{:S(2)}, u32[]{:S(2)}) collective-permute-start(f32[128,128]{1,0:T(8,128)S(1)} %weight_sum.1.refs_0_), channel_id=1, source_target_pairs={{0,16},{8,24},{16,0},{24,8},{1,17},{9,25},{17,1},{25,9},{2,18},{10... | collective-permute-start | bytes 196616 | tf_op jit(solution)/shard_map/ppermute | solution.py:20
  30.2 4.8 %collective-permute-start.11 = (f32[128,128]{1,0:T(8,128)S(1)}, f32[128,128]{1,0:T(8,128)S(1)}, u32[]{:S(2)}, u32[]{:S(2)}) collective-permute-start(f32[128,128]{1,0:T(8,128)S(1)} %weight_sum.1.refs_0_), channel_id=1, source_target_pairs={{0,8},{8,0},{16,24},{24,16},{1,9},{9,1},{17,25},{25,17},{2,10},{10... | collective-permute-start | bytes 196616 | tf_op jit(solution)/shard_map/ppermute | solution.py:20
  32.0 14.3 %collective-permute-start.17 = (bf16[4,128,128]{2,1,0:T(8,128)(2,1)S(1)}, bf16[4,128,128]{2,1,0:T(8,128)(2,1)S(1)}, u32[]{:S(2)}, u32[]{:S(2)}) collective-permute-start(bf16[4,128,128]{2,1,0:T(8,128)(2,1)S(1)} %get-tuple-element.32), channel_id=1, source_target_pairs={{0,8},{8,0},{16,24},{24,16},{1,9},{9,1},{17,25},{25,17},{2,10},{10... | collective-permute-start | bytes 393224 | tf_op jit(solution)/shard_map/ppermute | solution.py:20
  35.1 6.9 %collective-permute-start.16 = (f32[128,128]{1,0:T(8,128)S(1)}, f32[128,128]{1,0:T(8,128)S(1)}, u32[]{:S(2)}, u32[]{:S(2)}) collective-permute-start(f32[128,128]{1,0:T(8,128)S(1)} %weight_total.1.refs_0_), channel_id=1, source_target_pairs={{0,6},{1,7},{2,4},{3,5},{4,2},{5,3},{6,0},{7,1},{8,14},{9,15},{10,... | collective-permute-start | bytes 196616 | tf_op jit(solution)/shard_map/ppermute | solution.py:20
  36.5 9.7 %collective-permute-start.18 = (bf16[4,128,128]{2,1,0:T(8,128)(2,1)S(1)}, bf16[4,128,128]{2,1,0:T(8,128)(2,1)S(1)}, u32[]{:S(2)}, u32[]{:S(2)}) collective-permute-start(bf16[4,128,128]{2,1,0:T(8,128)(2,1)S(1)} %get-tuple-element.33), channel_id=1, source_target_pairs={{0,16},{8,24},{16,0},{24,8},{1,17},{9,25},{17,1},{25,9},{2,18},{10... | collective-permute-start | bytes 393224 | tf_op jit(solution)/shard_map/ppermute | solution.py:20
  38.0 8.2 %collective-permute-start.19 = (bf16[4,128,128]{2,1,0:T(8,128)(2,1)S(1)}, bf16[4,128,128]{2,1,0:T(8,128)(2,1)S(1)}, u32[]{:S(2)}, u32[]{:S(2)}) collective-permute-start(bf16[4,128,128]{2,1,0:T(8,128)(2,1)S(1)} %get-tuple-element.34), channel_id=1, source_target_pairs={{0,24},{8,16},{16,8},{24,0},{1,25},{9,17},{17,9},{25,1},{2,26},{10... | collective-permute-start | bytes 393224 | tf_op jit(solution)/shard_map/ppermute | solution.py:20
  38.2 5.9 %collective-permute-start.15 = (f32[128,128]{1,0:T(8,128)S(1)}, f32[128,128]{1,0:T(8,128)S(1)}, u32[]{:S(2)}, u32[]{:S(2)}) collective-permute-start(f32[128,128]{1,0:T(8,128)S(1)} %weight_total.1.refs_0_), channel_id=1, source_target_pairs={{0,4},{1,5},{2,6},{3,7},{4,0},{5,1},{6,2},{7,3},{8,12},{9,13},{10,... | collective-permute-start | bytes 196616 | tf_op jit(solution)/shard_map/ppermute | solution.py:20
  42.0 4.3 %collective-permute-start.14 = (f32[128,128]{1,0:T(8,128)S(1)}, f32[128,128]{1,0:T(8,128)S(1)}, u32[]{:S(2)}, u32[]{:S(2)}) collective-permute-start(f32[128,128]{1,0:T(8,128)S(1)} %weight_total.1.refs_0_), channel_id=1, source_target_pairs={{0,2},{1,3},{2,0},{3,1},{4,6},{5,7},{6,4},{7,5},{8,10},{9,11},{10,... | collective-permute-start | bytes 196616 | tf_op jit(solution)/shard_map/ppermute | solution.py:20

commit v3 on v2

--- a/solution.py
+++ b/solution.py
@@ -13,6 +13,7 @@
 VMEM = pl.BlockSpec(memory_space=pltpu.VMEM)
 SMEM = pl.BlockSpec(memory_space=pltpu.SMEM)
 HBM = pl.BlockSpec(memory_space=pltpu.HBM)
+ANY = pl.BlockSpec(memory_space=pl.ANY)
 
 
 def xor_permute(x, axis, distance):
@@ -62,50 +63,38 @@
 
 def middle_kernel(pairs, *refs):
     sums = refs[:pairs]
-    dst, w_self, w_neigh, cot, output = refs[pairs : pairs + 5]
-    payloads = refs[pairs + 5 : 2 * pairs + 5]
-    weights = refs[2 * pairs + 5]
-    z = lax.axis_index("col") // 2
-    width = dst.shape[1]
-    hidden = w_self.shape[1]
+    dst, w_self, w_neigh, cot, output, grad_t, grad_pre, aggregate = refs[pairs:]
     agg = tree_sum([ref[...] for ref in sums]).astype(BF16)
-    own = dst[...]
-    pre = jnp.dot(own, w_self[...], preferred_element_type=F32) + jnp.dot(
+    aggregate[...] = agg
+    pre = jnp.dot(dst[...], w_self[...], preferred_element_type=F32) + jnp.dot(
         agg, w_neigh[...], preferred_element_type=F32
     )
     sig = jax.nn.sigmoid(pre)
     output[...] = (pre * sig).astype(BF16)
-    grad_pre = (cot[...].astype(F32) * sig * (1.0 + pre * (1.0 - sig))).astype(BF16)
-    grad_t = lax.dot_general(
-        w_neigh[...], grad_pre, (((1,), (1,)), ((), ())), preferred_element_type=F32
+    grad = (cot[...].astype(F32) * sig * (1.0 + pre * (1.0 - sig))).astype(BF16)
+    grad_pre[...] = grad
+    grad_t[...] = lax.dot_general(
+        w_neigh[...], grad, (((1,), (1,)), ((), ())), preferred_element_type=F32
     ).astype(BF16)
+
+
+def weight_kernel(dst, aggregate, grad_pre, mine, theirs):
     nodes = (((0,), (0,)), ((), ()))
-    share = weights.shape[1]
-    w_both = [
-        lax.dot_general(own, grad_pre, nodes, preferred_element_type=F32),
-        lax.dot_general(agg, grad_pre, nodes, preferred_element_type=F32),
-    ]
-    for p in range(pairs):
-        first = p * share
-        weights[p] = w_both[first // width][first % width : first % width + share].astype(BF16)
-    halves = hidden // width
-    for p in range(pairs):
-        payloads[p][:width] = grad_t
-        chunk = weights[z ^ p]
-        for h in range(halves):
-            payloads[p][width + h * share : width + (h + 1) * share] = chunk[
-                :, h * width : (h + 1) * width
-            ]
-
-
-def weight_sum_kernel(count, *refs):
-    near, far, total = refs[:count], refs[count : 2 * count], refs[2 * count]
-    width = total.shape[1]
-
-    def chunk(ref):
-        return ref[width:].astype(F32)
-
-    total[...] = tree_sum([chunk(r) for r in near]) + tree_sum([chunk(r) for r in far])
+    grad = grad_pre[...]
+    for_self = lax.dot_general(dst[...], grad, nodes, preferred_element_type=F32)
+    for_neigh = lax.dot_general(aggregate[...], grad, nodes, preferred_element_type=F32)
+    first_core = lax.axis_index("col") % 2 == 0
+    mine[...] = jnp.where(first_core, for_self, for_neigh)
+    theirs[...] = jnp.where(first_core, for_neigh, for_self)
+
+
+def weight_fold_kernel(own, received, after, total):
+    total[...] = (own[...] + received[...]).astype(BF16)
+
+
+def weight_total_kernel(scale, count, *refs):
+    total = tree_sum([r[...].astype(F32) for r in refs[:count]]) * scale
+    refs[-1][...] = total.astype(refs[-1].dtype)
 
 
 def backward_kernel(pairs, groups, *refs):
@@ -121,8 +110,8 @@
     me = lax.axis_index("col")
     group = lax.axis_index("row")
     for p in range(pairs):
-        table[2 * p] = near[p][:width]
-        table[2 * p + 1] = far[p][:width]
+        table[2 * p] = near[p][...]
+        table[2 * p + 1] = far[p][...]
     acc[...] = jnp.zeros_like(acc)
     live = counts[0, 0]
     for s in range(slots):
@@ -135,29 +124,23 @@
         sends[g - 1][...] = acc[g * share : (g + 1) * share].astype(BF16)
 
 
-def final_kernel(pairs, groups, *refs):
-    chunks = refs[:pairs]
-    terms = refs[pairs : pairs + groups]
-    held, output, w_self, w_neigh, out, table = refs[pairs + groups :]
+def final_kernel(groups, *refs):
+    weight_mine, weight_theirs, held = refs[:3]
+    terms = refs[3 : 3 + groups]
+    output, w_self, w_neigh, out = refs[3 + groups :]
     output[...] = held[...]
-    z = lax.axis_index("col") // 2
-    share = table.shape[1]
-    width = chunks[0].shape[1]
-    for p in range(pairs):
-        for h in range(chunks[0].shape[0] // share):
-            table[z ^ p, :, h * width : (h + 1) * width] = chunks[p][h * share : (h + 1) * share]
-    half = pairs // 2
-    for p in range(half):
-        w_self[p * share : (p + 1) * share] = table[p]
-        w_neigh[p * share : (p + 1) * share] = table[p + half]
+    first_core = lax.axis_index("col") % 2 == 0
+    mine, theirs = weight_mine[...], weight_theirs[...]
+    w_self[...] = jnp.where(first_core, mine, theirs)
+    w_neigh[...] = jnp.where(first_core, theirs, mine)
     blocks, _, block = terms[0].shape
     for b in range(blocks):
         total = tree_sum([r[b].astype(F32) for r in terms])
         out[b * block : (b + 1) * block, :] = total.T
 
 
-def weight_total_kernel(scale, *refs):
-    refs[-1][...] = tree_sum([r[...] for r in refs[:-1]]) * scale
+def busy(mib):
+    return pl.CostEstimate(flops=0, bytes_accessed=mib * 1024 * 1024, transcendentals=0)
 
 
 def shaped(shape, dtype):
@@ -210,30 +193,51 @@
     chip_sum = mine + xor_permute(theirs, "col", 1)
     sums = [chip_sum[0]] + [xor_permute(chip_sum[p], "col", 2 * p) for p in range(1, pairs)]
 
-    share = 2 * width // pairs
-    packed = shaped((width + hidden // width * share, width), BF16)
-    held, *payloads = pl.pallas_call(
+    held, grad_t, grad_pre, aggregate = pl.pallas_call(
         functools.partial(middle_kernel, pairs),
-        out_shape=[shaped((local, hidden), BF16)] + [packed] * pairs,
+        out_shape=[
+            shaped((local, hidden), BF16),
+            shaped((width, local), BF16),
+            shaped((local, hidden), BF16),
+            shaped((local, width), BF16),
+        ],
         in_specs=[VMEM] * (pairs + 4),
-        out_specs=[VMEM] * (pairs + 1),
-        scratch_shapes=[pltpu.VMEM((pairs, share, hidden), BF16)],
+        out_specs=[VMEM] * 4,
         compiler_params=params,
         name="dense_layer",
     )(*sums, dst_features, w_self, w_neigh, cotangent)
-    near = [payloads[0]] + [xor_permute(payloads[p], "col", 2 * p) for p in range(1, pairs)]
+    near = [grad_t] + [xor_permute(grad_t, "col", 2 * p) for p in range(1, pairs)]
     far = [xor_permute(x, "col", 1) for x in near]
 
-    weight_part = pl.pallas_call(
-        functools.partial(weight_sum_kernel, pairs),
-        out_shape=shaped((hidden // width * share, width), F32),
-        in_specs=[VMEM] * (2 * pairs),
+    weight, weight_theirs = pl.pallas_call(
+        weight_kernel,
+        out_shape=[shaped((width, hidden), F32)] * 2,
+        in_specs=[VMEM] * 3,
+        out_specs=[VMEM] * 2,
+        compiler_params=params,
+        cost_estimate=busy(4),
+        name="weight_partial",
+    )(dst_features, aggregate, grad_pre)
+    weight = pl.pallas_call(
+        weight_fold_kernel,
+        out_shape=shaped((width, hidden), BF16),
+        in_specs=[VMEM, VMEM, ANY],
         out_specs=VMEM,
         compiler_params=params,
-        name="weight_sum",
-    )(*near, *far)
-    weight_terms = [weight_part] + [xor_permute(weight_part, "row", g) for g in range(1, groups)]
-
+        name="weight_fold",
+    )(weight, xor_permute(weight_theirs, "col", 1), near[-1])
+
+    def weight_total(terms, after, dtype, scale, label):
+        return pl.pallas_call(
+            functools.partial(weight_total_kernel, scale, len(terms)),
+            out_shape=shaped((width, hidden), dtype),
+            in_specs=[VMEM] * len(terms) + [ANY] * len(after),
+            out_specs=VMEM,
+            compiler_params=params,
+            name=label,
+        )(*terms, *after)
+
+    row_terms = [weight] + [xor_permute(weight, "row", g) for g in range(1, groups)]
     source_share = source_blocks // groups
     own, *sends = pl.pallas_call(
         functools.partial(backward_kernel, pairs, groups),
@@ -246,35 +250,30 @@
             pltpu.VMEM((source_blocks, width, block), F32),
         ],
         compiler_params=params,
+        cost_estimate=busy(32),
         name="backward_blocks",
     )(rows, cols, block_counts, values, *near, *far)
+    weight = weight_total(row_terms, [own], BF16, 1.0, "weight_rows")
+    col_terms = [weight] + [xor_permute(weight, "col", 2 * p) for p in range(1, pairs)]
+    scale = 1.0 / math.sqrt(local * groups * col_total)
+    weight = weight_total(col_terms, [], F32, scale, "weight_cols")
+    weight_other = xor_permute(weight, "col", 1)
+
     source_terms = [own] + [xor_permute(x, "row", g) for g, x in enumerate(sends, 1)]
 
-    node_total = local * groups * col_total
-    weight_chunk = pl.pallas_call(
-        functools.partial(weight_total_kernel, 1.0 / math.sqrt(node_total)),
-        out_shape=shaped(weight_part.shape, F32),
-        in_specs=[VMEM] * groups,
-        out_specs=VMEM,
-        compiler_params=params,
-        cost_estimate=pl.CostEstimate(flops=0, bytes_accessed=16 * 1024 * 1024, transcendentals=0),
-        name="weight_total",
-    )(*weight_terms)
-    chunks = [weight_chunk] + [xor_permute(weight_chunk, "col", 2 * p) for p in range(1, pairs)]
     output, grad_self, grad_neigh, grad_source = pl.pallas_call(
-        functools.partial(final_kernel, pairs, groups),
+        functools.partial(final_kernel, groups),
         out_shape=[
             shaped((local, hidden), BF16),
             shaped((width, hidden), F32),
             shaped((width, hidden), F32),
             shaped((source_share * block, width), F32),
         ],
-        in_specs=[VMEM] * (pairs + groups + 1),
+        in_specs=[VMEM] * (3 + groups),
         out_specs=[VMEM] * 4,
-        scratch_shapes=[pltpu.VMEM((pairs, share, hidden), F32)],
         compiler_params=params,
         name="join_outputs",
-    )(*chunks, *source_terms, held)
+    )(weight, weight_other, held, *source_terms)
     return output, grad_self, grad_neigh, grad_source.reshape(1, -1, width)
 
 

time: 47.3 us -> 45.5 us (0.962)
  waiting for transfers between devices: 21.9 us -> 16.6 us
  starting transfers between devices: 19 us -> 22.3 us
    ppermute x20 -> x22, waiting for transfers between devices: 21.9 us -> 16.6 us  [xor_permute(): return lax.ppermute(x, axis, [(i, i ^ distance) for i in range(total)])]
    ppermute x20 -> x22, starting transfers between devices: 19 us -> 22.3 us  [xor_permute(): return lax.ppermute(x, axis, [(i, i ^ distance) for i in range(total)])]
    pallas_call x3 -> x5, Pallas kernels: 0.95 us -> 1.21 us  [the longest x1 0.91 us: per_device(): pl.pallas_call(functools.partial(final_kernel, groups), out_shape=[shaped...]
  transfers between devices with their start and end apart: 20 -> 22, of which waited for: 12 -> 12; matrix products, arithmetic and copies ran while one was open for 0% -> 0% of each run, Pallas kernels for 2% -> 3%
where the time goes in v3:
time: 45.5 us; the launch traced here: 45.3 us
  starting transfers between devices  22.3 us (49%)
  waiting for transfers between devices  16.6 us (36%)
  Pallas kernels  4.94 us (11%)
  between operations  1.43 us (3%)
    ppermute x22, starting transfers between devices, xor_permute(): return lax.ppermute(x, axis, [(i, i ^ distance) for i in range(total)])  22.3 us
    ppermute x22, waiting for transfers between devices, xor_permute(): return lax.ppermute(x, axis, [(i, i ^ distance) for i in range(total)])  16.6 us
    pallas_call x1, Pallas kernels, per_device(): pl.pallas_call(forward_kernel, out_shape=[shaped((pairs, block, width), F...  2.21 us
    pallas_call x1, Pallas kernels, per_device(): pl.pallas_call(functools.partial(backward_kernel, pairs, groups), out_sha...  1.15 us
  transfers between devices with their start and end apart: 22, of which 12 were waited for; matrix products, arithmetic and copies ran while one was open for 0% of the time, Pallas kernels for 3%

profile of v3, /device:TPU:0, one launch (start us, length us, event | category | flops | bytes accessed | tf_op | source)
XLA Modules:
  0.0 45.3 jit_solution(11022928996048250698)
XLA Ops:
  1.3 2.2 %forward_blocks.1 = (f32[4,128,128]{2,1,0:T(8,128)S(1)}, f32[4,128,128]{2,1,0:T(8,128)S(1)}, s32[1,1,32]{2,1,0:T(1,128)S(1)}, s32[1,1,32]{2,1,0:T(1,128)S(1)}, bf16[1,1,32,128,128]{4,3,2,1,0:T(8,128)(2,1)S(1)}) custom-call(s32[1,1,32]{2,1,0:T(1,128)} %rows_in.1, s32[1,1,32]{2,1,0:T(1,128)} %cols_in.1, s32[1,1]{1,0:T(1,128)S(6)} %copy.13.counts.refs_2_, ...), custom_call_target="tpu_custom_call" | custom-call | tf_op jit(solution)/shard_map/forward_blocks/pallas_call | solution.py:173
  3.5 0.5 %collective-permute-start = (f32[4,128,128]{2,1,0:T(8,128)S(1)}, f32[4,128,128]{2,1,0:T(8,128)S(1)}, u32[]{:S(2)}, u32[]{:S(2)}) collective-permute-start(f32[4,128,128]{2,1,0:T(8,128)S(1)} %get-tuple-element.24), channel_id=1, source_target_pairs={{0,1},{1,0},{2,3},{3,2},{4,5},{5,4},{6,7},{7,6},{8,9},{9,8},{10,11... | collective-permute-start | bytes 786440 | tf_op jit(solution)/shard_map/ppermute | solution.py:21
  4.0 1.2 %collective-permute-done = f32[4,128,128]{2,1,0:T(8,128)S(1)} collective-permute-done((f32[4,128,128]{2,1,0:T(8,128)S(1)}, f32[4,128,128]{2,1,0:T(8,128)S(1)}, u32[]{:S(2)}, u32[]{:S(2)}) %collective-permute-start) | collective-permute-done | bytes 262176 | tf_op jit(solution)/shard_map/ppermute | solution.py:21
  5.2 0.0 copy-start
  5.2 0.0 copy-start.1
  5.2 0.0 copy-start.2
  5.3 0.0 copy-start.3
  5.3 5.0 %collective-permute-start.3 = (f32[128,128]{1,0:T(8,128)S(1)}, f32[128,128]{1,0:T(8,128)S(1)}, u32[]{:S(2)}, u32[]{:S(2)}) collective-permute-start(f32[128,128]{1,0:T(8,128)S(1)} %get-tuple-element.42), channel_id=1, source_target_pairs={{0,6},{1,7},{2,4},{3,5},{4,2},{5,3},{6,0},{7,1},{8,14},{9,15},{10,... | collective-permute-start | bytes 196616 | tf_op jit(solution)/shard_map/ppermute | solution.py:21
  10.3 0.0 collective-permute-start.2
  10.3 0.6 %collective-permute-start.1 = (f32[128,128]{1,0:T(8,128)S(1)}, f32[128,128]{1,0:T(8,128)S(1)}, u32[]{:S(2)}, u32[]{:S(2)}) collective-permute-start(f32[128,128]{1,0:T(8,128)S(1)} %get-tuple-element.44), channel_id=1, source_target_pairs={{0,2},{1,3},{2,0},{3,1},{4,6},{5,7},{6,4},{7,5},{8,10},{9,11},{10,... | collective-permute-start | bytes 196616 | tf_op jit(solution)/shard_map/ppermute | solution.py:21
  11.0 2.0 %collective-permute-done.3.refs_3_ = f32[128,128]{1,0:T(8,128)S(1)} collective-permute-done((f32[128,128]{1,0:T(8,128)S(1)}, f32[128,128]{1,0:T(8,128)S(1)}, u32[]{:S(2)}, u32[]{:S(2)}) %collective-permute-start.3) | collective-permute-done | bytes 65568 | tf_op jit(solution)/shard_map/ppermute | solution.py:21
  13.0 3.3 %collective-permute-done.2.refs_2_ = f32[128,128]{1,0:T(8,128)S(1)} collective-permute-done((f32[128,128]{1,0:T(8,128)S(1)}, f32[128,128]{1,0:T(8,128)S(1)}, u32[]{:S(2)}, u32[]{:S(2)}) %collective-permute-start.2) | collective-permute-done | bytes 65568 | tf_op jit(solution)/shard_map/ppermute | solution.py:21
  16.2 0.0 collective-permute-done.1.refs_1_
  16.2 0.4 dense_layer.1
  16.6 0.2 weight_partial.1
  16.8 0.1 collective-permute-start.4
  16.9 1.4 %collective-permute-start.10 = (bf16[128,128]{1,0:T(8,128)(2,1)S(1)}, bf16[128,128]{1,0:T(8,128)(2,1)S(1)}, u32[]{:S(2)}, u32[]{:S(2)}) collective-permute-start(bf16[128,128]{1,0:T(8,128)(2,1)S(1)} %get-tuple-element.29.refs_4_), channel_id=1, source_target_pairs={{0,4},{1,5},{2,6},{3,7},{4,0},{5,1},{6,2},{7,3},{8,12},{9,13},{10,... | collective-permute-start | bytes 98312 | tf_op jit(solution)/shard_map/ppermute | solution.py:21
  18.3 2.2 %collective-permute-start.5 = (bf16[128,128]{1,0:T(8,128)(2,1)S(1)}, bf16[128,128]{1,0:T(8,128)(2,1)S(1)}, u32[]{:S(2)}, u32[]{:S(2)}) collective-permute-start(bf16[128,128]{1,0:T(8,128)(2,1)S(1)} %get-tuple-element.29.refs_4_), channel_id=1, source_target_pairs={{0,6},{1,7},{2,4},{3,5},{4,2},{5,3},{6,0},{7,1},{8,14},{9,15},{10,... | collective-permute-start | bytes 98312 | tf_op jit(solution)/shard_map/ppermute | solution.py:21
  20.4 0.0 collective-permute-start.9
  20.5 2.2 %collective-permute-done.10.refs_6_ = bf16[128,128]{1,0:T(8,128)(2,1)S(1)} collective-permute-done((bf16[128,128]{1,0:T(8,128)(2,1)S(1)}, bf16[128,128]{1,0:T(8,128)(2,1)S(1)}, u32[]{:S(2)}, u32[]{:S(2)}) %collective-permute-start.10) | collective-permute-done | bytes 32800 | tf_op jit(solution)/shard_map/ppermute | solution.py:21
  22.7 1.4 %collective-permute-done.5.after.refs_7_ = bf16[128,128]{1,0:T(8,128)(2,1)S(1)} collective-permute-done((bf16[128,128]{1,0:T(8,128)(2,1)S(1)}, bf16[128,128]{1,0:T(8,128)(2,1)S(1)}, u32[]{:S(2)}, u32[]{:S(2)}) %collective-permute-start.5) | collective-permute-done | bytes 32800 | tf_op jit(solution)/shard_map/ppermute | solution.py:21
  24.1 0.0 collective-permute-done.4.received
  24.1 2.5 %collective-permute-start.8 = (bf16[128,256]{1,0:T(8,128)(2,1)S(1)}, bf16[128,256]{1,0:T(8,128)(2,1)S(1)}, u32[]{:S(2)}, u32[]{:S(2)}) collective-permute-start(bf16[128,256]{1,0:T(8,128)(2,1)S(1)} %weight_fold.1.refs_0_), channel_id=1, source_target_pairs={{0,24},{8,16},{16,8},{24,0},{1,25},{9,17},{17,9},{25,1},{2,26},{10... | collective-permute-start | bytes 196616 | tf_op jit(solution)/shard_map/ppermute | solution.py:21
  26.6 0.5 %collective-permute-start.7 = (bf16[128,256]{1,0:T(8,128)(2,1)S(1)}, bf16[128,256]{1,0:T(8,128)(2,1)S(1)}, u32[]{:S(2)}, u32[]{:S(2)}) collective-permute-start(bf16[128,256]{1,0:T(8,128)(2,1)S(1)} %weight_fold.1.refs_0_), channel_id=1, source_target_pairs={{0,16},{8,24},{16,0},{24,8},{1,17},{9,25},{17,1},{25,9},{2,18},{10... | collective-permute-start | bytes 196616 | tf_op jit(solution)/shard_map/ppermute | solution.py:21
  27.1 0.0 collective-permute-done.11.refs_8_
  27.1 0.5 %collective-permute-start.6 = (bf16[128,256]{1,0:T(8,128)(2,1)S(1)}, bf16[128,256]{1,0:T(8,128)(2,1)S(1)}, u32[]{:S(2)}, u32[]{:S(2)}) collective-permute-start(bf16[128,256]{1,0:T(8,128)(2,1)S(1)} %weight_fold.1.refs_0_), channel_id=1, source_target_pairs={{0,8},{8,0},{16,24},{24,16},{1,9},{9,1},{17,25},{25,17},{2,10},{10... | collective-permute-start | bytes 196616 | tf_op jit(solution)/shard_map/ppermute | solution.py:21
  27.7 0.0 collective-permute-done.9.refs_5_
  27.7 0.0 collective-permute-start.12
  27.7 0.0 collective-permute-done.13.refs_10_
  27.7 0.5 %collective-permute-start.14 = (bf16[128,128]{1,0:T(8,128)(2,1)S(1)}, bf16[128,128]{1,0:T(8,128)(2,1)S(1)}, u32[]{:S(2)}, u32[]{:S(2)}) collective-permute-start(bf16[128,128]{1,0:T(8,128)(2,1)S(1)} %collective-permute-done.5.after.refs_7_), channel_id=1, source_target_pairs={{0,1},{1,0},{2,3},{3,2},{4,5},{5,4},{6,7},{7,6},{8,9},{9,8},{10,11... | collective-permute-start | bytes 98312 | tf_op jit(solution)/shard_map/ppermute | solution.py:21
  28.2 0.7 %collective-permute-done.12.refs_9_ = bf16[128,128]{1,0:T(8,128)(2,1)S(1)} collective-permute-done((bf16[128,128]{1,0:T(8,128)(2,1)S(1)}, bf16[128,128]{1,0:T(8,128)(2,1)S(1)}, u32[]{:S(2)}, u32[]{:S(2)}) %collective-permute-start.12) | collective-permute-done | bytes 32800 | tf_op jit(solution)/shard_map/ppermute | solution.py:21
  28.9 0.2 collective-permute-done.14.refs_11_
  29.1 1.2 %backward_blocks.1 = (f32[4,128,128]{2,1,0:T(8,128)S(1)}, bf16[4,128,128]{2,1,0:T(8,128)(2,1)S(1)}, bf16[4,128,128]{2,1,0:T(8,128)(2,1)S(1)}, bf16[4,128,128]{2,1,0:T(8,128)(2,1)S(1)}) custom-call(s32[1,1,32]{2,1,0:T(1,128)S(1)} %get-tuple-element.30.refs_0_, s32[1,1,32]{2,1,0:T(1,128)S(1)} %get-tuple-element.31.refs_1_, s32[1,1]{1,0:T(1,128)S(6)} %copy.13.counts.refs_2_, ...), custom_call_target="tpu_custom_call" | custom-call | bytes 33554432 | tf_op jit(solution)/shard_map/backward_blocks/pallas_call | solution.py:242
  30.2 0.0 collective-permute-done.8.refs_3_
  30.2 0.7 %collective-permute-done.7.refs_2_ = bf16[128,256]{1,0:T(8,128)(2,1)S(1)} collective-permute-done((bf16[128,256]{1,0:T(8,128)(2,1)S(1)}, bf16[128,256]{1,0:T(8,128)(2,1)S(1)}, u32[]{:S(2)}, u32[]{:S(2)}) %collective-permute-start.7) | collective-permute-done | bytes 65568 | tf_op jit(solution)/shard_map/ppermute | solution.py:21
  30.9 0.5 %collective-permute-done.6.refs_1_ = bf16[128,256]{1,0:T(8,128)(2,1)S(1)} collective-permute-done((bf16[128,256]{1,0:T(8,128)(2,1)S(1)}, bf16[128,256]{1,0:T(8,128)(2,1)S(1)}, u32[]{:S(2)}, u32[]{:S(2)}) %collective-permute-start.6) | collective-permute-done | bytes 65568 | tf_op jit(solution)/shard_map/ppermute | solution.py:21
  31.5 2.3 %collective-permute-start.17 = (bf16[128,256]{1,0:T(8,128)(2,1)S(1)}, bf16[128,256]{1,0:T(8,128)(2,1)S(1)}, u32[]{:S(2)}, u32[]{:S(2)}) collective-permute-start(bf16[128,256]{1,0:T(8,128)(2,1)S(1)} %weight_rows.1.refs_0_), channel_id=1, source_target_pairs={{0,6},{1,7},{2,4},{3,5},{4,2},{5,3},{6,0},{7,1},{8,14},{9,15},{10,... | collective-permute-start | bytes 196616 | tf_op jit(solution)/shard_map/ppermute | solution.py:21
  33.8 0.0 collective-permute-start.16
  33.8 2.1 %collective-permute-start.15 = (bf16[128,256]{1,0:T(8,128)(2,1)S(1)}, bf16[128,256]{1,0:T(8,128)(2,1)S(1)}, u32[]{:S(2)}, u32[]{:S(2)}) collective-permute-start(bf16[128,256]{1,0:T(8,128)(2,1)S(1)} %weight_rows.1.refs_0_), channel_id=1, source_target_pairs={{0,2},{1,3},{2,0},{3,1},{4,6},{5,7},{6,4},{7,5},{8,10},{9,11},{10,... | collective-permute-start | bytes 196616 | tf_op jit(solution)/shard_map/ppermute | solution.py:21
  35.9 0.5 %collective-permute-start.19 = (bf16[4,128,128]{2,1,0:T(8,128)(2,1)S(1)}, bf16[4,128,128]{2,1,0:T(8,128)(2,1)S(1)}, u32[]{:S(2)}, u32[]{:S(2)}) collective-permute-start(bf16[4,128,128]{2,1,0:T(8,128)(2,1)S(1)} %get-tuple-element.35), channel_id=1, source_target_pairs={{0,8},{8,0},{16,24},{24,16},{1,9},{9,1},{17,25},{25,17},{2,10},{10... | collective-permute-start | bytes 393224 | tf_op jit(solution)/shard_map/ppermute | solution.py:21
  36.4 1.5 %collective-permute-start.20 = (bf16[4,128,128]{2,1,0:T(8,128)(2,1)S(1)}, bf16[4,128,128]{2,1,0:T(8,128)(2,1)S(1)}, u32[]{:S(2)}, u32[]{:S(2)}) collective-permute-start(bf16[4,128,128]{2,1,0:T(8,128)(2,1)S(1)} %get-tuple-element.36), channel_id=1, source_target_pairs={{0,16},{8,24},{16,0},{24,8},{1,17},{9,25},{17,1},{25,9},{2,18},{10... | collective-permute-start | bytes 393224 | tf_op jit(solution)/shard_map/ppermute | solution.py:21
  38.0 1.8 %collective-permute-start.21 = (bf16[4,128,128]{2,1,0:T(8,128)(2,1)S(1)}, bf16[4,128,128]{2,1,0:T(8,128)(2,1)S(1)}, u32[]{:S(2)}, u32[]{:S(2)}) collective-permute-start(bf16[4,128,128]{2,1,0:T(8,128)(2,1)S(1)} %get-tuple-element.37), channel_id=1, source_target_pairs={{0,24},{8,16},{16,8},{24,0},{1,25},{9,17},{17,9},{25,1},{2,26},{10... | collective-permute-start | bytes 393224 | tf_op jit(solution)/shard_map/ppermute | solution.py:21
  39.8 0.0 collective-permute-done.15.refs_1_
  39.8 0.1 collective-permute-start.18
  39.9 2.2 %collective-permute-done.19.refs_4_ = bf16[4,128,128]{2,1,0:T(8,128)(2,1)S(1)} collective-permute-done((bf16[4,128,128]{2,1,0:T(8,128)(2,1)S(1)}, bf16[4,128,128]{2,1,0:T(8,128)(2,1)S(1)}, u32[]{:S(2)}, u32[]{:S(2)}) %collective-permute-start.19) | collective-permute-done | bytes 131104 | tf_op jit(solution)/shard_map/ppermute | solution.py:21
  42.1 0.7 %collective-permute-done.20.refs_5_ = bf16[4,128,128]{2,1,0:T(8,128)(2,1)S(1)} collective-permute-done((bf16[4,128,128]{2,1,0:T(8,128)(2,1)S(1)}, bf16[4,128,128]{2,1,0:T(8,128)(2,1)S(1)}, u32[]{:S(2)}, u32[]{:S(2)}) %collective-permute-start.20) | collective-permute-done | bytes 131104 | tf_op jit(solution)/shard_map/ppermute | solution.py:21
  42.8 1.6 %collective-permute-done.21.refs_6_ = bf16[4,128,128]{2,1,0:T(8,128)(2,1)S(1)} collective-permute-done((bf16[4,128,128]{2,1,0:T(8,128)(2,1)S(1)}, bf16[4,128,128]{2,1,0:T(8,128)(2,1)S(1)}, u32[]{:S(2)}, u32[]{:S(2)}) %collective-permute-start.21) | collective-permute-done | bytes 131104 | tf_op jit(solution)/shard_map/ppermute | solution.py:21
  44.4 0.9 %join_outputs.1 = (bf16[128,256]{1,0:T(8,128)(2,1)}, f32[128,256]{1,0:T(8,128)}, f32[128,256]{1,0:T(8,128)}, f32[512,128]{1,0:T(8,128)}) custom-call(f32[128,256]{1,0:T(8,128)S(1)} %weight_cols.1.refs_0_, f32[128,256]{1,0:T(8,128)S(1)} %collective-permute-done.18.refs_1_, bf16[128,256]{1,0:T(8,128)(2,1)S(1)} %get-tuple-element.34.refs_2_, ...), custom_call_target="tpu_custom_call" | custom-call | tf_op jit(solution)/shard_map/join_outputs/pallas_call | solution.py:264
  (14 shorter events, 0.2 us)
Async XLA Ops:
  3.5 1.7 %collective-permute-start = (f32[4,128,128]{2,1,0:T(8,128)S(1)}, f32[4,128,128]{2,1,0:T(8,128)S(1)}, u32[]{:S(2)}, u32[]{:S(2)}) collective-permute-start(f32[4,128,128]{2,1,0:T(8,128)S(1)} %get-tuple-element.24), channel_id=1, source_target_pairs={{0,1},{1,0},{2,3},{3,2},{4,5},{5,4},{6,7},{7,6},{8,9},{9,8},{10,11... | collective-permute-start | bytes 786440 | tf_op jit(solution)/shard_map/ppermute | solution.py:21
  5.2 11.0 %copy-start = (bf16[128,128]{1,0:T(8,128)(2,1)S(1)}, bf16[128,128]{1,0:T(8,128)(2,1)}, u32[]{:S(2)}) copy-start(bf16[128,128]{1,0:T(8,128)(2,1)} %dst.1) | copy-start | bytes 98308
  5.2 11.0 %copy-start.1 = (bf16[128,256]{1,0:T(8,128)(2,1)S(1)}, bf16[128,256]{1,0:T(8,128)(2,1)}, u32[]{:S(2)}) copy-start(bf16[128,256]{1,0:T(8,128)(2,1)} %refs_5_.1) | copy-start | bytes 196612
  5.2 11.0 %copy-start.2 = (bf16[128,256]{1,0:T(8,128)(2,1)S(1)}, bf16[128,256]{1,0:T(8,128)(2,1)}, u32[]{:S(2)}) copy-start(bf16[128,256]{1,0:T(8,128)(2,1)} %refs_6_.1) | copy-start | bytes 196612
  5.3 11.0 %copy-start.3 = (bf16[128,256]{1,0:T(8,128)(2,1)S(1)}, bf16[128,256]{1,0:T(8,128)(2,1)}, u32[]{:S(2)}) copy-start(bf16[128,256]{1,0:T(8,128)(2,1)} %refs_7_.1) | copy-start | bytes 196612
  5.3 7.7 %collective-permute-start.3 = (f32[128,128]{1,0:T(8,128)S(1)}, f32[128,128]{1,0:T(8,128)S(1)}, u32[]{:S(2)}, u32[]{:S(2)}) collective-permute-start(f32[128,128]{1,0:T(8,128)S(1)} %get-tuple-element.42), channel_id=1, source_target_pairs={{0,6},{1,7},{2,4},{3,5},{4,2},{5,3},{6,0},{7,1},{8,14},{9,15},{10,... | collective-permute-start | bytes 196616 | tf_op jit(solution)/shard_map/ppermute | solution.py:21
  10.3 5.9 %collective-permute-start.2 = (f32[128,128]{1,0:T(8,128)S(1)}, f32[128,128]{1,0:T(8,128)S(1)}, u32[]{:S(2)}, u32[]{:S(2)}) collective-permute-start(f32[128,128]{1,0:T(8,128)S(1)} %get-tuple-element.43), channel_id=1, source_target_pairs={{0,4},{1,5},{2,6},{3,7},{4,0},{5,1},{6,2},{7,3},{8,12},{9,13},{10,... | collective-permute-start | bytes 196616 | tf_op jit(solution)/shard_map/ppermute | solution.py:21
  10.3 5.9 %collective-permute-start.1 = (f32[128,128]{1,0:T(8,128)S(1)}, f32[128,128]{1,0:T(8,128)S(1)}, u32[]{:S(2)}, u32[]{:S(2)}) collective-permute-start(f32[128,128]{1,0:T(8,128)S(1)} %get-tuple-element.44), channel_id=1, source_target_pairs={{0,2},{1,3},{2,0},{3,1},{4,6},{5,7},{6,4},{7,5},{8,10},{9,11},{10,... | collective-permute-start | bytes 196616 | tf_op jit(solution)/shard_map/ppermute | solution.py:21
  16.8 7.3 %collective-permute-start.4 = (f32[128,256]{1,0:T(8,128)S(1)}, f32[128,256]{1,0:T(8,128)S(1)}, u32[]{:S(2)}, u32[]{:S(2)}) collective-permute-start(f32[128,256]{1,0:T(8,128)S(1)} %get-tuple-element.28), channel_id=1, source_target_pairs={{0,1},{1,0},{2,3},{3,2},{4,5},{5,4},{6,7},{7,6},{8,9},{9,8},{10,11... | collective-permute-start | bytes 393224 | tf_op jit(solution)/shard_map/ppermute | solution.py:21
  16.9 5.8 %collective-permute-start.10 = (bf16[128,128]{1,0:T(8,128)(2,1)S(1)}, bf16[128,128]{1,0:T(8,128)(2,1)S(1)}, u32[]{:S(2)}, u32[]{:S(2)}) collective-permute-start(bf16[128,128]{1,0:T(8,128)(2,1)S(1)} %get-tuple-element.29.refs_4_), channel_id=1, source_target_pairs={{0,4},{1,5},{2,6},{3,7},{4,0},{5,1},{6,2},{7,3},{8,12},{9,13},{10,... | collective-permute-start | bytes 98312 | tf_op jit(solution)/shard_map/ppermute | solution.py:21
  18.3 5.8 %collective-permute-start.5 = (bf16[128,128]{1,0:T(8,128)(2,1)S(1)}, bf16[128,128]{1,0:T(8,128)(2,1)S(1)}, u32[]{:S(2)}, u32[]{:S(2)}) collective-permute-start(bf16[128,128]{1,0:T(8,128)(2,1)S(1)} %get-tuple-element.29.refs_4_), channel_id=1, source_target_pairs={{0,6},{1,7},{2,4},{3,5},{4,2},{5,3},{6,0},{7,1},{8,14},{9,15},{10,... | collective-permute-start | bytes 98312 | tf_op jit(solution)/shard_map/ppermute | solution.py:21
  20.4 6.7 %collective-permute-start.11 = (bf16[128,128]{1,0:T(8,128)(2,1)S(1)}, bf16[128,128]{1,0:T(8,128)(2,1)S(1)}, u32[]{:S(2)}, u32[]{:S(2)}) collective-permute-start(bf16[128,128]{1,0:T(8,128)(2,1)S(1)} %get-tuple-element.29.refs_4_), channel_id=1, source_target_pairs={{0,1},{1,0},{2,3},{3,2},{4,5},{5,4},{6,7},{7,6},{8,9},{9,8},{10,11... | collective-permute-start | bytes 98312 | tf_op jit(solution)/shard_map/ppermute | solution.py:21
  20.4 7.3 %collective-permute-start.9 = (bf16[128,128]{1,0:T(8,128)(2,1)S(1)}, bf16[128,128]{1,0:T(8,128)(2,1)S(1)}, u32[]{:S(2)}, u32[]{:S(2)}) collective-permute-start(bf16[128,128]{1,0:T(8,128)(2,1)S(1)} %get-tuple-element.29.refs_4_), channel_id=1, source_target_pairs={{0,2},{1,3},{2,0},{3,1},{4,6},{5,7},{6,4},{7,5},{8,10},{9,11},{10,... | collective-permute-start | bytes 98312 | tf_op jit(solution)/shard_map/ppermute | solution.py:21
  22.7 5.0 %collective-permute-start.13 = (bf16[128,128]{1,0:T(8,128)(2,1)S(1)}, bf16[128,128]{1,0:T(8,128)(2,1)S(1)}, u32[]{:S(2)}, u32[]{:S(2)}) collective-permute-start(bf16[128,128]{1,0:T(8,128)(2,1)S(1)} %collective-permute-done.10.refs_6_), channel_id=1, source_target_pairs={{0,1},{1,0},{2,3},{3,2},{4,5},{5,4},{6,7},{7,6},{8,9},{9,8},{10,11... | collective-permute-start | bytes 98312 | tf_op jit(solution)/shard_map/ppermute | solution.py:21
  24.1 6.1 %collective-permute-start.8 = (bf16[128,256]{1,0:T(8,128)(2,1)S(1)}, bf16[128,256]{1,0:T(8,128)(2,1)S(1)}, u32[]{:S(2)}, u32[]{:S(2)}) collective-permute-start(bf16[128,256]{1,0:T(8,128)(2,1)S(1)} %weight_fold.1.refs_0_), channel_id=1, source_target_pairs={{0,24},{8,16},{16,8},{24,0},{1,25},{9,17},{17,9},{25,1},{2,26},{10... | collective-permute-start | bytes 196616 | tf_op jit(solution)/shard_map/ppermute | solution.py:21
  26.6 4.3 %collective-permute-start.7 = (bf16[128,256]{1,0:T(8,128)(2,1)S(1)}, bf16[128,256]{1,0:T(8,128)(2,1)S(1)}, u32[]{:S(2)}, u32[]{:S(2)}) collective-permute-start(bf16[128,256]{1,0:T(8,128)(2,1)S(1)} %weight_fold.1.refs_0_), channel_id=1, source_target_pairs={{0,16},{8,24},{16,0},{24,8},{1,17},{9,25},{17,1},{25,9},{2,18},{10... | collective-permute-start | bytes 196616 | tf_op jit(solution)/shard_map/ppermute | solution.py:21
  27.1 4.3 %collective-permute-start.6 = (bf16[128,256]{1,0:T(8,128)(2,1)S(1)}, bf16[128,256]{1,0:T(8,128)(2,1)S(1)}, u32[]{:S(2)}, u32[]{:S(2)}) collective-permute-start(bf16[128,256]{1,0:T(8,128)(2,1)S(1)} %weight_fold.1.refs_0_), channel_id=1, source_target_pairs={{0,8},{8,0},{16,24},{24,16},{1,9},{9,1},{17,25},{25,17},{2,10},{10... | collective-permute-start | bytes 196616 | tf_op jit(solution)/shard_map/ppermute | solution.py:21
  27.7 1.2 %collective-permute-start.12 = (bf16[128,128]{1,0:T(8,128)(2,1)S(1)}, bf16[128,128]{1,0:T(8,128)(2,1)S(1)}, u32[]{:S(2)}, u32[]{:S(2)}) collective-permute-start(bf16[128,128]{1,0:T(8,128)(2,1)S(1)} %collective-permute-done.9.refs_5_), channel_id=1, source_target_pairs={{0,1},{1,0},{2,3},{3,2},{4,5},{5,4},{6,7},{7,6},{8,9},{9,8},{10,11... | collective-permute-start | bytes 98312 | tf_op jit(solution)/shard_map/ppermute | solution.py:21
  27.7 1.4 %collective-permute-start.14 = (bf16[128,128]{1,0:T(8,128)(2,1)S(1)}, bf16[128,128]{1,0:T(8,128)(2,1)S(1)}, u32[]{:S(2)}, u32[]{:S(2)}) collective-permute-start(bf16[128,128]{1,0:T(8,128)(2,1)S(1)} %collective-permute-done.5.after.refs_7_), channel_id=1, source_target_pairs={{0,1},{1,0},{2,3},{3,2},{4,5},{5,4},{6,7},{7,6},{8,9},{9,8},{10,11... | collective-permute-start | bytes 98312 | tf_op jit(solution)/shard_map/ppermute | solution.py:21
  31.5 6.5 %collective-permute-start.17 = (bf16[128,256]{1,0:T(8,128)(2,1)S(1)}, bf16[128,256]{1,0:T(8,128)(2,1)S(1)}, u32[]{:S(2)}, u32[]{:S(2)}) collective-permute-start(bf16[128,256]{1,0:T(8,128)(2,1)S(1)} %weight_rows.1.refs_0_), channel_id=1, source_target_pairs={{0,6},{1,7},{2,4},{3,5},{4,2},{5,3},{6,0},{7,1},{8,14},{9,15},{10,... | collective-permute-start | bytes 196616 | tf_op jit(solution)/shard_map/ppermute | solution.py:21
  33.8 6.0 %collective-permute-start.16 = (bf16[128,256]{1,0:T(8,128)(2,1)S(1)}, bf16[128,256]{1,0:T(8,128)(2,1)S(1)}, u32[]{:S(2)}, u32[]{:S(2)}) collective-permute-start(bf16[128,256]{1,0:T(8,128)(2,1)S(1)} %weight_rows.1.refs_0_), channel_id=1, source_target_pairs={{0,4},{1,5},{2,6},{3,7},{4,0},{5,1},{6,2},{7,3},{8,12},{9,13},{10,... | collective-permute-start | bytes 196616 | tf_op jit(solution)/shard_map/ppermute | solution.py:21
  33.8 6.0 %collective-permute-start.15 = (bf16[128,256]{1,0:T(8,128)(2,1)S(1)}, bf16[128,256]{1,0:T(8,128)(2,1)S(1)}, u32[]{:S(2)}, u32[]{:S(2)}) collective-permute-start(bf16[128,256]{1,0:T(8,128)(2,1)S(1)} %weight_rows.1.refs_0_), channel_id=1, source_target_pairs={{0,2},{1,3},{2,0},{3,1},{4,6},{5,7},{6,4},{7,5},{8,10},{9,11},{10,... | collective-permute-start | bytes 196616 | tf_op jit(solution)/shard_map/ppermute | solution.py:21
  35.9 6.2 %collective-permute-start.19 = (bf16[4,128,128]{2,1,0:T(8,128)(2,1)S(1)}, bf16[4,128,128]{2,1,0:T(8,128)(2,1)S(1)}, u32[]{:S(2)}, u32[]{:S(2)}) collective-permute-start(bf16[4,128,128]{2,1,0:T(8,128)(2,1)S(1)} %get-tuple-element.35), channel_id=1, source_target_pairs={{0,8},{8,0},{16,24},{24,16},{1,9},{9,1},{17,25},{25,17},{2,10},{10... | collective-permute-start | bytes 393224 | tf_op jit(solution)/shard_map/ppermute | solution.py:21
  36.4 6.4 %collective-permute-start.20 = (bf16[4,128,128]{2,1,0:T(8,128)(2,1)S(1)}, bf16[4,128,128]{2,1,0:T(8,128)(2,1)S(1)}, u32[]{:S(2)}, u32[]{:S(2)}) collective-permute-start(bf16[4,128,128]{2,1,0:T(8,128)(2,1)S(1)} %get-tuple-element.36), channel_id=1, source_target_pairs={{0,16},{8,24},{16,0},{24,8},{1,17},{9,25},{17,1},{25,9},{2,18},{10... | collective-permute-start | bytes 393224 | tf_op jit(solution)/shard_map/ppermute | solution.py:21
  38.0 6.5 %collective-permute-start.21 = (bf16[4,128,128]{2,1,0:T(8,128)(2,1)S(1)}, bf16[4,128,128]{2,1,0:T(8,128)(2,1)S(1)}, u32[]{:S(2)}, u32[]{:S(2)}) collective-permute-start(bf16[4,128,128]{2,1,0:T(8,128)(2,1)S(1)} %get-tuple-element.37), channel_id=1, source_target_pairs={{0,24},{8,16},{16,8},{24,0},{1,25},{9,17},{17,9},{25,1},{2,26},{10... | collective-permute-start | bytes 393224 | tf_op jit(solution)/shard_map/ppermute | solution.py:21
  39.8 4.6 %collective-permute-start.18 = (f32[128,256]{1,0:T(8,128)S(1)}, f32[128,256]{1,0:T(8,128)S(1)}, u32[]{:S(2)}, u32[]{:S(2)}) collective-permute-start(f32[128,256]{1,0:T(8,128)S(1)} %weight_cols.1.refs_0_), channel_id=1, source_target_pairs={{0,1},{1,0},{2,3},{3,2},{4,5},{5,4},{6,7},{7,6},{8,9},{9,8},{10,11... | collective-permute-start | bytes 393224 | tf_op jit(solution)/shard_map/ppermute | solution.py:21

commit v4 on v3

--- a/solution.py
+++ b/solution.py
@@ -21,10 +21,44 @@
     return lax.ppermute(x, axis, [(i, i ^ distance) for i in range(total)])
 
 
+def split_permute(x, axis, even, odd):
+    rows, cols = lax.axis_size("row"), lax.axis_size("col")
+    pairs = []
+    for r in range(rows):
+        for c in range(cols):
+            distance = odd if c % 2 else even
+            peer = (r ^ distance, c) if axis == "row" else (r, c ^ (2 * distance))
+            pairs.append((r * cols + c, peer[0] * cols + peer[1]))
+    return lax.ppermute(x, ("row", "col"), pairs)
+
+
+def gather_peers(whole, half, axis, count):
+    seen = [split_permute(whole, axis, d, d + 1) for d in range(2, count, 2)]
+    seen.append(split_permute(half, axis, 1, 1))
+    return seen, [xor_permute(x, "col", 1) for x in seen]
+
+
+def peer_terms(first_core, whole, seen, passed):
+    def both(ref):
+        return [ref[0], ref[1]]
+
+    near, far = seen[-1][...], passed[-1][...]
+    terms = [both(whole), [jnp.where(first_core, near, far), jnp.where(first_core, far, near)]]
+    for near, far in zip(seen[:-1], passed[:-1]):
+        near, far = both(near), both(far)
+        terms.append([jnp.where(first_core, n, f) for n, f in zip(near, far)])
+        terms.append([jnp.where(first_core, f, n) for n, f in zip(near, far)])
+    return terms
+
+
 def tree_sum(terms):
     while len(terms) > 1:
         terms = [terms[i] + terms[i + 1] for i in range(0, len(terms), 2)]
     return terms[0]
+
+
+def on_first_core():
+    return lax.axis_index("col") % 2 == 0
 
 
 def forward_kernel(
@@ -63,7 +97,7 @@
 
 def middle_kernel(pairs, *refs):
     sums = refs[:pairs]
-    dst, w_self, w_neigh, cot, output, grad_t, grad_pre, aggregate = refs[pairs:]
+    dst, w_self, w_neigh, cot, output, grad_t, grad_wide, grad_pre, aggregate = refs[pairs:]
     agg = tree_sum([ref[...] for ref in sums]).astype(BF16)
     aggregate[...] = agg
     pre = jnp.dot(dst[...], w_self[...], preferred_element_type=F32) + jnp.dot(
@@ -76,42 +110,52 @@
     grad_t[...] = lax.dot_general(
         w_neigh[...], grad, (((1,), (1,)), ((), ())), preferred_element_type=F32
     ).astype(BF16)
-
-
-def weight_kernel(dst, aggregate, grad_pre, mine, theirs):
+    grad_wide[...] = grad_t[...].astype(F32)
+
+
+def pair_kernel(mine, theirs, pair):
+    pair[0] = jnp.where(on_first_core(), mine[...], theirs[...])
+    pair[1] = jnp.where(on_first_core(), theirs[...], mine[...])
+
+
+def weight_kernel(dst, aggregate, grad_pre, partial):
     nodes = (((0,), (0,)), ((), ()))
     grad = grad_pre[...]
-    for_self = lax.dot_general(dst[...], grad, nodes, preferred_element_type=F32)
-    for_neigh = lax.dot_general(aggregate[...], grad, nodes, preferred_element_type=F32)
-    first_core = lax.axis_index("col") % 2 == 0
-    mine[...] = jnp.where(first_core, for_self, for_neigh)
-    theirs[...] = jnp.where(first_core, for_neigh, for_self)
-
-
-def weight_fold_kernel(own, received, after, total):
-    total[...] = (own[...] + received[...]).astype(BF16)
-
-
-def weight_total_kernel(scale, count, *refs):
-    total = tree_sum([r[...].astype(F32) for r in refs[:count]]) * scale
-    refs[-1][...] = total.astype(refs[-1].dtype)
-
-
-def backward_kernel(pairs, groups, *refs):
-    rows, cols, counts, values = refs[:4]
-    near = refs[4 : 4 + pairs]
-    far = refs[4 + pairs : 4 + 2 * pairs]
-    own = refs[4 + 2 * pairs]
-    sends = refs[5 + 2 * pairs : 4 + 2 * pairs + groups]
-    table, acc = refs[4 + 2 * pairs + groups :]
-    width = table.shape[1]
+    partial[0] = lax.dot_general(dst[...], grad, nodes, preferred_element_type=F32)
+    partial[1] = lax.dot_general(aggregate[...], grad, nodes, preferred_element_type=F32)
+
+
+def weight_fold_kernel(mine, theirs, *rest):
+    whole, half = rest[-2:]
+    first = (mine[0] + theirs[0]).astype(BF16)
+    second = (mine[1] + theirs[1]).astype(BF16)
+    whole[0] = first
+    whole[1] = second
+    half[...] = jnp.where(on_first_core(), first, second)
+
+
+def weight_rows_kernel(peers, *refs):
+    whole, seen, passed = refs[0], refs[1 : 1 + peers], refs[1 + peers : 1 + 2 * peers]
+    total, half = refs[-2:]
+    terms = peer_terms(on_first_core(), whole, seen, passed)
+    sums = [tree_sum([t[h].astype(F32) for t in terms]).astype(BF16) for h in range(2)]
+    total[0] = sums[0]
+    total[1] = sums[1]
+    half[...] = jnp.where(on_first_core(), sums[0], sums[1])
+
+
+def backward_kernel(peers, groups, *refs):
+    rows, cols, counts, values, pair = refs[:5]
+    seen, passed = refs[5 : 5 + peers], refs[5 + peers : 5 + 2 * peers]
+    own, *sends = refs[5 + 2 * peers : 5 + 2 * peers + groups]
+    table, acc = refs[5 + 2 * peers + groups :]
     slots = values.shape[2]
     share = own.shape[0]
-    me = lax.axis_index("col")
+    me = lax.axis_index("col") // 2 * 2
     group = lax.axis_index("row")
-    for p in range(pairs):
-        table[2 * p] = near[p][...]
-        table[2 * p + 1] = far[p][...]
+    for p, term in enumerate(peer_terms(on_first_core(), pair, seen, passed)):
+        table[2 * p] = term[0].astype(BF16)
+        table[2 * p + 1] = term[1].astype(BF16)
     acc[...] = jnp.zeros_like(acc)
     live = counts[0, 0]
     for s in range(slots):
@@ -124,15 +168,15 @@
         sends[g - 1][...] = acc[g * share : (g + 1) * share].astype(BF16)
 
 
-def final_kernel(groups, *refs):
-    weight_mine, weight_theirs, held = refs[:3]
-    terms = refs[3 : 3 + groups]
-    output, w_self, w_neigh, out = refs[3 + groups :]
+def final_kernel(scale, peers, groups, *refs):
+    whole, seen, passed = refs[0], refs[1 : 1 + peers], refs[1 + peers : 1 + 2 * peers]
+    held = refs[1 + 2 * peers]
+    terms = refs[2 + 2 * peers : 2 + 2 * peers + groups]
+    output, w_self, w_neigh, out = refs[2 + 2 * peers + groups :]
     output[...] = held[...]
-    first_core = lax.axis_index("col") % 2 == 0
-    mine, theirs = weight_mine[...], weight_theirs[...]
-    w_self[...] = jnp.where(first_core, mine, theirs)
-    w_neigh[...] = jnp.where(first_core, theirs, mine)
+    weights = peer_terms(on_first_core(), whole, seen, passed)
+    w_self[...] = tree_sum([t[0].astype(F32) for t in weights]) * scale
+    w_neigh[...] = tree_sum([t[1].astype(F32) for t in weights]) * scale
     blocks, _, block = terms[0].shape
     for b in range(blocks):
         total = tree_sum([r[b].astype(F32) for r in terms])
@@ -193,57 +237,57 @@
     chip_sum = mine + xor_permute(theirs, "col", 1)
     sums = [chip_sum[0]] + [xor_permute(chip_sum[p], "col", 2 * p) for p in range(1, pairs)]
 
-    held, grad_t, grad_pre, aggregate = pl.pallas_call(
+    held, grad_t, grad_wide, grad_pre, aggregate = pl.pallas_call(
         functools.partial(middle_kernel, pairs),
         out_shape=[
             shaped((local, hidden), BF16),
             shaped((width, local), BF16),
+            shaped((width, local), F32),
             shaped((local, hidden), BF16),
             shaped((local, width), BF16),
         ],
         in_specs=[VMEM] * (pairs + 4),
-        out_specs=[VMEM] * 4,
+        out_specs=[VMEM] * 5,
         compiler_params=params,
         name="dense_layer",
     )(*sums, dst_features, w_self, w_neigh, cotangent)
-    near = [grad_t] + [xor_permute(grad_t, "col", 2 * p) for p in range(1, pairs)]
-    far = [xor_permute(x, "col", 1) for x in near]
-
-    weight, weight_theirs = pl.pallas_call(
+    col_peers, row_peers = pairs // 2, groups // 2
+    pair = pl.pallas_call(
+        pair_kernel,
+        out_shape=shaped((2, width, local), BF16),
+        in_specs=[VMEM] * 2,
+        out_specs=VMEM,
+        compiler_params=params,
+        name="gradient_pair",
+    )(grad_t, xor_permute(grad_t, "col", 1))
+    seen, passed = gather_peers(pair, grad_wide, "col", pairs)
+
+    partial = pl.pallas_call(
         weight_kernel,
-        out_shape=[shaped((width, hidden), F32)] * 2,
+        out_shape=shaped((2, width, hidden), F32),
         in_specs=[VMEM] * 3,
-        out_specs=[VMEM] * 2,
+        out_specs=VMEM,
         compiler_params=params,
         cost_estimate=busy(4),
         name="weight_partial",
     )(dst_features, aggregate, grad_pre)
-    weight = pl.pallas_call(
+    after = [pair]
+    weight, weight_half = pl.pallas_call(
         weight_fold_kernel,
-        out_shape=shaped((width, hidden), BF16),
-        in_specs=[VMEM, VMEM, ANY],
-        out_specs=VMEM,
+        out_shape=[shaped((2, width, hidden), BF16), shaped((width, hidden), BF16)],
+        in_specs=[VMEM] * 2 + [ANY] * len(after),
+        out_specs=[VMEM] * 2,
         compiler_params=params,
         name="weight_fold",
-    )(weight, xor_permute(weight_theirs, "col", 1), near[-1])
-
-    def weight_total(terms, after, dtype, scale, label):
-        return pl.pallas_call(
-            functools.partial(weight_total_kernel, scale, len(terms)),
-            out_shape=shaped((width, hidden), dtype),
-            in_specs=[VMEM] * len(terms) + [ANY] * len(after),
-            out_specs=VMEM,
-            compiler_params=params,
-            name=label,
-        )(*terms, *after)
-
-    row_terms = [weight] + [xor_permute(weight, "row", g) for g in range(1, groups)]
+    )(partial, xor_permute(partial, "col", 1), *after)
+    weight_seen, weight_passed = gather_peers(weight, weight_half, "row", groups)
+
     source_share = source_blocks // groups
     own, *sends = pl.pallas_call(
-        functools.partial(backward_kernel, pairs, groups),
+        functools.partial(backward_kernel, col_peers, groups),
         out_shape=[shaped((source_share, width, block), F32)]
         + [shaped((source_share, width, block), BF16)] * (groups - 1),
-        in_specs=[SMEM, SMEM, SMEM] + [VMEM] * (1 + 2 * pairs),
+        in_specs=[SMEM, SMEM, SMEM] + [VMEM] * (2 + 2 * col_peers),
         out_specs=[VMEM] * groups,
         scratch_shapes=[
             pltpu.VMEM((col_total, width, block), BF16),
@@ -252,28 +296,33 @@
         compiler_params=params,
         cost_estimate=busy(32),
         name="backward_blocks",
-    )(rows, cols, block_counts, values, *near, *far)
-    weight = weight_total(row_terms, [own], BF16, 1.0, "weight_rows")
-    col_terms = [weight] + [xor_permute(weight, "col", 2 * p) for p in range(1, pairs)]
+    )(rows, cols, block_counts, values, pair, *seen, *passed)
+    after = [own]
+    weight, weight_half = pl.pallas_call(
+        functools.partial(weight_rows_kernel, row_peers),
+        out_shape=[shaped((2, width, hidden), BF16), shaped((width, hidden), BF16)],
+        in_specs=[VMEM] * (1 + 2 * row_peers) + [ANY] * len(after),
+        out_specs=[VMEM] * 2,
+        compiler_params=params,
+        name="weight_rows",
+    )(weight, *weight_seen, *weight_passed, *after)
+    weight_seen, weight_passed = gather_peers(weight, weight_half, "col", pairs)
     scale = 1.0 / math.sqrt(local * groups * col_total)
-    weight = weight_total(col_terms, [], F32, scale, "weight_cols")
-    weight_other = xor_permute(weight, "col", 1)
-
     source_terms = [own] + [xor_permute(x, "row", g) for g, x in enumerate(sends, 1)]
 
     output, grad_self, grad_neigh, grad_source = pl.pallas_call(
-        functools.partial(final_kernel, groups),
+        functools.partial(final_kernel, scale, col_peers, groups),
         out_shape=[
             shaped((local, hidden), BF16),
             shaped((width, hidden), F32),
             shaped((width, hidden), F32),
             shaped((source_share * block, width), F32),
         ],
-        in_specs=[VMEM] * (3 + groups),
+        in_specs=[VMEM] * (2 + 2 * col_peers + groups),
         out_specs=[VMEM] * 4,
         compiler_params=params,
         name="join_outputs",
-    )(weight, weight_other, held, *source_terms)
+    )(weight, *weight_seen, *weight_passed, held, *source_terms)
     return output, grad_self, grad_neigh, grad_source.reshape(1, -1, width)
 
 

time: 45.5 us -> 42.6 us (0.936)
  starting transfers between devices: 22.3 us -> 20.3 us
  waiting for transfers between devices: 16.6 us -> 15.6 us
    ppermute x22 -> x15, starting transfers between devices: 22.3 us -> 11.3 us  [xor_permute(): return lax.ppermute(x, axis, [(i, i ^ distance) for i in range(total)])]
    ppermute x0 -> x6, starting transfers between devices: none -> 8.93 us  [split_permute(): return lax.ppermute(x, ('row', 'col'), pairs)]
    ppermute x22 -> x15, waiting for transfers between devices: 16.6 us -> 9.42 us  [xor_permute(): return lax.ppermute(x, axis, [(i, i ^ distance) for i in range(total)])]
    ppermute x0 -> x6, waiting for transfers between devices: none -> 6.16 us  [split_permute(): return lax.ppermute(x, ('row', 'col'), pairs)]
  transfers between devices with their start and end apart: 22 -> 21, of which waited for: 12 -> 11; matrix products, arithmetic and copies ran while one was open for 0% -> 0% of each run, Pallas kernels for 3% -> 3%
where the time goes in v4:
time: 42.6 us; the launch traced here: 42.4 us
  starting transfers between devices  20.3 us (48%)
  waiting for transfers between devices  15.6 us (37%)
  Pallas kernels  5.06 us (12%)
  between operations  1.44 us (3%)
    ppermute x15, starting transfers between devices, xor_permute(): return lax.ppermute(x, axis, [(i, i ^ distance) for i in range(total)])  11.3 us
    ppermute x15, waiting for transfers between devices, xor_permute(): return lax.ppermute(x, axis, [(i, i ^ distance) for i in range(total)])  9.42 us
    ppermute x6, starting transfers between devices, split_permute(): return lax.ppermute(x, ('row', 'col'), pairs)  8.93 us
    ppermute x6, waiting for transfers between devices, split_permute(): return lax.ppermute(x, ('row', 'col'), pairs)  6.16 us
    pallas_call x1, Pallas kernels, per_device(): pl.pallas_call(forward_kernel, out_shape=[shaped((pairs, block, width), F...  2.21 us
    pallas_call x1, Pallas kernels, per_device(): pl.pallas_call(functools.partial(backward_kernel, col_peers, groups), out...  1.18 us
    pallas_call x1, Pallas kernels, per_device(): pl.pallas_call(functools.partial(final_kernel, scale, col_peers, groups),...  0.94 us
  transfers between devices with their start and end apart: 21, of which 11 were waited for; matrix products, arithmetic and copies ran while one was open for 0% of the time, Pallas kernels for 3%

profile of v4, /device:TPU:0, one launch (start us, length us, event | category | flops | bytes accessed | tf_op | source)
XLA Modules:
  0.0 42.4 jit_solution(2119760134627455622)
XLA Ops:
  1.3 2.2 %forward_blocks.1 = (f32[4,128,128]{2,1,0:T(8,128)S(1)}, f32[4,128,128]{2,1,0:T(8,128)S(1)}, s32[1,1,32]{2,1,0:T(1,128)S(1)}, s32[1,1,32]{2,1,0:T(1,128)S(1)}, bf16[1,1,32,128,128]{4,3,2,1,0:T(8,128)(2,1)S(1)}) custom-call(s32[1,1,32]{2,1,0:T(1,128)} %rows_in.1, s32[1,1,32]{2,1,0:T(1,128)} %cols_in.1, s32[1,1]{1,0:T(1,128)S(6)} %copy.13.counts.refs_2_, ...), custom_call_target="tpu_custom_call" | custom-call | tf_op jit(solution)/shard_map/forward_blocks/pallas_call | solution.py:217
  3.5 0.5 %collective-permute-start = (f32[4,128,128]{2,1,0:T(8,128)S(1)}, f32[4,128,128]{2,1,0:T(8,128)S(1)}, u32[]{:S(2)}, u32[]{:S(2)}) collective-permute-start(f32[4,128,128]{2,1,0:T(8,128)S(1)} %get-tuple-element.27), channel_id=1, source_target_pairs={{0,1},{1,0},{2,3},{3,2},{4,5},{5,4},{6,7},{7,6},{8,9},{9,8},{10,11... | collective-permute-start | bytes 786440 | tf_op jit(solution)/shard_map/ppermute | solution.py:21
  4.0 1.2 %collective-permute-done = f32[4,128,128]{2,1,0:T(8,128)S(1)} collective-permute-done((f32[4,128,128]{2,1,0:T(8,128)S(1)}, f32[4,128,128]{2,1,0:T(8,128)S(1)}, u32[]{:S(2)}, u32[]{:S(2)}) %collective-permute-start) | collective-permute-done | bytes 262176 | tf_op jit(solution)/shard_map/ppermute | solution.py:21
  5.2 0.0 copy-start
  5.2 0.0 copy-start.1
  5.2 0.0 copy-start.2
  5.3 0.0 copy-start.3
  5.3 5.0 %collective-permute-start.3 = (f32[128,128]{1,0:T(8,128)S(1)}, f32[128,128]{1,0:T(8,128)S(1)}, u32[]{:S(2)}, u32[]{:S(2)}) collective-permute-start(f32[128,128]{1,0:T(8,128)S(1)} %get-tuple-element.48), channel_id=1, source_target_pairs={{0,6},{1,7},{2,4},{3,5},{4,2},{5,3},{6,0},{7,1},{8,14},{9,15},{10,... | collective-permute-start | bytes 196616 | tf_op jit(solution)/shard_map/ppermute | solution.py:21
  10.3 0.0 collective-permute-start.2
  10.3 0.6 %collective-permute-start.1 = (f32[128,128]{1,0:T(8,128)S(1)}, f32[128,128]{1,0:T(8,128)S(1)}, u32[]{:S(2)}, u32[]{:S(2)}) collective-permute-start(f32[128,128]{1,0:T(8,128)S(1)} %get-tuple-element.50), channel_id=1, source_target_pairs={{0,2},{1,3},{2,0},{3,1},{4,6},{5,7},{6,4},{7,5},{8,10},{9,11},{10,... | collective-permute-start | bytes 196616 | tf_op jit(solution)/shard_map/ppermute | solution.py:21
  11.0 2.0 %collective-permute-done.3.refs_3_ = f32[128,128]{1,0:T(8,128)S(1)} collective-permute-done((f32[128,128]{1,0:T(8,128)S(1)}, f32[128,128]{1,0:T(8,128)S(1)}, u32[]{:S(2)}, u32[]{:S(2)}) %collective-permute-start.3) | collective-permute-done | bytes 65568 | tf_op jit(solution)/shard_map/ppermute | solution.py:21
  13.0 3.3 %collective-permute-done.2.refs_2_ = f32[128,128]{1,0:T(8,128)S(1)} collective-permute-done((f32[128,128]{1,0:T(8,128)S(1)}, f32[128,128]{1,0:T(8,128)S(1)}, u32[]{:S(2)}, u32[]{:S(2)}) %collective-permute-start.2) | collective-permute-done | bytes 65568 | tf_op jit(solution)/shard_map/ppermute | solution.py:21
  16.2 0.0 collective-permute-done.1.refs_1_
  16.2 0.4 dense_layer.1
  16.6 0.2 weight_partial.1.mine
  16.8 0.1 collective-permute-start.4
  16.9 0.5 %collective-permute-start.5 = (bf16[128,128]{1,0:T(8,128)(2,1)S(1)}, bf16[128,128]{1,0:T(8,128)(2,1)S(1)}, u32[]{:S(2)}, u32[]{:S(2)}) collective-permute-start(bf16[128,128]{1,0:T(8,128)(2,1)S(1)} %get-tuple-element.30.mine), channel_id=1, source_target_pairs={{0,1},{1,0},{2,3},{3,2},{4,5},{5,4},{6,7},{7,6},{8,9},{9,8},{10,11... | collective-permute-start | bytes 98312 | tf_op jit(solution)/shard_map/ppermute | solution.py:21
  17.4 1.1 %collective-permute-done.5.theirs = bf16[128,128]{1,0:T(8,128)(2,1)S(1)} collective-permute-done((bf16[128,128]{1,0:T(8,128)(2,1)S(1)}, bf16[128,128]{1,0:T(8,128)(2,1)S(1)}, u32[]{:S(2)}, u32[]{:S(2)}) %collective-permute-start.5) | collective-permute-done | bytes 32800 | tf_op jit(solution)/shard_map/ppermute | solution.py:21
  18.5 0.0 collective-permute-done.4.theirs
  18.6 1.6 %collective-permute-start.6 = (bf16[2,128,256]{2,1,0:T(8,128)(2,1)S(1)}, bf16[2,128,256]{2,1,0:T(8,128)(2,1)S(1)}, u32[]{:S(2)}, u32[]{:S(2)}) collective-permute-start(bf16[2,128,256]{2,1,0:T(8,128)(2,1)S(1)} %get-tuple-element.31.refs_0_), channel_id=1, source_target_pairs={{0,16},{1,25},{2,18},{3,27},{4,20},{5,29},{6,22},{7,31},{8,24},{9,... | collective-permute-start | bytes 393224 | tf_op jit(solution)/shard_map/ppermute | solution.py:32
  20.1 1.1 %collective-permute-start.11 = (f32[128,128]{1,0:T(8,128)S(1)}, f32[128,128]{1,0:T(8,128)S(1)}, u32[]{:S(2)}, u32[]{:S(2)}) collective-permute-start(f32[128,128]{1,0:T(8,128)S(1)} %get-tuple-element.36), channel_id=1, source_target_pairs={{0,2},{1,3},{2,0},{3,1},{4,6},{5,7},{6,4},{7,5},{8,10},{9,11},{10,... | collective-permute-start | bytes 196616 | tf_op jit(solution)/shard_map/ppermute | solution.py:32
  21.2 2.0 %collective-permute-start.10 = (bf16[2,128,128]{2,1,0:T(8,128)(2,1)S(1)}, bf16[2,128,128]{2,1,0:T(8,128)(2,1)S(1)}, u32[]{:S(2)}, u32[]{:S(2)}) collective-permute-start(bf16[2,128,128]{2,1,0:T(8,128)(2,1)S(1)} %gradient_pair.1.rest_0_.refs_4_), channel_id=1, source_target_pairs={{0,4},{1,7},{2,6},{3,5},{4,0},{5,3},{6,2},{7,1},{8,12},{9,15},{10,... | collective-permute-start | bytes 196616 | tf_op jit(solution)/shard_map/ppermute | solution.py:32
  23.2 1.5 %collective-permute-start.7 = (bf16[128,256]{1,0:T(8,128)(2,1)S(1)}, bf16[128,256]{1,0:T(8,128)(2,1)S(1)}, u32[]{:S(2)}, u32[]{:S(2)}) collective-permute-start(bf16[128,256]{1,0:T(8,128)(2,1)S(1)} %get-tuple-element.32), channel_id=1, source_target_pairs={{0,8},{1,9},{2,10},{3,11},{4,12},{5,13},{6,14},{7,15},{8,0},{9,1},... | collective-permute-start | bytes 196616 | tf_op jit(solution)/shard_map/ppermute | solution.py:32
  24.7 0.3 collective-permute-done.6.refs_1_
  25.0 0.0 collective-permute-start.8
  25.0 0.0 collective-permute-done.11.refs_6_
  25.0 0.5 %collective-permute-start.13 = (f32[128,128]{1,0:T(8,128)S(1)}, f32[128,128]{1,0:T(8,128)S(1)}, u32[]{:S(2)}, u32[]{:S(2)}) collective-permute-start(f32[128,128]{1,0:T(8,128)S(1)} %collective-permute-done.11.refs_6_), channel_id=1, source_target_pairs={{0,1},{1,0},{2,3},{3,2},{4,5},{5,4},{6,7},{7,6},{8,9},{9,8},{10,11... | collective-permute-start | bytes 196616 | tf_op jit(solution)/shard_map/ppermute | solution.py:21
  25.5 2.3 %collective-permute-done.10.refs_5_ = bf16[2,128,128]{2,1,0:T(8,128)(2,1)S(1)} collective-permute-done((bf16[2,128,128]{2,1,0:T(8,128)(2,1)S(1)}, bf16[2,128,128]{2,1,0:T(8,128)(2,1)S(1)}, u32[]{:S(2)}, u32[]{:S(2)}) %collective-permute-start.10) | collective-permute-done | bytes 65568 | tf_op jit(solution)/shard_map/ppermute | solution.py:32
  27.8 0.0 collective-permute-start.12
  27.8 0.0 collective-permute-done.7.refs_2_
  27.8 0.5 %collective-permute-start.9 = (bf16[128,256]{1,0:T(8,128)(2,1)S(1)}, bf16[128,256]{1,0:T(8,128)(2,1)S(1)}, u32[]{:S(2)}, u32[]{:S(2)}) collective-permute-start(bf16[128,256]{1,0:T(8,128)(2,1)S(1)} %collective-permute-done.7.refs_2_), channel_id=1, source_target_pairs={{0,1},{1,0},{2,3},{3,2},{4,5},{5,4},{6,7},{7,6},{8,9},{9,8},{10,11... | collective-permute-start | bytes 196616 | tf_op jit(solution)/shard_map/ppermute | solution.py:21
  28.3 0.0 collective-permute-done.13.refs_8_
  28.3 0.7 %collective-permute-done.12.refs_7_ = bf16[2,128,128]{2,1,0:T(8,128)(2,1)S(1)} collective-permute-done((bf16[2,128,128]{2,1,0:T(8,128)(2,1)S(1)}, bf16[2,128,128]{2,1,0:T(8,128)(2,1)S(1)}, u32[]{:S(2)}, u32[]{:S(2)}) %collective-permute-start.12) | collective-permute-done | bytes 65568 | tf_op jit(solution)/shard_map/ppermute | solution.py:21
  29.1 1.2 %backward_blocks.1 = (f32[4,128,128]{2,1,0:T(8,128)S(1)}, bf16[4,128,128]{2,1,0:T(8,128)(2,1)S(1)}, bf16[4,128,128]{2,1,0:T(8,128)(2,1)S(1)}, bf16[4,128,128]{2,1,0:T(8,128)(2,1)S(1)}) custom-call(s32[1,1,32]{2,1,0:T(1,128)S(1)} %get-tuple-element.33.refs_0_, s32[1,1,32]{2,1,0:T(1,128)S(1)} %get-tuple-element.34.refs_1_, s32[1,1]{1,0:T(1,128)S(6)} %copy.13.counts.refs_2_, ...), custom_call_target="tpu_custom_call" | custom-call | bytes 33554432 | tf_op jit(solution)/shard_map/backward_blocks/pallas_call | solution.py:286
  30.2 0.0 collective-permute-done.9.refs_4_
  30.3 0.1 weight_rows.1
  30.4 0.7 %collective-permute-start.14 = (bf16[2,128,256]{2,1,0:T(8,128)(2,1)S(1)}, bf16[2,128,256]{2,1,0:T(8,128)(2,1)S(1)}, u32[]{:S(2)}, u32[]{:S(2)}) collective-permute-start(bf16[2,128,256]{2,1,0:T(8,128)(2,1)S(1)} %get-tuple-element.38.refs_0_), channel_id=1, source_target_pairs={{0,4},{1,7},{2,6},{3,5},{4,0},{5,3},{6,2},{7,1},{8,12},{9,15},{10,... | collective-permute-start | bytes 393224 | tf_op jit(solution)/shard_map/ppermute | solution.py:32
  31.1 1.4 %collective-permute-start.18 = (bf16[4,128,128]{2,1,0:T(8,128)(2,1)S(1)}, bf16[4,128,128]{2,1,0:T(8,128)(2,1)S(1)}, u32[]{:S(2)}, u32[]{:S(2)}) collective-permute-start(bf16[4,128,128]{2,1,0:T(8,128)(2,1)S(1)} %get-tuple-element.41), channel_id=1, source_target_pairs={{0,8},{8,0},{16,24},{24,16},{1,9},{9,1},{17,25},{25,17},{2,10},{10... | collective-permute-start | bytes 393224 | tf_op jit(solution)/shard_map/ppermute | solution.py:21
  32.5 0.5 %collective-permute-start.19 = (bf16[4,128,128]{2,1,0:T(8,128)(2,1)S(1)}, bf16[4,128,128]{2,1,0:T(8,128)(2,1)S(1)}, u32[]{:S(2)}, u32[]{:S(2)}) collective-permute-start(bf16[4,128,128]{2,1,0:T(8,128)(2,1)S(1)} %get-tuple-element.42), channel_id=1, source_target_pairs={{0,16},{8,24},{16,0},{24,8},{1,17},{9,25},{17,1},{25,9},{2,18},{10... | collective-permute-start | bytes 393224 | tf_op jit(solution)/shard_map/ppermute | solution.py:21
  33.0 1.6 %collective-permute-start.20 = (bf16[4,128,128]{2,1,0:T(8,128)(2,1)S(1)}, bf16[4,128,128]{2,1,0:T(8,128)(2,1)S(1)}, u32[]{:S(2)}, u32[]{:S(2)}) collective-permute-start(bf16[4,128,128]{2,1,0:T(8,128)(2,1)S(1)} %get-tuple-element.43), channel_id=1, source_target_pairs={{0,24},{8,16},{16,8},{24,0},{1,25},{9,17},{17,9},{25,1},{2,26},{10... | collective-permute-start | bytes 393224 | tf_op jit(solution)/shard_map/ppermute | solution.py:21
  34.5 2.1 %collective-permute-start.15 = (bf16[128,256]{1,0:T(8,128)(2,1)S(1)}, bf16[128,256]{1,0:T(8,128)(2,1)S(1)}, u32[]{:S(2)}, u32[]{:S(2)}) collective-permute-start(bf16[128,256]{1,0:T(8,128)(2,1)S(1)} %get-tuple-element.39), channel_id=1, source_target_pairs={{0,2},{1,3},{2,0},{3,1},{4,6},{5,7},{6,4},{7,5},{8,10},{9,11},{10,... | collective-permute-start | bytes 196616 | tf_op jit(solution)/shard_map/ppermute | solution.py:32
  36.7 2.3 %collective-permute-done.14.refs_1_ = bf16[2,128,256]{2,1,0:T(8,128)(2,1)S(1)} collective-permute-done((bf16[2,128,256]{2,1,0:T(8,128)(2,1)S(1)}, bf16[2,128,256]{2,1,0:T(8,128)(2,1)S(1)}, u32[]{:S(2)}, u32[]{:S(2)}) %collective-permute-start.14) | collective-permute-done | bytes 131104 | tf_op jit(solution)/shard_map/ppermute | solution.py:32
  38.9 0.0 collective-permute-start.16
  38.9 1.3 %collective-permute-done.15.refs_2_ = bf16[128,256]{1,0:T(8,128)(2,1)S(1)} collective-permute-done((bf16[128,256]{1,0:T(8,128)(2,1)S(1)}, bf16[128,256]{1,0:T(8,128)(2,1)S(1)}, u32[]{:S(2)}, u32[]{:S(2)}) %collective-permute-start.15) | collective-permute-done | bytes 65568 | tf_op jit(solution)/shard_map/ppermute | solution.py:32
  40.2 0.1 collective-permute-start.17
  40.3 0.4 collective-permute-done.19.refs_8_
  40.7 0.8 %collective-permute-done.17.refs_4_ = bf16[128,256]{1,0:T(8,128)(2,1)S(1)} collective-permute-done((bf16[128,256]{1,0:T(8,128)(2,1)S(1)}, bf16[128,256]{1,0:T(8,128)(2,1)S(1)}, u32[]{:S(2)}, u32[]{:S(2)}) %collective-permute-start.17) | collective-permute-done | bytes 65568 | tf_op jit(solution)/shard_map/ppermute | solution.py:21
  41.5 0.9 %join_outputs.1 = (bf16[128,256]{1,0:T(8,128)(2,1)}, f32[128,256]{1,0:T(8,128)}, f32[128,256]{1,0:T(8,128)}, f32[512,128]{1,0:T(8,128)}) custom-call(bf16[2,128,256]{2,1,0:T(8,128)(2,1)S(1)} %get-tuple-element.38.refs_0_, bf16[2,128,256]{2,1,0:T(8,128)(2,1)S(1)} %collective-permute-done.14.refs_1_, bf16[128,256]{1,0:T(8,128)(2,1)S(1)} %collective-permute-done.15.refs_2_, ...), custom_call_target="tpu_custom_call" | custom-call | tf_op jit(solution)/shard_map/join_outputs/pallas_call | solution.py:313
  (12 shorter events, 0.1 us)
Async XLA Ops:
  3.5 1.7 %collective-permute-start = (f32[4,128,128]{2,1,0:T(8,128)S(1)}, f32[4,128,128]{2,1,0:T(8,128)S(1)}, u32[]{:S(2)}, u32[]{:S(2)}) collective-permute-start(f32[4,128,128]{2,1,0:T(8,128)S(1)} %get-tuple-element.27), channel_id=1, source_target_pairs={{0,1},{1,0},{2,3},{3,2},{4,5},{5,4},{6,7},{7,6},{8,9},{9,8},{10,11... | collective-permute-start | bytes 786440 | tf_op jit(solution)/shard_map/ppermute | solution.py:21
  5.2 11.0 %copy-start = (bf16[128,128]{1,0:T(8,128)(2,1)S(1)}, bf16[128,128]{1,0:T(8,128)(2,1)}, u32[]{:S(2)}) copy-start(bf16[128,128]{1,0:T(8,128)(2,1)} %dst.1) | copy-start | bytes 98308
  5.2 11.0 %copy-start.1 = (bf16[128,256]{1,0:T(8,128)(2,1)S(1)}, bf16[128,256]{1,0:T(8,128)(2,1)}, u32[]{:S(2)}) copy-start(bf16[128,256]{1,0:T(8,128)(2,1)} %refs_5_.1) | copy-start | bytes 196612
  5.2 11.0 %copy-start.2 = (bf16[128,256]{1,0:T(8,128)(2,1)S(1)}, bf16[128,256]{1,0:T(8,128)(2,1)}, u32[]{:S(2)}) copy-start(bf16[128,256]{1,0:T(8,128)(2,1)} %refs_6_.1) | copy-start | bytes 196612
  5.3 11.0 %copy-start.3 = (bf16[128,256]{1,0:T(8,128)(2,1)S(1)}, bf16[128,256]{1,0:T(8,128)(2,1)}, u32[]{:S(2)}) copy-start(bf16[128,256]{1,0:T(8,128)(2,1)} %refs_7_.1) | copy-start | bytes 196612
  5.3 7.7 %collective-permute-start.3 = (f32[128,128]{1,0:T(8,128)S(1)}, f32[128,128]{1,0:T(8,128)S(1)}, u32[]{:S(2)}, u32[]{:S(2)}) collective-permute-start(f32[128,128]{1,0:T(8,128)S(1)} %get-tuple-element.48), channel_id=1, source_target_pairs={{0,6},{1,7},{2,4},{3,5},{4,2},{5,3},{6,0},{7,1},{8,14},{9,15},{10,... | collective-permute-start | bytes 196616 | tf_op jit(solution)/shard_map/ppermute | solution.py:21
  10.3 5.9 %collective-permute-start.2 = (f32[128,128]{1,0:T(8,128)S(1)}, f32[128,128]{1,0:T(8,128)S(1)}, u32[]{:S(2)}, u32[]{:S(2)}) collective-permute-start(f32[128,128]{1,0:T(8,128)S(1)} %get-tuple-element.49), channel_id=1, source_target_pairs={{0,4},{1,5},{2,6},{3,7},{4,0},{5,1},{6,2},{7,3},{8,12},{9,13},{10,... | collective-permute-start | bytes 196616 | tf_op jit(solution)/shard_map/ppermute | solution.py:21
  10.3 5.9 %collective-permute-start.1 = (f32[128,128]{1,0:T(8,128)S(1)}, f32[128,128]{1,0:T(8,128)S(1)}, u32[]{:S(2)}, u32[]{:S(2)}) collective-permute-start(f32[128,128]{1,0:T(8,128)S(1)} %get-tuple-element.50), channel_id=1, source_target_pairs={{0,2},{1,3},{2,0},{3,1},{4,6},{5,7},{6,4},{7,5},{8,10},{9,11},{10,... | collective-permute-start | bytes 196616 | tf_op jit(solution)/shard_map/ppermute | solution.py:21
  16.8 1.7 %collective-permute-start.4 = (f32[2,128,256]{2,1,0:T(8,128)S(1)}, f32[2,128,256]{2,1,0:T(8,128)S(1)}, u32[]{:S(2)}, u32[]{:S(2)}) collective-permute-start(f32[2,128,256]{2,1,0:T(8,128)S(1)} %weight_partial.1.mine), channel_id=1, source_target_pairs={{0,1},{1,0},{2,3},{3,2},{4,5},{5,4},{6,7},{7,6},{8,9},{9,8},{10,11... | collective-permute-start | bytes 786440 | tf_op jit(solution)/shard_map/ppermute | solution.py:21
  16.9 1.6 %collective-permute-start.5 = (bf16[128,128]{1,0:T(8,128)(2,1)S(1)}, bf16[128,128]{1,0:T(8,128)(2,1)S(1)}, u32[]{:S(2)}, u32[]{:S(2)}) collective-permute-start(bf16[128,128]{1,0:T(8,128)(2,1)S(1)} %get-tuple-element.30.mine), channel_id=1, source_target_pairs={{0,1},{1,0},{2,3},{3,2},{4,5},{5,4},{6,7},{7,6},{8,9},{9,8},{10,11... | collective-permute-start | bytes 98312 | tf_op jit(solution)/shard_map/ppermute | solution.py:21
  18.6 6.4 %collective-permute-start.6 = (bf16[2,128,256]{2,1,0:T(8,128)(2,1)S(1)}, bf16[2,128,256]{2,1,0:T(8,128)(2,1)S(1)}, u32[]{:S(2)}, u32[]{:S(2)}) collective-permute-start(bf16[2,128,256]{2,1,0:T(8,128)(2,1)S(1)} %get-tuple-element.31.refs_0_), channel_id=1, source_target_pairs={{0,16},{1,25},{2,18},{3,27},{4,20},{5,29},{6,22},{7,31},{8,24},{9,... | collective-permute-start | bytes 393224 | tf_op jit(solution)/shard_map/ppermute | solution.py:32
  20.1 4.9 %collective-permute-start.11 = (f32[128,128]{1,0:T(8,128)S(1)}, f32[128,128]{1,0:T(8,128)S(1)}, u32[]{:S(2)}, u32[]{:S(2)}) collective-permute-start(f32[128,128]{1,0:T(8,128)S(1)} %get-tuple-element.36), channel_id=1, source_target_pairs={{0,2},{1,3},{2,0},{3,1},{4,6},{5,7},{6,4},{7,5},{8,10},{9,11},{10,... | collective-permute-start | bytes 196616 | tf_op jit(solution)/shard_map/ppermute | solution.py:32
  21.2 6.6 %collective-permute-start.10 = (bf16[2,128,128]{2,1,0:T(8,128)(2,1)S(1)}, bf16[2,128,128]{2,1,0:T(8,128)(2,1)S(1)}, u32[]{:S(2)}, u32[]{:S(2)}) collective-permute-start(bf16[2,128,128]{2,1,0:T(8,128)(2,1)S(1)} %gradient_pair.1.rest_0_.refs_4_), channel_id=1, source_target_pairs={{0,4},{1,7},{2,6},{3,5},{4,0},{5,3},{6,2},{7,1},{8,12},{9,15},{10,... | collective-permute-start | bytes 196616 | tf_op jit(solution)/shard_map/ppermute | solution.py:32
  23.2 4.6 %collective-permute-start.7 = (bf16[128,256]{1,0:T(8,128)(2,1)S(1)}, bf16[128,256]{1,0:T(8,128)(2,1)S(1)}, u32[]{:S(2)}, u32[]{:S(2)}) collective-permute-start(bf16[128,256]{1,0:T(8,128)(2,1)S(1)} %get-tuple-element.32), channel_id=1, source_target_pairs={{0,8},{1,9},{2,10},{3,11},{4,12},{5,13},{6,14},{7,15},{8,0},{9,1},... | collective-permute-start | bytes 196616 | tf_op jit(solution)/shard_map/ppermute | solution.py:32
  25.0 5.3 %collective-permute-start.8 = (bf16[2,128,256]{2,1,0:T(8,128)(2,1)S(1)}, bf16[2,128,256]{2,1,0:T(8,128)(2,1)S(1)}, u32[]{:S(2)}, u32[]{:S(2)}) collective-permute-start(bf16[2,128,256]{2,1,0:T(8,128)(2,1)S(1)} %collective-permute-done.6.refs_1_), channel_id=1, source_target_pairs={{0,1},{1,0},{2,3},{3,2},{4,5},{5,4},{6,7},{7,6},{8,9},{9,8},{10,11... | collective-permute-start | bytes 393224 | tf_op jit(solution)/shard_map/ppermute | solution.py:21
  25.0 3.3 %collective-permute-start.13 = (f32[128,128]{1,0:T(8,128)S(1)}, f32[128,128]{1,0:T(8,128)S(1)}, u32[]{:S(2)}, u32[]{:S(2)}) collective-permute-start(f32[128,128]{1,0:T(8,128)S(1)} %collective-permute-done.11.refs_6_), channel_id=1, source_target_pairs={{0,1},{1,0},{2,3},{3,2},{4,5},{5,4},{6,7},{7,6},{8,9},{9,8},{10,11... | collective-permute-start | bytes 196616 | tf_op jit(solution)/shard_map/ppermute | solution.py:21
  27.8 1.3 %collective-permute-start.12 = (bf16[2,128,128]{2,1,0:T(8,128)(2,1)S(1)}, bf16[2,128,128]{2,1,0:T(8,128)(2,1)S(1)}, u32[]{:S(2)}, u32[]{:S(2)}) collective-permute-start(bf16[2,128,128]{2,1,0:T(8,128)(2,1)S(1)} %collective-permute-done.10.refs_5_), channel_id=1, source_target_pairs={{0,1},{1,0},{2,3},{3,2},{4,5},{5,4},{6,7},{7,6},{8,9},{9,8},{10,11... | collective-permute-start | bytes 196616 | tf_op jit(solution)/shard_map/ppermute | solution.py:21
  27.8 2.4 %collective-permute-start.9 = (bf16[128,256]{1,0:T(8,128)(2,1)S(1)}, bf16[128,256]{1,0:T(8,128)(2,1)S(1)}, u32[]{:S(2)}, u32[]{:S(2)}) collective-permute-start(bf16[128,256]{1,0:T(8,128)(2,1)S(1)} %collective-permute-done.7.refs_2_), channel_id=1, source_target_pairs={{0,1},{1,0},{2,3},{3,2},{4,5},{5,4},{6,7},{7,6},{8,9},{9,8},{10,11... | collective-permute-start | bytes 196616 | tf_op jit(solution)/shard_map/ppermute | solution.py:21
  30.4 8.6 %collective-permute-start.14 = (bf16[2,128,256]{2,1,0:T(8,128)(2,1)S(1)}, bf16[2,128,256]{2,1,0:T(8,128)(2,1)S(1)}, u32[]{:S(2)}, u32[]{:S(2)}) collective-permute-start(bf16[2,128,256]{2,1,0:T(8,128)(2,1)S(1)} %get-tuple-element.38.refs_0_), channel_id=1, source_target_pairs={{0,4},{1,7},{2,6},{3,5},{4,0},{5,3},{6,2},{7,1},{8,12},{9,15},{10,... | collective-permute-start | bytes 393224 | tf_op jit(solution)/shard_map/ppermute | solution.py:32
  31.1 9.3 %collective-permute-start.18 = (bf16[4,128,128]{2,1,0:T(8,128)(2,1)S(1)}, bf16[4,128,128]{2,1,0:T(8,128)(2,1)S(1)}, u32[]{:S(2)}, u32[]{:S(2)}) collective-permute-start(bf16[4,128,128]{2,1,0:T(8,128)(2,1)S(1)} %get-tuple-element.41), channel_id=1, source_target_pairs={{0,8},{8,0},{16,24},{24,16},{1,9},{9,1},{17,25},{25,17},{2,10},{10... | collective-permute-start | bytes 393224 | tf_op jit(solution)/shard_map/ppermute | solution.py:21
  32.5 8.2 %collective-permute-start.19 = (bf16[4,128,128]{2,1,0:T(8,128)(2,1)S(1)}, bf16[4,128,128]{2,1,0:T(8,128)(2,1)S(1)}, u32[]{:S(2)}, u32[]{:S(2)}) collective-permute-start(bf16[4,128,128]{2,1,0:T(8,128)(2,1)S(1)} %get-tuple-element.42), channel_id=1, source_target_pairs={{0,16},{8,24},{16,0},{24,8},{1,17},{9,25},{17,1},{25,9},{2,18},{10... | collective-permute-start | bytes 393224 | tf_op jit(solution)/shard_map/ppermute | solution.py:21
  33.0 7.7 %collective-permute-start.20 = (bf16[4,128,128]{2,1,0:T(8,128)(2,1)S(1)}, bf16[4,128,128]{2,1,0:T(8,128)(2,1)S(1)}, u32[]{:S(2)}, u32[]{:S(2)}) collective-permute-start(bf16[4,128,128]{2,1,0:T(8,128)(2,1)S(1)} %get-tuple-element.43), channel_id=1, source_target_pairs={{0,24},{8,16},{16,8},{24,0},{1,25},{9,17},{17,9},{25,1},{2,26},{10... | collective-permute-start | bytes 393224 | tf_op jit(solution)/shard_map/ppermute | solution.py:21
  34.5 5.7 %collective-permute-start.15 = (bf16[128,256]{1,0:T(8,128)(2,1)S(1)}, bf16[128,256]{1,0:T(8,128)(2,1)S(1)}, u32[]{:S(2)}, u32[]{:S(2)}) collective-permute-start(bf16[128,256]{1,0:T(8,128)(2,1)S(1)} %get-tuple-element.39), channel_id=1, source_target_pairs={{0,2},{1,3},{2,0},{3,1},{4,6},{5,7},{6,4},{7,5},{8,10},{9,11},{10,... | collective-permute-start | bytes 196616 | tf_op jit(solution)/shard_map/ppermute | solution.py:32
  38.9 2.6 %collective-permute-start.16 = (bf16[2,128,256]{2,1,0:T(8,128)(2,1)S(1)}, bf16[2,128,256]{2,1,0:T(8,128)(2,1)S(1)}, u32[]{:S(2)}, u32[]{:S(2)}) collective-permute-start(bf16[2,128,256]{2,1,0:T(8,128)(2,1)S(1)} %collective-permute-done.14.refs_1_), channel_id=1, source_target_pairs={{0,1},{1,0},{2,3},{3,2},{4,5},{5,4},{6,7},{7,6},{8,9},{9,8},{10,11... | collective-permute-start | bytes 393224 | tf_op jit(solution)/shard_map/ppermute | solution.py:21
  40.2 1.3 %collective-permute-start.17 = (bf16[128,256]{1,0:T(8,128)(2,1)S(1)}, bf16[128,256]{1,0:T(8,128)(2,1)S(1)}, u32[]{:S(2)}, u32[]{:S(2)}) collective-permute-start(bf16[128,256]{1,0:T(8,128)(2,1)S(1)} %collective-permute-done.15.refs_2_), channel_id=1, source_target_pairs={{0,1},{1,0},{2,3},{3,2},{4,5},{5,4},{6,7},{7,6},{8,9},{9,8},{10,11... | collective-permute-start | bytes 196616 | tf_op jit(solution)/shard_map/ppermute | solution.py:21

commit v5 on v4

--- a/solution.py
+++ b/solution.py
@@ -42,7 +42,7 @@
     def both(ref):
         return [ref[0], ref[1]]
 
-    near, far = seen[-1][...], passed[-1][...]
+    near, far = seen[-1][:, : whole.shape[2]], passed[-1][:, : whole.shape[2]]
     terms = [both(whole), [jnp.where(first_core, near, far), jnp.where(first_core, far, near)]]
     for near, far in zip(seen[:-1], passed[:-1]):
         near, far = both(near), both(far)
@@ -97,32 +97,26 @@
 
 def middle_kernel(pairs, *refs):
     sums = refs[:pairs]
-    dst, w_self, w_neigh, cot, output, grad_t, grad_wide, grad_pre, aggregate = refs[pairs:]
+    dst, w_self, w_neigh, cot, output, grad_t, grad_wide, partial = refs[pairs:]
     agg = tree_sum([ref[...] for ref in sums]).astype(BF16)
-    aggregate[...] = agg
     pre = jnp.dot(dst[...], w_self[...], preferred_element_type=F32) + jnp.dot(
         agg, w_neigh[...], preferred_element_type=F32
     )
     sig = jax.nn.sigmoid(pre)
     output[...] = (pre * sig).astype(BF16)
     grad = (cot[...].astype(F32) * sig * (1.0 + pre * (1.0 - sig))).astype(BF16)
-    grad_pre[...] = grad
     grad_t[...] = lax.dot_general(
         w_neigh[...], grad, (((1,), (1,)), ((), ())), preferred_element_type=F32
     ).astype(BF16)
-    grad_wide[...] = grad_t[...].astype(F32)
+    grad_wide[...] = jnp.concatenate([grad_t[...], jnp.zeros_like(grad_t)], axis=1).astype(F32)
+    nodes = (((0,), (0,)), ((), ()))
+    partial[0] = lax.dot_general(dst[...], grad, nodes, preferred_element_type=F32)
+    partial[1] = lax.dot_general(agg, grad, nodes, preferred_element_type=F32)
 
 
 def pair_kernel(mine, theirs, pair):
     pair[0] = jnp.where(on_first_core(), mine[...], theirs[...])
     pair[1] = jnp.where(on_first_core(), theirs[...], mine[...])
-
-
-def weight_kernel(dst, aggregate, grad_pre, partial):
-    nodes = (((0,), (0,)), ((), ()))
-    grad = grad_pre[...]
-    partial[0] = lax.dot_general(dst[...], grad, nodes, preferred_element_type=F32)
-    partial[1] = lax.dot_general(aggregate[...], grad, nodes, preferred_element_type=F32)
 
 
 def weight_fold_kernel(mine, theirs, *rest):
@@ -237,17 +231,16 @@
     chip_sum = mine + xor_permute(theirs, "col", 1)
     sums = [chip_sum[0]] + [xor_permute(chip_sum[p], "col", 2 * p) for p in range(1, pairs)]
 
-    held, grad_t, grad_wide, grad_pre, aggregate = pl.pallas_call(
+    held, grad_t, grad_wide, partial = pl.pallas_call(
         functools.partial(middle_kernel, pairs),
         out_shape=[
             shaped((local, hidden), BF16),
             shaped((width, local), BF16),
-            shaped((width, local), F32),
-            shaped((local, hidden), BF16),
-            shaped((local, width), BF16),
+            shaped((width, 2 * local), F32),
+            shaped((2, width, hidden), F32),
         ],
         in_specs=[VMEM] * (pairs + 4),
-        out_specs=[VMEM] * 5,
+        out_specs=[VMEM] * 4,
         compiler_params=params,
         name="dense_layer",
     )(*sums, dst_features, w_self, w_neigh, cotangent)
@@ -262,15 +255,6 @@
     )(grad_t, xor_permute(grad_t, "col", 1))
     seen, passed = gather_peers(pair, grad_wide, "col", pairs)
 
-    partial = pl.pallas_call(
-        weight_kernel,
-        out_shape=shaped((2, width, hidden), F32),
-        in_specs=[VMEM] * 3,
-        out_specs=VMEM,
-        compiler_params=params,
-        cost_estimate=busy(4),
-        name="weight_partial",
-    )(dst_features, aggregate, grad_pre)
     after = [pair]
     weight, weight_half = pl.pallas_call(
         weight_fold_kernel,

time: 42.6 us -> 41.6 us (0.977)
  starting transfers between devices: 20.3 us -> 19.4 us
    ppermute x6, waiting for transfers between devices: 6.16 us -> 7.33 us  [split_permute(): return lax.ppermute(x, ('row', 'col'), pairs)]
    ppermute x15, waiting for transfers between devices: 9.42 us -> 8.32 us  [xor_permute(): return lax.ppermute(x, axis, [(i, i ^ distance) for i in range(total)])]
    ppermute x15, starting transfers between devices: 11.3 us -> 10.6 us  [xor_permute(): return lax.ppermute(x, axis, [(i, i ^ distance) for i in range(total)])]
where the time goes in v5:
time: 41.6 us; the launch traced here: 41.5 us
  starting transfers between devices  19.4 us (47%)
  waiting for transfers between devices  15.6 us (38%)
  Pallas kernels  4.91 us (12%)
  between operations  1.43 us (3%)
    ppermute x15, starting transfers between devices, xor_permute(): return lax.ppermute(x, axis, [(i, i ^ distance) for i in range(total)])  10.6 us
    ppermute x6, starting transfers between devices, split_permute(): return lax.ppermute(x, ('row', 'col'), pairs)  8.86 us
    ppermute x15, waiting for transfers between devices, xor_permute(): return lax.ppermute(x, axis, [(i, i ^ distance) for i in range(total)])  8.32 us
    ppermute x6, waiting for transfers between devices, split_permute(): return lax.ppermute(x, ('row', 'col'), pairs)  7.33 us
    pallas_call x1, Pallas kernels, per_device(): pl.pallas_call(forward_kernel, out_shape=[shaped((pairs, block, width), F...  2.21 us
    pallas_call x1, Pallas kernels, per_device(): pl.pallas_call(functools.partial(backward_kernel, col_peers, groups), out...  1.18 us
    pallas_call x1, Pallas kernels, per_device(): pl.pallas_call(functools.partial(final_kernel, scale, col_peers, groups),...  0.94 us
  transfers between devices with their start and end apart: 21, of which 11 were waited for; matrix products, arithmetic and copies ran while one was open for 0% of the time, Pallas kernels for 3%

profile of v5, /device:TPU:0, one launch (start us, length us, event | category | flops | bytes accessed | tf_op | source)
XLA Modules:
  0.0 41.5 jit_solution(2451437011385101648)
XLA Ops:
  1.3 2.2 %forward_blocks.1 = (f32[4,128,128]{2,1,0:T(8,128)S(1)}, f32[4,128,128]{2,1,0:T(8,128)S(1)}, s32[1,1,32]{2,1,0:T(1,128)S(1)}, s32[1,1,32]{2,1,0:T(1,128)S(1)}, bf16[1,1,32,128,128]{4,3,2,1,0:T(8,128)(2,1)S(1)}) custom-call(s32[1,1,32]{2,1,0:T(1,128)} %rows_in.1, s32[1,1,32]{2,1,0:T(1,128)} %cols_in.1, s32[1,1]{1,0:T(1,128)S(6)} %copy.13.counts.refs_2_, ...), custom_call_target="tpu_custom_call" | custom-call | tf_op jit(solution)/shard_map/forward_blocks/pallas_call | solution.py:211
  3.5 0.5 %collective-permute-start = (f32[4,128,128]{2,1,0:T(8,128)S(1)}, f32[4,128,128]{2,1,0:T(8,128)S(1)}, u32[]{:S(2)}, u32[]{:S(2)}) collective-permute-start(f32[4,128,128]{2,1,0:T(8,128)S(1)} %get-tuple-element.26), channel_id=1, source_target_pairs={{0,1},{1,0},{2,3},{3,2},{4,5},{5,4},{6,7},{7,6},{8,9},{9,8},{10,11... | collective-permute-start | bytes 786440 | tf_op jit(solution)/shard_map/ppermute | solution.py:21
  4.0 1.2 %collective-permute-done = f32[4,128,128]{2,1,0:T(8,128)S(1)} collective-permute-done((f32[4,128,128]{2,1,0:T(8,128)S(1)}, f32[4,128,128]{2,1,0:T(8,128)S(1)}, u32[]{:S(2)}, u32[]{:S(2)}) %collective-permute-start) | collective-permute-done | bytes 262176 | tf_op jit(solution)/shard_map/ppermute | solution.py:21
  5.2 0.0 copy-start
  5.2 0.0 copy-start.1
  5.2 0.0 copy-start.2
  5.2 0.0 copy-start.3
  5.3 5.0 %collective-permute-start.3 = (f32[128,128]{1,0:T(8,128)S(1)}, f32[128,128]{1,0:T(8,128)S(1)}, u32[]{:S(2)}, u32[]{:S(2)}) collective-permute-start(f32[128,128]{1,0:T(8,128)S(1)} %get-tuple-element.46), channel_id=1, source_target_pairs={{0,6},{1,7},{2,4},{3,5},{4,2},{5,3},{6,0},{7,1},{8,14},{9,15},{10,... | collective-permute-start | bytes 196616 | tf_op jit(solution)/shard_map/ppermute | solution.py:21
  10.3 0.0 collective-permute-start.2
  10.3 0.6 %collective-permute-start.1 = (f32[128,128]{1,0:T(8,128)S(1)}, f32[128,128]{1,0:T(8,128)S(1)}, u32[]{:S(2)}, u32[]{:S(2)}) collective-permute-start(f32[128,128]{1,0:T(8,128)S(1)} %get-tuple-element.48), channel_id=1, source_target_pairs={{0,2},{1,3},{2,0},{3,1},{4,6},{5,7},{6,4},{7,5},{8,10},{9,11},{10,... | collective-permute-start | bytes 196616 | tf_op jit(solution)/shard_map/ppermute | solution.py:21
  11.0 2.0 %collective-permute-done.3.refs_3_ = f32[128,128]{1,0:T(8,128)S(1)} collective-permute-done((f32[128,128]{1,0:T(8,128)S(1)}, f32[128,128]{1,0:T(8,128)S(1)}, u32[]{:S(2)}, u32[]{:S(2)}) %collective-permute-start.3) | collective-permute-done | bytes 65568 | tf_op jit(solution)/shard_map/ppermute | solution.py:21
  13.0 3.3 %collective-permute-done.2.refs_2_ = f32[128,128]{1,0:T(8,128)S(1)} collective-permute-done((f32[128,128]{1,0:T(8,128)S(1)}, f32[128,128]{1,0:T(8,128)S(1)}, u32[]{:S(2)}, u32[]{:S(2)}) %collective-permute-start.2) | collective-permute-done | bytes 65568 | tf_op jit(solution)/shard_map/ppermute | solution.py:21
  16.2 0.0 collective-permute-done.1.refs_1_
  16.2 0.4 %dense_layer.1 = (bf16[128,256]{1,0:T(8,128)(2,1)S(1)}, bf16[128,128]{1,0:T(8,128)(2,1)S(1)}, f32[128,256]{1,0:T(8,128)S(1)}, f32[2,128,256]{2,1,0:T(8,128)S(1)}) custom-call(f32[128,128]{1,0:T(8,128)S(1)} %get-tuple-element.49.refs_0_, f32[128,128]{1,0:T(8,128)S(1)} %collective-permute-done.1.refs_1_, f32[128,128]{1,0:T(8,128)S(1)} %collective-permute-done.2.refs_2_, ...), custom_call_target="tpu_custom_call" | custom-call | tf_op jit(solution)/shard_map/dense_layer/pallas_call | solution.py:234
  16.7 0.1 collective-permute-start.4
  16.7 0.5 %collective-permute-start.5 = (bf16[128,128]{1,0:T(8,128)(2,1)S(1)}, bf16[128,128]{1,0:T(8,128)(2,1)S(1)}, u32[]{:S(2)}, u32[]{:S(2)}) collective-permute-start(bf16[128,128]{1,0:T(8,128)(2,1)S(1)} %get-tuple-element.28.mine), channel_id=1, source_target_pairs={{0,1},{1,0},{2,3},{3,2},{4,5},{5,4},{6,7},{7,6},{8,9},{9,8},{10,11... | collective-permute-start | bytes 98312 | tf_op jit(solution)/shard_map/ppermute | solution.py:21
  17.2 1.1 %collective-permute-start.11 = (f32[128,256]{1,0:T(8,128)S(1)}, f32[128,256]{1,0:T(8,128)S(1)}, u32[]{:S(2)}, u32[]{:S(2)}) collective-permute-start(f32[128,256]{1,0:T(8,128)S(1)} %get-tuple-element.34), channel_id=1, source_target_pairs={{0,2},{1,3},{2,0},{3,1},{4,6},{5,7},{6,4},{7,5},{8,10},{9,11},{10,... | collective-permute-start | bytes 393224 | tf_op jit(solution)/shard_map/ppermute | solution.py:32
  18.3 0.0 collective-permute-done.5.theirs
  18.4 0.0 collective-permute-done.4.theirs
  18.4 1.6 %collective-permute-start.6 = (bf16[2,128,256]{2,1,0:T(8,128)(2,1)S(1)}, bf16[2,128,256]{2,1,0:T(8,128)(2,1)S(1)}, u32[]{:S(2)}, u32[]{:S(2)}) collective-permute-start(bf16[2,128,256]{2,1,0:T(8,128)(2,1)S(1)} %get-tuple-element.29.refs_0_), channel_id=1, source_target_pairs={{0,16},{1,25},{2,18},{3,27},{4,20},{5,29},{6,22},{7,31},{8,24},{9,... | collective-permute-start | bytes 393224 | tf_op jit(solution)/shard_map/ppermute | solution.py:32
  20.0 2.0 %collective-permute-start.10 = (bf16[2,128,128]{2,1,0:T(8,128)(2,1)S(1)}, bf16[2,128,128]{2,1,0:T(8,128)(2,1)S(1)}, u32[]{:S(2)}, u32[]{:S(2)}) collective-permute-start(bf16[2,128,128]{2,1,0:T(8,128)(2,1)S(1)} %gradient_pair.1.rest_0_.refs_4_), channel_id=1, source_target_pairs={{0,4},{1,7},{2,6},{3,5},{4,0},{5,3},{6,2},{7,1},{8,12},{9,15},{10,... | collective-permute-start | bytes 196616 | tf_op jit(solution)/shard_map/ppermute | solution.py:32
  22.0 0.8 %collective-permute-done.11.refs_6_ = f32[128,256]{1,0:T(8,128)S(1)} collective-permute-done((f32[128,256]{1,0:T(8,128)S(1)}, f32[128,256]{1,0:T(8,128)S(1)}, u32[]{:S(2)}, u32[]{:S(2)}) %collective-permute-start.11) | collective-permute-done | bytes 131104 | tf_op jit(solution)/shard_map/ppermute | solution.py:32
  22.7 0.2 collective-permute-start.13
  23.0 1.3 %collective-permute-start.7 = (bf16[128,256]{1,0:T(8,128)(2,1)S(1)}, bf16[128,256]{1,0:T(8,128)(2,1)S(1)}, u32[]{:S(2)}, u32[]{:S(2)}) collective-permute-start(bf16[128,256]{1,0:T(8,128)(2,1)S(1)} %get-tuple-element.30), channel_id=1, source_target_pairs={{0,8},{1,9},{2,10},{3,11},{4,12},{5,13},{6,14},{7,15},{8,0},{9,1},... | collective-permute-start | bytes 196616 | tf_op jit(solution)/shard_map/ppermute | solution.py:32
  24.2 0.6 %collective-permute-done.6.refs_1_ = bf16[2,128,256]{2,1,0:T(8,128)(2,1)S(1)} collective-permute-done((bf16[2,128,256]{2,1,0:T(8,128)(2,1)S(1)}, bf16[2,128,256]{2,1,0:T(8,128)(2,1)S(1)}, u32[]{:S(2)}, u32[]{:S(2)}) %collective-permute-start.6) | collective-permute-done | bytes 131104 | tf_op jit(solution)/shard_map/ppermute | solution.py:32
  24.8 0.0 collective-permute-start.8
  24.9 1.8 %collective-permute-done.10.refs_5_ = bf16[2,128,128]{2,1,0:T(8,128)(2,1)S(1)} collective-permute-done((bf16[2,128,128]{2,1,0:T(8,128)(2,1)S(1)}, bf16[2,128,128]{2,1,0:T(8,128)(2,1)S(1)}, u32[]{:S(2)}, u32[]{:S(2)}) %collective-permute-start.10) | collective-permute-done | bytes 65568 | tf_op jit(solution)/shard_map/ppermute | solution.py:32
  26.7 0.0 collective-permute-start.12
  26.7 0.5 %collective-permute-done.7.refs_2_ = bf16[128,256]{1,0:T(8,128)(2,1)S(1)} collective-permute-done((bf16[128,256]{1,0:T(8,128)(2,1)S(1)}, bf16[128,256]{1,0:T(8,128)(2,1)S(1)}, u32[]{:S(2)}, u32[]{:S(2)}) %collective-permute-start.7) | collective-permute-done | bytes 65568 | tf_op jit(solution)/shard_map/ppermute | solution.py:32
  27.2 0.0 collective-permute-start.9
  27.2 0.7 %collective-permute-done.12.refs_7_ = bf16[2,128,128]{2,1,0:T(8,128)(2,1)S(1)} collective-permute-done((bf16[2,128,128]{2,1,0:T(8,128)(2,1)S(1)}, bf16[2,128,128]{2,1,0:T(8,128)(2,1)S(1)}, u32[]{:S(2)}, u32[]{:S(2)}) %collective-permute-start.12) | collective-permute-done | bytes 65568 | tf_op jit(solution)/shard_map/ppermute | solution.py:21
  27.9 1.2 %backward_blocks.1 = (f32[4,128,128]{2,1,0:T(8,128)S(1)}, bf16[4,128,128]{2,1,0:T(8,128)(2,1)S(1)}, bf16[4,128,128]{2,1,0:T(8,128)(2,1)S(1)}, bf16[4,128,128]{2,1,0:T(8,128)(2,1)S(1)}) custom-call(s32[1,1,32]{2,1,0:T(1,128)S(1)} %get-tuple-element.31.refs_0_, s32[1,1,32]{2,1,0:T(1,128)S(1)} %get-tuple-element.32.refs_1_, s32[1,1]{1,0:T(1,128)S(6)} %copy.13.counts.refs_2_, ...), custom_call_target="tpu_custom_call" | custom-call | bytes 33554432 | tf_op jit(solution)/shard_map/backward_blocks/pallas_call | solution.py:270
  29.1 0.0 collective-permute-done.9.refs_4_
  29.1 0.0 collective-permute-done.8.refs_3_
  29.2 0.1 weight_rows.1
  29.3 1.0 %collective-permute-start.14 = (bf16[2,128,256]{2,1,0:T(8,128)(2,1)S(1)}, bf16[2,128,256]{2,1,0:T(8,128)(2,1)S(1)}, u32[]{:S(2)}, u32[]{:S(2)}) collective-permute-start(bf16[2,128,256]{2,1,0:T(8,128)(2,1)S(1)} %get-tuple-element.36.refs_0_), channel_id=1, source_target_pairs={{0,4},{1,7},{2,6},{3,5},{4,0},{5,3},{6,2},{7,1},{8,12},{9,15},{10,... | collective-permute-start | bytes 393224 | tf_op jit(solution)/shard_map/ppermute | solution.py:32
  30.2 1.2 %collective-permute-start.18 = (bf16[4,128,128]{2,1,0:T(8,128)(2,1)S(1)}, bf16[4,128,128]{2,1,0:T(8,128)(2,1)S(1)}, u32[]{:S(2)}, u32[]{:S(2)}) collective-permute-start(bf16[4,128,128]{2,1,0:T(8,128)(2,1)S(1)} %get-tuple-element.39), channel_id=1, source_target_pairs={{0,8},{8,0},{16,24},{24,16},{1,9},{9,1},{17,25},{25,17},{2,10},{10... | collective-permute-start | bytes 393224 | tf_op jit(solution)/shard_map/ppermute | solution.py:21
  31.5 1.7 %collective-permute-start.19 = (bf16[4,128,128]{2,1,0:T(8,128)(2,1)S(1)}, bf16[4,128,128]{2,1,0:T(8,128)(2,1)S(1)}, u32[]{:S(2)}, u32[]{:S(2)}) collective-permute-start(bf16[4,128,128]{2,1,0:T(8,128)(2,1)S(1)} %get-tuple-element.40), channel_id=1, source_target_pairs={{0,16},{8,24},{16,0},{24,8},{1,17},{9,25},{17,1},{25,9},{2,18},{10... | collective-permute-start | bytes 393224 | tf_op jit(solution)/shard_map/ppermute | solution.py:21
  33.2 0.6 %collective-permute-start.20 = (bf16[4,128,128]{2,1,0:T(8,128)(2,1)S(1)}, bf16[4,128,128]{2,1,0:T(8,128)(2,1)S(1)}, u32[]{:S(2)}, u32[]{:S(2)}) collective-permute-start(bf16[4,128,128]{2,1,0:T(8,128)(2,1)S(1)} %get-tuple-element.41), channel_id=1, source_target_pairs={{0,24},{8,16},{16,8},{24,0},{1,25},{9,17},{17,9},{25,1},{2,26},{10... | collective-permute-start | bytes 393224 | tf_op jit(solution)/shard_map/ppermute | solution.py:21
  33.7 2.0 %collective-permute-start.15 = (bf16[128,256]{1,0:T(8,128)(2,1)S(1)}, bf16[128,256]{1,0:T(8,128)(2,1)S(1)}, u32[]{:S(2)}, u32[]{:S(2)}) collective-permute-start(bf16[128,256]{1,0:T(8,128)(2,1)S(1)} %get-tuple-element.37), channel_id=1, source_target_pairs={{0,2},{1,3},{2,0},{3,1},{4,6},{5,7},{6,4},{7,5},{8,10},{9,11},{10,... | collective-permute-start | bytes 196616 | tf_op jit(solution)/shard_map/ppermute | solution.py:32
  35.7 2.3 %collective-permute-done.14.refs_1_ = bf16[2,128,256]{2,1,0:T(8,128)(2,1)S(1)} collective-permute-done((bf16[2,128,256]{2,1,0:T(8,128)(2,1)S(1)}, bf16[2,128,256]{2,1,0:T(8,128)(2,1)S(1)}, u32[]{:S(2)}, u32[]{:S(2)}) %collective-permute-start.14) | collective-permute-done | bytes 131104 | tf_op jit(solution)/shard_map/ppermute | solution.py:32
  38.0 0.0 collective-permute-start.16
  38.0 1.3 %collective-permute-done.15.refs_2_ = bf16[128,256]{1,0:T(8,128)(2,1)S(1)} collective-permute-done((bf16[128,256]{1,0:T(8,128)(2,1)S(1)}, bf16[128,256]{1,0:T(8,128)(2,1)S(1)}, u32[]{:S(2)}, u32[]{:S(2)}) %collective-permute-start.15) | collective-permute-done | bytes 65568 | tf_op jit(solution)/shard_map/ppermute | solution.py:32
  39.3 0.1 collective-permute-start.17
  39.3 0.0 collective-permute-done.18.refs_7_
  39.3 1.2 %collective-permute-done.19.refs_8_ = bf16[4,128,128]{2,1,0:T(8,128)(2,1)S(1)} collective-permute-done((bf16[4,128,128]{2,1,0:T(8,128)(2,1)S(1)}, bf16[4,128,128]{2,1,0:T(8,128)(2,1)S(1)}, u32[]{:S(2)}, u32[]{:S(2)}) %collective-permute-start.19) | collective-permute-done | bytes 131104 | tf_op jit(solution)/shard_map/ppermute | solution.py:21
  40.5 0.0 collective-permute-done.17.refs_4_
  40.5 0.9 %join_outputs.1 = (bf16[128,256]{1,0:T(8,128)(2,1)}, f32[128,256]{1,0:T(8,128)}, f32[128,256]{1,0:T(8,128)}, f32[512,128]{1,0:T(8,128)}) custom-call(bf16[2,128,256]{2,1,0:T(8,128)(2,1)S(1)} %get-tuple-element.36.refs_0_, bf16[2,128,256]{2,1,0:T(8,128)(2,1)S(1)} %collective-permute-done.14.refs_1_, bf16[128,256]{1,0:T(8,128)(2,1)S(1)} %collective-permute-done.15.refs_2_, ...), custom_call_target="tpu_custom_call" | custom-call | tf_op jit(solution)/shard_map/join_outputs/pallas_call | solution.py:297
  (11 shorter events, 0.1 us)
Async XLA Ops:
  3.5 1.7 %collective-permute-start = (f32[4,128,128]{2,1,0:T(8,128)S(1)}, f32[4,128,128]{2,1,0:T(8,128)S(1)}, u32[]{:S(2)}, u32[]{:S(2)}) collective-permute-start(f32[4,128,128]{2,1,0:T(8,128)S(1)} %get-tuple-element.26), channel_id=1, source_target_pairs={{0,1},{1,0},{2,3},{3,2},{4,5},{5,4},{6,7},{7,6},{8,9},{9,8},{10,11... | collective-permute-start | bytes 786440 | tf_op jit(solution)/shard_map/ppermute | solution.py:21
  5.2 11.0 %copy-start = (bf16[128,256]{1,0:T(8,128)(2,1)S(1)}, bf16[128,256]{1,0:T(8,128)(2,1)}, u32[]{:S(2)}) copy-start(bf16[128,256]{1,0:T(8,128)(2,1)} %refs_5_.1) | copy-start | bytes 196612
  5.2 11.0 %copy-start.1 = (bf16[128,256]{1,0:T(8,128)(2,1)S(1)}, bf16[128,256]{1,0:T(8,128)(2,1)}, u32[]{:S(2)}) copy-start(bf16[128,256]{1,0:T(8,128)(2,1)} %refs_6_.1) | copy-start | bytes 196612
  5.2 11.0 %copy-start.2 = (bf16[128,256]{1,0:T(8,128)(2,1)S(1)}, bf16[128,256]{1,0:T(8,128)(2,1)}, u32[]{:S(2)}) copy-start(bf16[128,256]{1,0:T(8,128)(2,1)} %refs_7_.1) | copy-start | bytes 196612
  5.2 11.0 %copy-start.3 = (bf16[128,128]{1,0:T(8,128)(2,1)S(1)}, bf16[128,128]{1,0:T(8,128)(2,1)}, u32[]{:S(2)}) copy-start(bf16[128,128]{1,0:T(8,128)(2,1)} %refs_4_.1) | copy-start | bytes 98308
  5.3 7.7 %collective-permute-start.3 = (f32[128,128]{1,0:T(8,128)S(1)}, f32[128,128]{1,0:T(8,128)S(1)}, u32[]{:S(2)}, u32[]{:S(2)}) collective-permute-start(f32[128,128]{1,0:T(8,128)S(1)} %get-tuple-element.46), channel_id=1, source_target_pairs={{0,6},{1,7},{2,4},{3,5},{4,2},{5,3},{6,0},{7,1},{8,14},{9,15},{10,... | collective-permute-start | bytes 196616 | tf_op jit(solution)/shard_map/ppermute | solution.py:21
  10.3 5.9 %collective-permute-start.2 = (f32[128,128]{1,0:T(8,128)S(1)}, f32[128,128]{1,0:T(8,128)S(1)}, u32[]{:S(2)}, u32[]{:S(2)}) collective-permute-start(f32[128,128]{1,0:T(8,128)S(1)} %get-tuple-element.47), channel_id=1, source_target_pairs={{0,4},{1,5},{2,6},{3,7},{4,0},{5,1},{6,2},{7,3},{8,12},{9,13},{10,... | collective-permute-start | bytes 196616 | tf_op jit(solution)/shard_map/ppermute | solution.py:21
  10.3 5.9 %collective-permute-start.1 = (f32[128,128]{1,0:T(8,128)S(1)}, f32[128,128]{1,0:T(8,128)S(1)}, u32[]{:S(2)}, u32[]{:S(2)}) collective-permute-start(f32[128,128]{1,0:T(8,128)S(1)} %get-tuple-element.48), channel_id=1, source_target_pairs={{0,2},{1,3},{2,0},{3,1},{4,6},{5,7},{6,4},{7,5},{8,10},{9,11},{10,... | collective-permute-start | bytes 196616 | tf_op jit(solution)/shard_map/ppermute | solution.py:21
  16.7 1.7 %collective-permute-start.4 = (f32[2,128,256]{2,1,0:T(8,128)S(1)}, f32[2,128,256]{2,1,0:T(8,128)S(1)}, u32[]{:S(2)}, u32[]{:S(2)}) collective-permute-start(f32[2,128,256]{2,1,0:T(8,128)S(1)} %get-tuple-element.27.mine), channel_id=1, source_target_pairs={{0,1},{1,0},{2,3},{3,2},{4,5},{5,4},{6,7},{7,6},{8,9},{9,8},{10,11... | collective-permute-start | bytes 786440 | tf_op jit(solution)/shard_map/ppermute | solution.py:21
  16.7 1.6 %collective-permute-start.5 = (bf16[128,128]{1,0:T(8,128)(2,1)S(1)}, bf16[128,128]{1,0:T(8,128)(2,1)S(1)}, u32[]{:S(2)}, u32[]{:S(2)}) collective-permute-start(bf16[128,128]{1,0:T(8,128)(2,1)S(1)} %get-tuple-element.28.mine), channel_id=1, source_target_pairs={{0,1},{1,0},{2,3},{3,2},{4,5},{5,4},{6,7},{7,6},{8,9},{9,8},{10,11... | collective-permute-start | bytes 98312 | tf_op jit(solution)/shard_map/ppermute | solution.py:21
  17.2 5.5 %collective-permute-start.11 = (f32[128,256]{1,0:T(8,128)S(1)}, f32[128,256]{1,0:T(8,128)S(1)}, u32[]{:S(2)}, u32[]{:S(2)}) collective-permute-start(f32[128,256]{1,0:T(8,128)S(1)} %get-tuple-element.34), channel_id=1, source_target_pairs={{0,2},{1,3},{2,0},{3,1},{4,6},{5,7},{6,4},{7,5},{8,10},{9,11},{10,... | collective-permute-start | bytes 393224 | tf_op jit(solution)/shard_map/ppermute | solution.py:32
  18.4 6.4 %collective-permute-start.6 = (bf16[2,128,256]{2,1,0:T(8,128)(2,1)S(1)}, bf16[2,128,256]{2,1,0:T(8,128)(2,1)S(1)}, u32[]{:S(2)}, u32[]{:S(2)}) collective-permute-start(bf16[2,128,256]{2,1,0:T(8,128)(2,1)S(1)} %get-tuple-element.29.refs_0_), channel_id=1, source_target_pairs={{0,16},{1,25},{2,18},{3,27},{4,20},{5,29},{6,22},{7,31},{8,24},{9,... | collective-permute-start | bytes 393224 | tf_op jit(solution)/shard_map/ppermute | solution.py:32
  20.0 6.7 %collective-permute-start.10 = (bf16[2,128,128]{2,1,0:T(8,128)(2,1)S(1)}, bf16[2,128,128]{2,1,0:T(8,128)(2,1)S(1)}, u32[]{:S(2)}, u32[]{:S(2)}) collective-permute-start(bf16[2,128,128]{2,1,0:T(8,128)(2,1)S(1)} %gradient_pair.1.rest_0_.refs_4_), channel_id=1, source_target_pairs={{0,4},{1,7},{2,6},{3,5},{4,0},{5,3},{6,2},{7,1},{8,12},{9,15},{10,... | collective-permute-start | bytes 196616 | tf_op jit(solution)/shard_map/ppermute | solution.py:32
  22.7 5.2 %collective-permute-start.13 = (f32[128,256]{1,0:T(8,128)S(1)}, f32[128,256]{1,0:T(8,128)S(1)}, u32[]{:S(2)}, u32[]{:S(2)}) collective-permute-start(f32[128,256]{1,0:T(8,128)S(1)} %collective-permute-done.11.refs_6_), channel_id=1, source_target_pairs={{0,1},{1,0},{2,3},{3,2},{4,5},{5,4},{6,7},{7,6},{8,9},{9,8},{10,11... | collective-permute-start | bytes 393224 | tf_op jit(solution)/shard_map/ppermute | solution.py:21
  23.0 4.3 %collective-permute-start.7 = (bf16[128,256]{1,0:T(8,128)(2,1)S(1)}, bf16[128,256]{1,0:T(8,128)(2,1)S(1)}, u32[]{:S(2)}, u32[]{:S(2)}) collective-permute-start(bf16[128,256]{1,0:T(8,128)(2,1)S(1)} %get-tuple-element.30), channel_id=1, source_target_pairs={{0,8},{1,9},{2,10},{3,11},{4,12},{5,13},{6,14},{7,15},{8,0},{9,1},... | collective-permute-start | bytes 196616 | tf_op jit(solution)/shard_map/ppermute | solution.py:32
  24.8 4.3 %collective-permute-start.8 = (bf16[2,128,256]{2,1,0:T(8,128)(2,1)S(1)}, bf16[2,128,256]{2,1,0:T(8,128)(2,1)S(1)}, u32[]{:S(2)}, u32[]{:S(2)}) collective-permute-start(bf16[2,128,256]{2,1,0:T(8,128)(2,1)S(1)} %collective-permute-done.6.refs_1_), channel_id=1, source_target_pairs={{0,1},{1,0},{2,3},{3,2},{4,5},{5,4},{6,7},{7,6},{8,9},{9,8},{10,11... | collective-permute-start | bytes 393224 | tf_op jit(solution)/shard_map/ppermute | solution.py:21
  26.7 1.3 %collective-permute-start.12 = (bf16[2,128,128]{2,1,0:T(8,128)(2,1)S(1)}, bf16[2,128,128]{2,1,0:T(8,128)(2,1)S(1)}, u32[]{:S(2)}, u32[]{:S(2)}) collective-permute-start(bf16[2,128,128]{2,1,0:T(8,128)(2,1)S(1)} %collective-permute-done.10.refs_5_), channel_id=1, source_target_pairs={{0,1},{1,0},{2,3},{3,2},{4,5},{5,4},{6,7},{7,6},{8,9},{9,8},{10,11... | collective-permute-start | bytes 196616 | tf_op jit(solution)/shard_map/ppermute | solution.py:21
  27.2 1.9 %collective-permute-start.9 = (bf16[128,256]{1,0:T(8,128)(2,1)S(1)}, bf16[128,256]{1,0:T(8,128)(2,1)S(1)}, u32[]{:S(2)}, u32[]{:S(2)}) collective-permute-start(bf16[128,256]{1,0:T(8,128)(2,1)S(1)} %collective-permute-done.7.refs_2_), channel_id=1, source_target_pairs={{0,1},{1,0},{2,3},{3,2},{4,5},{5,4},{6,7},{7,6},{8,9},{9,8},{10,11... | collective-permute-start | bytes 196616 | tf_op jit(solution)/shard_map/ppermute | solution.py:21
  29.3 8.7 %collective-permute-start.14 = (bf16[2,128,256]{2,1,0:T(8,128)(2,1)S(1)}, bf16[2,128,256]{2,1,0:T(8,128)(2,1)S(1)}, u32[]{:S(2)}, u32[]{:S(2)}) collective-permute-start(bf16[2,128,256]{2,1,0:T(8,128)(2,1)S(1)} %get-tuple-element.36.refs_0_), channel_id=1, source_target_pairs={{0,4},{1,7},{2,6},{3,5},{4,0},{5,3},{6,2},{7,1},{8,12},{9,15},{10,... | collective-permute-start | bytes 393224 | tf_op jit(solution)/shard_map/ppermute | solution.py:32
  30.2 9.1 %collective-permute-start.18 = (bf16[4,128,128]{2,1,0:T(8,128)(2,1)S(1)}, bf16[4,128,128]{2,1,0:T(8,128)(2,1)S(1)}, u32[]{:S(2)}, u32[]{:S(2)}) collective-permute-start(bf16[4,128,128]{2,1,0:T(8,128)(2,1)S(1)} %get-tuple-element.39), channel_id=1, source_target_pairs={{0,8},{8,0},{16,24},{24,16},{1,9},{9,1},{17,25},{25,17},{2,10},{10... | collective-permute-start | bytes 393224 | tf_op jit(solution)/shard_map/ppermute | solution.py:21
  31.5 9.1 %collective-permute-start.19 = (bf16[4,128,128]{2,1,0:T(8,128)(2,1)S(1)}, bf16[4,128,128]{2,1,0:T(8,128)(2,1)S(1)}, u32[]{:S(2)}, u32[]{:S(2)}) collective-permute-start(bf16[4,128,128]{2,1,0:T(8,128)(2,1)S(1)} %get-tuple-element.40), channel_id=1, source_target_pairs={{0,16},{8,24},{16,0},{24,8},{1,17},{9,25},{17,1},{25,9},{2,18},{10... | collective-permute-start | bytes 393224 | tf_op jit(solution)/shard_map/ppermute | solution.py:21
  33.2 7.3 %collective-permute-start.20 = (bf16[4,128,128]{2,1,0:T(8,128)(2,1)S(1)}, bf16[4,128,128]{2,1,0:T(8,128)(2,1)S(1)}, u32[]{:S(2)}, u32[]{:S(2)}) collective-permute-start(bf16[4,128,128]{2,1,0:T(8,128)(2,1)S(1)} %get-tuple-element.41), channel_id=1, source_target_pairs={{0,24},{8,16},{16,8},{24,0},{1,25},{9,17},{17,9},{25,1},{2,26},{10... | collective-permute-start | bytes 393224 | tf_op jit(solution)/shard_map/ppermute | solution.py:21
  33.7 5.5 %collective-permute-start.15 = (bf16[128,256]{1,0:T(8,128)(2,1)S(1)}, bf16[128,256]{1,0:T(8,128)(2,1)S(1)}, u32[]{:S(2)}, u32[]{:S(2)}) collective-permute-start(bf16[128,256]{1,0:T(8,128)(2,1)S(1)} %get-tuple-element.37), channel_id=1, source_target_pairs={{0,2},{1,3},{2,0},{3,1},{4,6},{5,7},{6,4},{7,5},{8,10},{9,11},{10,... | collective-permute-start | bytes 196616 | tf_op jit(solution)/shard_map/ppermute | solution.py:32
  38.0 2.6 %collective-permute-start.16 = (bf16[2,128,256]{2,1,0:T(8,128)(2,1)S(1)}, bf16[2,128,256]{2,1,0:T(8,128)(2,1)S(1)}, u32[]{:S(2)}, u32[]{:S(2)}) collective-permute-start(bf16[2,128,256]{2,1,0:T(8,128)(2,1)S(1)} %collective-permute-done.14.refs_1_), channel_id=1, source_target_pairs={{0,1},{1,0},{2,3},{3,2},{4,5},{5,4},{6,7},{7,6},{8,9},{9,8},{10,11... | collective-permute-start | bytes 393224 | tf_op jit(solution)/shard_map/ppermute | solution.py:21
  39.3 1.3 %collective-permute-start.17 = (bf16[128,256]{1,0:T(8,128)(2,1)S(1)}, bf16[128,256]{1,0:T(8,128)(2,1)S(1)}, u32[]{:S(2)}, u32[]{:S(2)}) collective-permute-start(bf16[128,256]{1,0:T(8,128)(2,1)S(1)} %collective-permute-done.15.refs_2_), channel_id=1, source_target_pairs={{0,1},{1,0},{2,3},{3,2},{4,5},{5,4},{6,7},{7,6},{8,9},{9,8},{10,11... | collective-permute-start | bytes 196616 | tf_op jit(solution)/shard_map/ppermute | solution.py:21

commit v6 on v5

--- a/solution.py
+++ b/solution.py
@@ -98,7 +98,7 @@
 def middle_kernel(pairs, *refs):
     sums = refs[:pairs]
     dst, w_self, w_neigh, cot, output, grad_t, grad_wide, partial = refs[pairs:]
-    agg = tree_sum([ref[...] for ref in sums]).astype(BF16)
+    agg = tree_sum([ref[...].astype(F32) for ref in sums]).astype(BF16)
     pre = jnp.dot(dst[...], w_self[...], preferred_element_type=F32) + jnp.dot(
         agg, w_neigh[...], preferred_element_type=F32
     )
@@ -229,7 +229,7 @@
         *[pltpu.with_memory_space_constraint(x, pltpu.HBM) for x in inputs[2:]],
     )
     chip_sum = mine + xor_permute(theirs, "col", 1)
-    sums = [chip_sum[0]] + [xor_permute(chip_sum[p], "col", 2 * p) for p in range(1, pairs)]
+    sums = [chip_sum[0]] + [xor_permute(chip_sum[p].astype(BF16), "col", 2 * p) for p in range(1, pairs)]
 
     held, grad_t, grad_wide, partial = pl.pallas_call(
         functools.partial(middle_kernel, pairs),
@@ -281,7 +281,7 @@
         cost_estimate=busy(32),
         name="backward_blocks",
     )(rows, cols, block_counts, values, pair, *seen, *passed)
-    after = [own]
+    after = passed
     weight, weight_half = pl.pallas_call(
         functools.partial(weight_rows_kernel, row_peers),
         out_shape=[shaped((2, width, hidden), BF16), shaped((width, hidden), BF16)],

time: 41.6 us -> 40.7 us (0.978)
  waiting for transfers between devices: 15.6 us -> 15.1 us
    ppermute x6, waiting for transfers between devices: 7.33 us -> 5.73 us  [split_permute(): return lax.ppermute(x, ('row', 'col'), pairs)]
    ppermute x15, waiting for transfers between devices: 8.32 us -> 9.36 us  [xor_permute(): return lax.ppermute(x, axis, [(i, i ^ distance) for i in range(total)])]
    ppermute x6, starting transfers between devices: 8.86 us -> 8.26 us  [split_permute(): return lax.ppermute(x, ('row', 'col'), pairs)]
where the time goes in v6:
time: 40.7 us; the launch traced here: 40.5 us
  starting transfers between devices  19.1 us (47%)
  waiting for transfers between devices  15.1 us (37%)
  Pallas kernels  4.88 us (12%)
  between operations  1.41 us (3%)
    ppermute x15, starting transfers between devices, xor_permute(): return lax.ppermute(x, axis, [(i, i ^ distance) for i in range(total)])  10.8 us
    ppermute x15, waiting for transfers between devices, xor_permute(): return lax.ppermute(x, axis, [(i, i ^ distance) for i in range(total)])  9.36 us
    ppermute x6, starting transfers between devices, split_permute(): return lax.ppermute(x, ('row', 'col'), pairs)  8.26 us
    ppermute x6, waiting for transfers between devices, split_permute(): return lax.ppermute(x, ('row', 'col'), pairs)  5.73 us
    pallas_call x1, Pallas kernels, per_device(): pl.pallas_call(forward_kernel, out_shape=[shaped((pairs, block, width), F...  2.21 us
    pallas_call x1, Pallas kernels, per_device(): pl.pallas_call(functools.partial(backward_kernel, col_peers, groups), out...  1.17 us
    pallas_call x1, Pallas kernels, per_device(): pl.pallas_call(functools.partial(final_kernel, scale, col_peers, groups),...  0.93 us
  transfers between devices with their start and end apart: 21, of which 11 were waited for; matrix products, arithmetic and copies ran while one was open for 0% of the time, Pallas kernels for 3%

profile of v6, /device:TPU:0, one launch (start us, length us, event | category | flops | bytes accessed | tf_op | source)
XLA Modules:
  0.0 40.5 jit_solution(6559711435125386427)
XLA Ops:
  1.3 2.2 %forward_blocks.1 = (f32[4,128,128]{2,1,0:T(8,128)S(1)}, f32[4,128,128]{2,1,0:T(8,128)S(1)}, s32[1,1,32]{2,1,0:T(1,128)S(1)}, s32[1,1,32]{2,1,0:T(1,128)S(1)}, bf16[1,1,32,128,128]{4,3,2,1,0:T(8,128)(2,1)S(1)}) custom-call(s32[1,1,32]{2,1,0:T(1,128)} %rows_in.1, s32[1,1,32]{2,1,0:T(1,128)} %cols_in.1, s32[1,1]{1,0:T(1,128)S(6)} %copy.13.counts.refs_2_, ...), custom_call_target="tpu_custom_call" | custom-call | tf_op jit(solution)/shard_map/forward_blocks/pallas_call | solution.py:211
  3.5 0.5 %collective-permute-start = (f32[4,128,128]{2,1,0:T(8,128)S(1)}, f32[4,128,128]{2,1,0:T(8,128)S(1)}, u32[]{:S(2)}, u32[]{:S(2)}) collective-permute-start(f32[4,128,128]{2,1,0:T(8,128)S(1)} %get-tuple-element.26), channel_id=1, source_target_pairs={{0,1},{1,0},{2,3},{3,2},{4,5},{5,4},{6,7},{7,6},{8,9},{9,8},{10,11... | collective-permute-start | bytes 786440 | tf_op jit(solution)/shard_map/ppermute | solution.py:21
  4.0 1.2 %collective-permute-done = f32[4,128,128]{2,1,0:T(8,128)S(1)} collective-permute-done((f32[4,128,128]{2,1,0:T(8,128)S(1)}, f32[4,128,128]{2,1,0:T(8,128)S(1)}, u32[]{:S(2)}, u32[]{:S(2)}) %collective-permute-start) | collective-permute-done | bytes 262176 | tf_op jit(solution)/shard_map/ppermute | solution.py:21
  5.2 0.0 copy-start.2
  5.2 0.0 copy-start.3
  5.3 5.0 %collective-permute-start.3 = (bf16[128,128]{1,0:T(8,128)(2,1)S(1)}, bf16[128,128]{1,0:T(8,128)(2,1)S(1)}, u32[]{:S(2)}, u32[]{:S(2)}) collective-permute-start(bf16[128,128]{1,0:T(8,128)(2,1)S(1)} %get-tuple-element.48), channel_id=1, source_target_pairs={{0,6},{1,7},{2,4},{3,5},{4,2},{5,3},{6,0},{7,1},{8,14},{9,15},{10,... | collective-permute-start | bytes 98312 | tf_op jit(solution)/shard_map/ppermute | solution.py:21
  10.3 0.0 collective-permute-start.2
  10.3 0.6 %collective-permute-start.1 = (bf16[128,128]{1,0:T(8,128)(2,1)S(1)}, bf16[128,128]{1,0:T(8,128)(2,1)S(1)}, u32[]{:S(2)}, u32[]{:S(2)}) collective-permute-start(bf16[128,128]{1,0:T(8,128)(2,1)S(1)} %get-tuple-element.50), channel_id=1, source_target_pairs={{0,2},{1,3},{2,0},{3,1},{4,6},{5,7},{6,4},{7,5},{8,10},{9,11},{10,... | collective-permute-start | bytes 98312 | tf_op jit(solution)/shard_map/ppermute | solution.py:21
  11.0 1.3 %collective-permute-done.3.refs_3_ = bf16[128,128]{1,0:T(8,128)(2,1)S(1)} collective-permute-done((bf16[128,128]{1,0:T(8,128)(2,1)S(1)}, bf16[128,128]{1,0:T(8,128)(2,1)S(1)}, u32[]{:S(2)}, u32[]{:S(2)}) %collective-permute-start.3) | collective-permute-done | bytes 32800 | tf_op jit(solution)/shard_map/ppermute | solution.py:21
  12.2 2.9 %collective-permute-done.2.refs_2_ = bf16[128,128]{1,0:T(8,128)(2,1)S(1)} collective-permute-done((bf16[128,128]{1,0:T(8,128)(2,1)S(1)}, bf16[128,128]{1,0:T(8,128)(2,1)S(1)}, u32[]{:S(2)}, u32[]{:S(2)}) %collective-permute-start.2) | collective-permute-done | bytes 32800 | tf_op jit(solution)/shard_map/ppermute | solution.py:21
  15.1 0.0 collective-permute-done.1.refs_1_
  15.1 0.4 %dense_layer.1 = (bf16[128,256]{1,0:T(8,128)(2,1)S(1)}, bf16[128,128]{1,0:T(8,128)(2,1)S(1)}, f32[128,256]{1,0:T(8,128)S(1)}, f32[2,128,256]{2,1,0:T(8,128)S(1)}) custom-call(f32[128,128]{1,0:T(8,128)S(1)} %slice_bitcast_fusion.refs_0_, bf16[128,128]{1,0:T(8,128)(2,1)S(1)} %collective-permute-done.1.refs_1_, ...), custom_call_target="tpu_custom_call" | custom-call | tf_op jit(solution)/shard_map/dense_layer/pallas_call | solution.py:234
  15.6 0.1 collective-permute-start.4
  15.6 0.5 %collective-permute-start.5 = (bf16[128,128]{1,0:T(8,128)(2,1)S(1)}, bf16[128,128]{1,0:T(8,128)(2,1)S(1)}, u32[]{:S(2)}, u32[]{:S(2)}) collective-permute-start(bf16[128,128]{1,0:T(8,128)(2,1)S(1)} %get-tuple-element.28.mine), channel_id=1, source_target_pairs={{0,1},{1,0},{2,3},{3,2},{4,5},{5,4},{6,7},{7,6},{8,9},{9,8},{10,11... | collective-permute-start | bytes 98312 | tf_op jit(solution)/shard_map/ppermute | solution.py:21
  16.1 0.0 collective-permute-start.12
  16.2 1.1 %collective-permute-done.5.theirs = bf16[128,128]{1,0:T(8,128)(2,1)S(1)} collective-permute-done((bf16[128,128]{1,0:T(8,128)(2,1)S(1)}, bf16[128,128]{1,0:T(8,128)(2,1)S(1)}, u32[]{:S(2)}, u32[]{:S(2)}) %collective-permute-start.5) | collective-permute-done | bytes 32800 | tf_op jit(solution)/shard_map/ppermute | solution.py:21
  17.2 0.0 collective-permute-done.4.theirs
  17.3 1.6 %collective-permute-start.6 = (bf16[2,128,256]{2,1,0:T(8,128)(2,1)S(1)}, bf16[2,128,256]{2,1,0:T(8,128)(2,1)S(1)}, u32[]{:S(2)}, u32[]{:S(2)}) collective-permute-start(bf16[2,128,256]{2,1,0:T(8,128)(2,1)S(1)} %get-tuple-element.29.refs_0_), channel_id=1, source_target_pairs={{0,16},{1,25},{2,18},{3,27},{4,20},{5,29},{6,22},{7,31},{8,24},{9,... | collective-permute-start | bytes 393224 | tf_op jit(solution)/shard_map/ppermute | solution.py:32
  18.9 2.0 %collective-permute-start.10 = (bf16[2,128,128]{2,1,0:T(8,128)(2,1)S(1)}, bf16[2,128,128]{2,1,0:T(8,128)(2,1)S(1)}, u32[]{:S(2)}, u32[]{:S(2)}) collective-permute-start(bf16[2,128,128]{2,1,0:T(8,128)(2,1)S(1)} %gradient_pair.1.rest_0_.refs_4_), channel_id=1, source_target_pairs={{0,4},{1,7},{2,6},{3,5},{4,0},{5,3},{6,2},{7,1},{8,12},{9,15},{10,... | collective-permute-start | bytes 196616 | tf_op jit(solution)/shard_map/ppermute | solution.py:32
  20.9 1.5 %collective-permute-start.7 = (bf16[128,256]{1,0:T(8,128)(2,1)S(1)}, bf16[128,256]{1,0:T(8,128)(2,1)S(1)}, u32[]{:S(2)}, u32[]{:S(2)}) collective-permute-start(bf16[128,256]{1,0:T(8,128)(2,1)S(1)} %get-tuple-element.30), channel_id=1, source_target_pairs={{0,8},{1,9},{2,10},{3,11},{4,12},{5,13},{6,14},{7,15},{8,0},{9,1},... | collective-permute-start | bytes 196616 | tf_op jit(solution)/shard_map/ppermute | solution.py:32
  22.4 0.0 collective-permute-done.12.refs_6_
  22.4 0.0 collective-permute-start.13
  22.4 1.3 %collective-permute-done.6.refs_1_ = bf16[2,128,256]{2,1,0:T(8,128)(2,1)S(1)} collective-permute-done((bf16[2,128,256]{2,1,0:T(8,128)(2,1)S(1)}, bf16[2,128,256]{2,1,0:T(8,128)(2,1)S(1)}, u32[]{:S(2)}, u32[]{:S(2)}) %collective-permute-start.6) | collective-permute-done | bytes 131104 | tf_op jit(solution)/shard_map/ppermute | solution.py:32
  23.7 0.0 collective-permute-start.8
  23.7 1.7 %collective-permute-done.10.refs_5_ = bf16[2,128,128]{2,1,0:T(8,128)(2,1)S(1)} collective-permute-done((bf16[2,128,128]{2,1,0:T(8,128)(2,1)S(1)}, bf16[2,128,128]{2,1,0:T(8,128)(2,1)S(1)}, u32[]{:S(2)}, u32[]{:S(2)}) %collective-permute-start.10) | collective-permute-done | bytes 65568 | tf_op jit(solution)/shard_map/ppermute | solution.py:32
  25.4 0.0 collective-permute-start.11
  25.4 0.0 collective-permute-done.7.refs_2_
  25.4 0.5 %collective-permute-start.9 = (bf16[128,256]{1,0:T(8,128)(2,1)S(1)}, bf16[128,256]{1,0:T(8,128)(2,1)S(1)}, u32[]{:S(2)}, u32[]{:S(2)}) collective-permute-start(bf16[128,256]{1,0:T(8,128)(2,1)S(1)} %collective-permute-done.7.refs_2_), channel_id=1, source_target_pairs={{0,1},{1,0},{2,3},{3,2},{4,5},{5,4},{6,7},{7,6},{8,9},{9,8},{10,11... | collective-permute-start | bytes 196616 | tf_op jit(solution)/shard_map/ppermute | solution.py:21
  26.0 0.7 %collective-permute-done.11.refs_5_.refs_7_ = bf16[2,128,128]{2,1,0:T(8,128)(2,1)S(1)} collective-permute-done((bf16[2,128,128]{2,1,0:T(8,128)(2,1)S(1)}, bf16[2,128,128]{2,1,0:T(8,128)(2,1)S(1)}, u32[]{:S(2)}, u32[]{:S(2)}) %collective-permute-start.11) | collective-permute-done | bytes 65568 | tf_op jit(solution)/shard_map/ppermute | solution.py:21
  26.7 0.0 collective-permute-done.13.refs_6_.refs_8_
  26.7 0.2 collective-permute-done.9.refs_4_
  26.9 0.0 collective-permute-done.8.refs_3_
  26.9 0.1 weight_rows.1
  27.0 1.3 %collective-permute-start.14 = (bf16[2,128,256]{2,1,0:T(8,128)(2,1)S(1)}, bf16[2,128,256]{2,1,0:T(8,128)(2,1)S(1)}, u32[]{:S(2)}, u32[]{:S(2)}) collective-permute-start(bf16[2,128,256]{2,1,0:T(8,128)(2,1)S(1)} %get-tuple-element.32.refs_0_), channel_id=1, source_target_pairs={{0,4},{1,7},{2,6},{3,5},{4,0},{5,3},{6,2},{7,1},{8,12},{9,15},{10,... | collective-permute-start | bytes 393224 | tf_op jit(solution)/shard_map/ppermute | solution.py:32
  28.3 1.2 %backward_blocks.1 = (f32[4,128,128]{2,1,0:T(8,128)S(1)}, bf16[4,128,128]{2,1,0:T(8,128)(2,1)S(1)}, bf16[4,128,128]{2,1,0:T(8,128)(2,1)S(1)}, bf16[4,128,128]{2,1,0:T(8,128)(2,1)S(1)}) custom-call(s32[1,1,32]{2,1,0:T(1,128)S(1)} %get-tuple-element.35.refs_0_, s32[1,1,32]{2,1,0:T(1,128)S(1)} %get-tuple-element.36.refs_1_, s32[1,1]{1,0:T(1,128)S(6)} %copy.13.counts.refs_2_, ...), custom_call_target="tpu_custom_call" | custom-call | bytes 33554432 | tf_op jit(solution)/shard_map/backward_blocks/pallas_call | solution.py:270
  29.5 0.9 %collective-permute-start.18 = (bf16[4,128,128]{2,1,0:T(8,128)(2,1)S(1)}, bf16[4,128,128]{2,1,0:T(8,128)(2,1)S(1)}, u32[]{:S(2)}, u32[]{:S(2)}) collective-permute-start(bf16[4,128,128]{2,1,0:T(8,128)(2,1)S(1)} %get-tuple-element.39), channel_id=1, source_target_pairs={{0,8},{8,0},{16,24},{24,16},{1,9},{9,1},{17,25},{25,17},{2,10},{10... | collective-permute-start | bytes 393224 | tf_op jit(solution)/shard_map/ppermute | solution.py:21
  30.4 1.5 %collective-permute-start.19 = (bf16[4,128,128]{2,1,0:T(8,128)(2,1)S(1)}, bf16[4,128,128]{2,1,0:T(8,128)(2,1)S(1)}, u32[]{:S(2)}, u32[]{:S(2)}) collective-permute-start(bf16[4,128,128]{2,1,0:T(8,128)(2,1)S(1)} %get-tuple-element.40), channel_id=1, source_target_pairs={{0,16},{8,24},{16,0},{24,8},{1,17},{9,25},{17,1},{25,9},{2,18},{10... | collective-permute-start | bytes 393224 | tf_op jit(solution)/shard_map/ppermute | solution.py:21
  31.9 1.1 %collective-permute-start.20 = (bf16[4,128,128]{2,1,0:T(8,128)(2,1)S(1)}, bf16[4,128,128]{2,1,0:T(8,128)(2,1)S(1)}, u32[]{:S(2)}, u32[]{:S(2)}) collective-permute-start(bf16[4,128,128]{2,1,0:T(8,128)(2,1)S(1)} %get-tuple-element.41), channel_id=1, source_target_pairs={{0,24},{8,16},{16,8},{24,0},{1,25},{9,17},{17,9},{25,1},{2,26},{10... | collective-permute-start | bytes 393224 | tf_op jit(solution)/shard_map/ppermute | solution.py:21
  33.0 1.8 %collective-permute-start.15 = (bf16[128,256]{1,0:T(8,128)(2,1)S(1)}, bf16[128,256]{1,0:T(8,128)(2,1)S(1)}, u32[]{:S(2)}, u32[]{:S(2)}) collective-permute-start(bf16[128,256]{1,0:T(8,128)(2,1)S(1)} %get-tuple-element.33), channel_id=1, source_target_pairs={{0,2},{1,3},{2,0},{3,1},{4,6},{5,7},{6,4},{7,5},{8,10},{9,11},{10,... | collective-permute-start | bytes 196616 | tf_op jit(solution)/shard_map/ppermute | solution.py:32
  34.9 0.8 %collective-permute-done.14.refs_1_ = bf16[2,128,256]{2,1,0:T(8,128)(2,1)S(1)} collective-permute-done((bf16[2,128,256]{2,1,0:T(8,128)(2,1)S(1)}, bf16[2,128,256]{2,1,0:T(8,128)(2,1)S(1)}, u32[]{:S(2)}, u32[]{:S(2)}) %collective-permute-start.14) | collective-permute-done | bytes 131104 | tf_op jit(solution)/shard_map/ppermute | solution.py:32
  35.7 0.0 collective-permute-start.16
  35.7 1.9 %collective-permute-done.15.refs_2_ = bf16[128,256]{1,0:T(8,128)(2,1)S(1)} collective-permute-done((bf16[128,256]{1,0:T(8,128)(2,1)S(1)}, bf16[128,256]{1,0:T(8,128)(2,1)S(1)}, u32[]{:S(2)}, u32[]{:S(2)}) %collective-permute-start.15) | collective-permute-done | bytes 65568 | tf_op jit(solution)/shard_map/ppermute | solution.py:32
  37.5 0.0 collective-permute-start.17
  37.5 0.0 collective-permute-done.18.refs_7_
  37.5 2.1 %collective-permute-done.19.refs_8_ = bf16[4,128,128]{2,1,0:T(8,128)(2,1)S(1)} collective-permute-done((bf16[4,128,128]{2,1,0:T(8,128)(2,1)S(1)}, bf16[4,128,128]{2,1,0:T(8,128)(2,1)S(1)}, u32[]{:S(2)}, u32[]{:S(2)}) %collective-permute-start.19) | collective-permute-done | bytes 131104 | tf_op jit(solution)/shard_map/ppermute | solution.py:21
  39.6 0.0 collective-permute-done.20.refs_9_
  39.6 0.0 collective-permute-done.17.refs_4_
  39.6 0.9 %join_outputs.1 = (bf16[128,256]{1,0:T(8,128)(2,1)}, f32[128,256]{1,0:T(8,128)}, f32[128,256]{1,0:T(8,128)}, f32[512,128]{1,0:T(8,128)}) custom-call(bf16[2,128,256]{2,1,0:T(8,128)(2,1)S(1)} %get-tuple-element.32.refs_0_, bf16[2,128,256]{2,1,0:T(8,128)(2,1)S(1)} %collective-permute-done.14.refs_1_, bf16[128,256]{1,0:T(8,128)(2,1)S(1)} %collective-permute-done.15.refs_2_, ...), custom_call_target="tpu_custom_call" | custom-call | tf_op jit(solution)/shard_map/join_outputs/pallas_call | solution.py:297
  (12 shorter events, 0.1 us)
Async XLA Ops:
  3.5 1.7 %collective-permute-start = (f32[4,128,128]{2,1,0:T(8,128)S(1)}, f32[4,128,128]{2,1,0:T(8,128)S(1)}, u32[]{:S(2)}, u32[]{:S(2)}) collective-permute-start(f32[4,128,128]{2,1,0:T(8,128)S(1)} %get-tuple-element.26), channel_id=1, source_target_pairs={{0,1},{1,0},{2,3},{3,2},{4,5},{5,4},{6,7},{7,6},{8,9},{9,8},{10,11... | collective-permute-start | bytes 786440 | tf_op jit(solution)/shard_map/ppermute | solution.py:21
  5.2 9.9 %copy-start.2 = (bf16[128,256]{1,0:T(8,128)(2,1)S(1)}, bf16[128,256]{1,0:T(8,128)(2,1)}, u32[]{:S(2)}) copy-start(bf16[128,256]{1,0:T(8,128)(2,1)} %refs_7_.1) | copy-start | bytes 196612
  5.2 9.9 %copy-start.3 = (bf16[128,128]{1,0:T(8,128)(2,1)S(1)}, bf16[128,128]{1,0:T(8,128)(2,1)}, u32[]{:S(2)}) copy-start(bf16[128,128]{1,0:T(8,128)(2,1)} %refs_4_.1) | copy-start | bytes 98308
  5.3 7.0 %collective-permute-start.3 = (bf16[128,128]{1,0:T(8,128)(2,1)S(1)}, bf16[128,128]{1,0:T(8,128)(2,1)S(1)}, u32[]{:S(2)}, u32[]{:S(2)}) collective-permute-start(bf16[128,128]{1,0:T(8,128)(2,1)S(1)} %get-tuple-element.48), channel_id=1, source_target_pairs={{0,6},{1,7},{2,4},{3,5},{4,2},{5,3},{6,0},{7,1},{8,14},{9,15},{10,... | collective-permute-start | bytes 98312 | tf_op jit(solution)/shard_map/ppermute | solution.py:21
  10.3 4.8 %collective-permute-start.2 = (bf16[128,128]{1,0:T(8,128)(2,1)S(1)}, bf16[128,128]{1,0:T(8,128)(2,1)S(1)}, u32[]{:S(2)}, u32[]{:S(2)}) collective-permute-start(bf16[128,128]{1,0:T(8,128)(2,1)S(1)} %get-tuple-element.49), channel_id=1, source_target_pairs={{0,4},{1,5},{2,6},{3,7},{4,0},{5,1},{6,2},{7,3},{8,12},{9,13},{10,... | collective-permute-start | bytes 98312 | tf_op jit(solution)/shard_map/ppermute | solution.py:21
  10.3 4.8 %collective-permute-start.1 = (bf16[128,128]{1,0:T(8,128)(2,1)S(1)}, bf16[128,128]{1,0:T(8,128)(2,1)S(1)}, u32[]{:S(2)}, u32[]{:S(2)}) collective-permute-start(bf16[128,128]{1,0:T(8,128)(2,1)S(1)} %get-tuple-element.50), channel_id=1, source_target_pairs={{0,2},{1,3},{2,0},{3,1},{4,6},{5,7},{6,4},{7,5},{8,10},{9,11},{10,... | collective-permute-start | bytes 98312 | tf_op jit(solution)/shard_map/ppermute | solution.py:21
  10.9 4.2 %copy-start = (bf16[128,256]{1,0:T(8,128)(2,1)S(1)}, bf16[128,256]{1,0:T(8,128)(2,1)}, u32[]{:S(2)}) copy-start(bf16[128,256]{1,0:T(8,128)(2,1)} %refs_5_.1) | copy-start | bytes 196612
  10.9 4.2 %copy-start.1 = (bf16[128,256]{1,0:T(8,128)(2,1)S(1)}, bf16[128,256]{1,0:T(8,128)(2,1)}, u32[]{:S(2)}) copy-start(bf16[128,256]{1,0:T(8,128)(2,1)} %refs_6_.1) | copy-start | bytes 196612
  15.6 1.7 %collective-permute-start.4 = (f32[2,128,256]{2,1,0:T(8,128)S(1)}, f32[2,128,256]{2,1,0:T(8,128)S(1)}, u32[]{:S(2)}, u32[]{:S(2)}) collective-permute-start(f32[2,128,256]{2,1,0:T(8,128)S(1)} %get-tuple-element.27.mine), channel_id=1, source_target_pairs={{0,1},{1,0},{2,3},{3,2},{4,5},{5,4},{6,7},{7,6},{8,9},{9,8},{10,11... | collective-permute-start | bytes 786440 | tf_op jit(solution)/shard_map/ppermute | solution.py:21
  15.6 1.6 %collective-permute-start.5 = (bf16[128,128]{1,0:T(8,128)(2,1)S(1)}, bf16[128,128]{1,0:T(8,128)(2,1)S(1)}, u32[]{:S(2)}, u32[]{:S(2)}) collective-permute-start(bf16[128,128]{1,0:T(8,128)(2,1)S(1)} %get-tuple-element.28.mine), channel_id=1, source_target_pairs={{0,1},{1,0},{2,3},{3,2},{4,5},{5,4},{6,7},{7,6},{8,9},{9,8},{10,11... | collective-permute-start | bytes 98312 | tf_op jit(solution)/shard_map/ppermute | solution.py:21
  16.1 6.2 %collective-permute-start.12 = (f32[128,256]{1,0:T(8,128)S(1)}, f32[128,256]{1,0:T(8,128)S(1)}, u32[]{:S(2)}, u32[]{:S(2)}) collective-permute-start(f32[128,256]{1,0:T(8,128)S(1)} %get-tuple-element.31), channel_id=1, source_target_pairs={{0,2},{1,3},{2,0},{3,1},{4,6},{5,7},{6,4},{7,5},{8,10},{9,11},{10,... | collective-permute-start | bytes 393224 | tf_op jit(solution)/shard_map/ppermute | solution.py:32
  17.3 6.4 %collective-permute-start.6 = (bf16[2,128,256]{2,1,0:T(8,128)(2,1)S(1)}, bf16[2,128,256]{2,1,0:T(8,128)(2,1)S(1)}, u32[]{:S(2)}, u32[]{:S(2)}) collective-permute-start(bf16[2,128,256]{2,1,0:T(8,128)(2,1)S(1)} %get-tuple-element.29.refs_0_), channel_id=1, source_target_pairs={{0,16},{1,25},{2,18},{3,27},{4,20},{5,29},{6,22},{7,31},{8,24},{9,... | collective-permute-start | bytes 393224 | tf_op jit(solution)/shard_map/ppermute | solution.py:32
  18.9 6.6 %collective-permute-start.10 = (bf16[2,128,128]{2,1,0:T(8,128)(2,1)S(1)}, bf16[2,128,128]{2,1,0:T(8,128)(2,1)S(1)}, u32[]{:S(2)}, u32[]{:S(2)}) collective-permute-start(bf16[2,128,128]{2,1,0:T(8,128)(2,1)S(1)} %gradient_pair.1.rest_0_.refs_4_), channel_id=1, source_target_pairs={{0,4},{1,7},{2,6},{3,5},{4,0},{5,3},{6,2},{7,1},{8,12},{9,15},{10,... | collective-permute-start | bytes 196616 | tf_op jit(solution)/shard_map/ppermute | solution.py:32
  20.9 4.6 %collective-permute-start.7 = (bf16[128,256]{1,0:T(8,128)(2,1)S(1)}, bf16[128,256]{1,0:T(8,128)(2,1)S(1)}, u32[]{:S(2)}, u32[]{:S(2)}) collective-permute-start(bf16[128,256]{1,0:T(8,128)(2,1)S(1)} %get-tuple-element.30), channel_id=1, source_target_pairs={{0,8},{1,9},{2,10},{3,11},{4,12},{5,13},{6,14},{7,15},{8,0},{9,1},... | collective-permute-start | bytes 196616 | tf_op jit(solution)/shard_map/ppermute | solution.py:32
  22.4 4.3 %collective-permute-start.13 = (f32[128,256]{1,0:T(8,128)S(1)}, f32[128,256]{1,0:T(8,128)S(1)}, u32[]{:S(2)}, u32[]{:S(2)}) collective-permute-start(f32[128,256]{1,0:T(8,128)S(1)} %collective-permute-done.12.refs_6_), channel_id=1, source_target_pairs={{0,1},{1,0},{2,3},{3,2},{4,5},{5,4},{6,7},{7,6},{8,9},{9,8},{10,11... | collective-permute-start | bytes 393224 | tf_op jit(solution)/shard_map/ppermute | solution.py:21
  23.7 3.1 %collective-permute-start.8 = (bf16[2,128,256]{2,1,0:T(8,128)(2,1)S(1)}, bf16[2,128,256]{2,1,0:T(8,128)(2,1)S(1)}, u32[]{:S(2)}, u32[]{:S(2)}) collective-permute-start(bf16[2,128,256]{2,1,0:T(8,128)(2,1)S(1)} %collective-permute-done.6.refs_1_), channel_id=1, source_target_pairs={{0,1},{1,0},{2,3},{3,2},{4,5},{5,4},{6,7},{7,6},{8,9},{9,8},{10,11... | collective-permute-start | bytes 393224 | tf_op jit(solution)/shard_map/ppermute | solution.py:21
  25.4 1.3 %collective-permute-start.11 = (bf16[2,128,128]{2,1,0:T(8,128)(2,1)S(1)}, bf16[2,128,128]{2,1,0:T(8,128)(2,1)S(1)}, u32[]{:S(2)}, u32[]{:S(2)}) collective-permute-start(bf16[2,128,128]{2,1,0:T(8,128)(2,1)S(1)} %collective-permute-done.10.refs_5_), channel_id=1, source_target_pairs={{0,1},{1,0},{2,3},{3,2},{4,5},{5,4},{6,7},{7,6},{8,9},{9,8},{10,11... | collective-permute-start | bytes 196616 | tf_op jit(solution)/shard_map/ppermute | solution.py:21
  25.4 1.4 %collective-permute-start.9 = (bf16[128,256]{1,0:T(8,128)(2,1)S(1)}, bf16[128,256]{1,0:T(8,128)(2,1)S(1)}, u32[]{:S(2)}, u32[]{:S(2)}) collective-permute-start(bf16[128,256]{1,0:T(8,128)(2,1)S(1)} %collective-permute-done.7.refs_2_), channel_id=1, source_target_pairs={{0,1},{1,0},{2,3},{3,2},{4,5},{5,4},{6,7},{7,6},{8,9},{9,8},{10,11... | collective-permute-start | bytes 196616 | tf_op jit(solution)/shard_map/ppermute | solution.py:21
  27.0 8.7 %collective-permute-start.14 = (bf16[2,128,256]{2,1,0:T(8,128)(2,1)S(1)}, bf16[2,128,256]{2,1,0:T(8,128)(2,1)S(1)}, u32[]{:S(2)}, u32[]{:S(2)}) collective-permute-start(bf16[2,128,256]{2,1,0:T(8,128)(2,1)S(1)} %get-tuple-element.32.refs_0_), channel_id=1, source_target_pairs={{0,4},{1,7},{2,6},{3,5},{4,0},{5,3},{6,2},{7,1},{8,12},{9,15},{10,... | collective-permute-start | bytes 393224 | tf_op jit(solution)/shard_map/ppermute | solution.py:32
  29.5 8.0 %collective-permute-start.18 = (bf16[4,128,128]{2,1,0:T(8,128)(2,1)S(1)}, bf16[4,128,128]{2,1,0:T(8,128)(2,1)S(1)}, u32[]{:S(2)}, u32[]{:S(2)}) collective-permute-start(bf16[4,128,128]{2,1,0:T(8,128)(2,1)S(1)} %get-tuple-element.39), channel_id=1, source_target_pairs={{0,8},{8,0},{16,24},{24,16},{1,9},{9,1},{17,25},{25,17},{2,10},{10... | collective-permute-start | bytes 393224 | tf_op jit(solution)/shard_map/ppermute | solution.py:21
  30.4 9.2 %collective-permute-start.19 = (bf16[4,128,128]{2,1,0:T(8,128)(2,1)S(1)}, bf16[4,128,128]{2,1,0:T(8,128)(2,1)S(1)}, u32[]{:S(2)}, u32[]{:S(2)}) collective-permute-start(bf16[4,128,128]{2,1,0:T(8,128)(2,1)S(1)} %get-tuple-element.40), channel_id=1, source_target_pairs={{0,16},{8,24},{16,0},{24,8},{1,17},{9,25},{17,1},{25,9},{2,18},{10... | collective-permute-start | bytes 393224 | tf_op jit(solution)/shard_map/ppermute | solution.py:21
  31.9 7.7 %collective-permute-start.20 = (bf16[4,128,128]{2,1,0:T(8,128)(2,1)S(1)}, bf16[4,128,128]{2,1,0:T(8,128)(2,1)S(1)}, u32[]{:S(2)}, u32[]{:S(2)}) collective-permute-start(bf16[4,128,128]{2,1,0:T(8,128)(2,1)S(1)} %get-tuple-element.41), channel_id=1, source_target_pairs={{0,24},{8,16},{16,8},{24,0},{1,25},{9,17},{17,9},{25,1},{2,26},{10... | collective-permute-start | bytes 393224 | tf_op jit(solution)/shard_map/ppermute | solution.py:21
  33.0 4.5 %collective-permute-start.15 = (bf16[128,256]{1,0:T(8,128)(2,1)S(1)}, bf16[128,256]{1,0:T(8,128)(2,1)S(1)}, u32[]{:S(2)}, u32[]{:S(2)}) collective-permute-start(bf16[128,256]{1,0:T(8,128)(2,1)S(1)} %get-tuple-element.33), channel_id=1, source_target_pairs={{0,2},{1,3},{2,0},{3,1},{4,6},{5,7},{6,4},{7,5},{8,10},{9,11},{10,... | collective-permute-start | bytes 196616 | tf_op jit(solution)/shard_map/ppermute | solution.py:32
  35.7 4.0 %collective-permute-start.16 = (bf16[2,128,256]{2,1,0:T(8,128)(2,1)S(1)}, bf16[2,128,256]{2,1,0:T(8,128)(2,1)S(1)}, u32[]{:S(2)}, u32[]{:S(2)}) collective-permute-start(bf16[2,128,256]{2,1,0:T(8,128)(2,1)S(1)} %collective-permute-done.14.refs_1_), channel_id=1, source_target_pairs={{0,1},{1,0},{2,3},{3,2},{4,5},{5,4},{6,7},{7,6},{8,9},{9,8},{10,11... | collective-permute-start | bytes 393224 | tf_op jit(solution)/shard_map/ppermute | solution.py:21
  37.5 2.1 %collective-permute-start.17 = (bf16[128,256]{1,0:T(8,128)(2,1)S(1)}, bf16[128,256]{1,0:T(8,128)(2,1)S(1)}, u32[]{:S(2)}, u32[]{:S(2)}) collective-permute-start(bf16[128,256]{1,0:T(8,128)(2,1)S(1)} %collective-permute-done.15.refs_2_), channel_id=1, source_target_pairs={{0,1},{1,0},{2,3},{3,2},{4,5},{5,4},{6,7},{7,6},{8,9},{9,8},{10,11... | collective-permute-start | bytes 196616 | tf_op jit(solution)/shard_map/ppermute | solution.py:21

commit v7 on v6

--- a/solution.py
+++ b/solution.py
@@ -281,7 +281,7 @@
         cost_estimate=busy(32),
         name="backward_blocks",
     )(rows, cols, block_counts, values, pair, *seen, *passed)
-    after = passed
+    after = [own]
     weight, weight_half = pl.pallas_call(
         functools.partial(weight_rows_kernel, row_peers),
         out_shape=[shaped((2, width, hidden), BF16), shaped((width, hidden), BF16)],

time: 40.7 us -> 40.3 us (level)
  starting transfers between devices: 19.1 us -> 18.5 us
    ppermute x6, waiting for transfers between devices: 5.73 us -> 6.99 us  [split_permute(): return lax.ppermute(x, ('row', 'col'), pairs)]
    ppermute x15, waiting for transfers between devices: 9.36 us -> 8.24 us  [xor_permute(): return lax.ppermute(x, axis, [(i, i ^ distance) for i in range(total)])]
  transfers between devices with their start and end apart: 21 -> 21, of which waited for: 11 -> 12; matrix products, arithmetic and copies ran while one was open for 0% -> 0% of each run, Pallas kernels for 3% -> 3%
where the time goes in v7:
time: 40.3 us; the launch traced here: 40.2 us
  starting transfers between devices  18.5 us (46%)
  waiting for transfers between devices  15.2 us (38%)
  Pallas kernels  4.91 us (12%)
  between operations  1.42 us (4%)
    ppermute x15, starting transfers between devices, xor_permute(): return lax.ppermute(x, axis, [(i, i ^ distance) for i in range(total)])  10.5 us
    ppermute x15, waiting for transfers between devices, xor_permute(): return lax.ppermute(x, axis, [(i, i ^ distance) for i in range(total)])  8.24 us
    ppermute x6, starting transfers between devices, split_permute(): return lax.ppermute(x, ('row', 'col'), pairs)  8.04 us
    ppermute x6, waiting for transfers between devices, split_permute(): return lax.ppermute(x, ('row', 'col'), pairs)  6.99 us
    pallas_call x1, Pallas kernels, per_device(): pl.pallas_call(forward_kernel, out_shape=[shaped((pairs, block, width), F...  2.21 us
    pallas_call x1, Pallas kernels, per_device(): pl.pallas_call(functools.partial(backward_kernel, col_peers, groups), out...  1.18 us
    pallas_call x1, Pallas kernels, per_device(): pl.pallas_call(functools.partial(final_kernel, scale, col_peers, groups),...  0.94 us
  transfers between devices with their start and end apart: 21, of which 12 were waited for; matrix products, arithmetic and copies ran while one was open for 0% of the time, Pallas kernels for 3%

profile of v7, /device:TPU:0, one launch (start us, length us, event | category | flops | bytes accessed | tf_op | source)
XLA Modules:
  0.0 40.2 jit_solution(15580604955538807441)
XLA Ops:
  1.3 2.2 %forward_blocks.1 = (f32[4,128,128]{2,1,0:T(8,128)S(1)}, f32[4,128,128]{2,1,0:T(8,128)S(1)}, s32[1,1,32]{2,1,0:T(1,128)S(1)}, s32[1,1,32]{2,1,0:T(1,128)S(1)}, bf16[1,1,32,128,128]{4,3,2,1,0:T(8,128)(2,1)S(1)}) custom-call(s32[1,1,32]{2,1,0:T(1,128)} %rows_in.1, s32[1,1,32]{2,1,0:T(1,128)} %cols_in.1, s32[1,1]{1,0:T(1,128)S(6)} %copy.13.counts.refs_2_, ...), custom_call_target="tpu_custom_call" | custom-call | tf_op jit(solution)/shard_map/forward_blocks/pallas_call | solution.py:211
  3.5 0.5 %collective-permute-start = (f32[4,128,128]{2,1,0:T(8,128)S(1)}, f32[4,128,128]{2,1,0:T(8,128)S(1)}, u32[]{:S(2)}, u32[]{:S(2)}) collective-permute-start(f32[4,128,128]{2,1,0:T(8,128)S(1)} %get-tuple-element.26), channel_id=1, source_target_pairs={{0,1},{1,0},{2,3},{3,2},{4,5},{5,4},{6,7},{7,6},{8,9},{9,8},{10,11... | collective-permute-start | bytes 786440 | tf_op jit(solution)/shard_map/ppermute | solution.py:21
  4.0 1.2 %collective-permute-done = f32[4,128,128]{2,1,0:T(8,128)S(1)} collective-permute-done((f32[4,128,128]{2,1,0:T(8,128)S(1)}, f32[4,128,128]{2,1,0:T(8,128)S(1)}, u32[]{:S(2)}, u32[]{:S(2)}) %collective-permute-start) | collective-permute-done | bytes 262176 | tf_op jit(solution)/shard_map/ppermute | solution.py:21
  5.2 0.0 copy-start.2
  5.2 0.0 copy-start.3
  5.3 5.0 %collective-permute-start.3 = (bf16[128,128]{1,0:T(8,128)(2,1)S(1)}, bf16[128,128]{1,0:T(8,128)(2,1)S(1)}, u32[]{:S(2)}, u32[]{:S(2)}) collective-permute-start(bf16[128,128]{1,0:T(8,128)(2,1)S(1)} %get-tuple-element.48), channel_id=1, source_target_pairs={{0,6},{1,7},{2,4},{3,5},{4,2},{5,3},{6,0},{7,1},{8,14},{9,15},{10,... | collective-permute-start | bytes 98312 | tf_op jit(solution)/shard_map/ppermute | solution.py:21
  10.3 0.0 collective-permute-start.2
  10.3 0.6 %collective-permute-start.1 = (bf16[128,128]{1,0:T(8,128)(2,1)S(1)}, bf16[128,128]{1,0:T(8,128)(2,1)S(1)}, u32[]{:S(2)}, u32[]{:S(2)}) collective-permute-start(bf16[128,128]{1,0:T(8,128)(2,1)S(1)} %get-tuple-element.50), channel_id=1, source_target_pairs={{0,2},{1,3},{2,0},{3,1},{4,6},{5,7},{6,4},{7,5},{8,10},{9,11},{10,... | collective-permute-start | bytes 98312 | tf_op jit(solution)/shard_map/ppermute | solution.py:21
  11.0 1.3 %collective-permute-done.3.refs_3_ = bf16[128,128]{1,0:T(8,128)(2,1)S(1)} collective-permute-done((bf16[128,128]{1,0:T(8,128)(2,1)S(1)}, bf16[128,128]{1,0:T(8,128)(2,1)S(1)}, u32[]{:S(2)}, u32[]{:S(2)}) %collective-permute-start.3) | collective-permute-done | bytes 32800 | tf_op jit(solution)/shard_map/ppermute | solution.py:21
  12.2 2.9 %collective-permute-done.2.refs_2_ = bf16[128,128]{1,0:T(8,128)(2,1)S(1)} collective-permute-done((bf16[128,128]{1,0:T(8,128)(2,1)S(1)}, bf16[128,128]{1,0:T(8,128)(2,1)S(1)}, u32[]{:S(2)}, u32[]{:S(2)}) %collective-permute-start.2) | collective-permute-done | bytes 32800 | tf_op jit(solution)/shard_map/ppermute | solution.py:21
  15.1 0.0 collective-permute-done.1.refs_1_
  15.1 0.4 %dense_layer.1 = (bf16[128,256]{1,0:T(8,128)(2,1)S(1)}, bf16[128,128]{1,0:T(8,128)(2,1)S(1)}, f32[128,256]{1,0:T(8,128)S(1)}, f32[2,128,256]{2,1,0:T(8,128)S(1)}) custom-call(f32[128,128]{1,0:T(8,128)S(1)} %slice_bitcast_fusion.refs_0_, bf16[128,128]{1,0:T(8,128)(2,1)S(1)} %collective-permute-done.1.refs_1_, ...), custom_call_target="tpu_custom_call" | custom-call | tf_op jit(solution)/shard_map/dense_layer/pallas_call | solution.py:234
  15.6 0.1 collective-permute-start.4
  15.6 0.5 %collective-permute-start.5 = (bf16[128,128]{1,0:T(8,128)(2,1)S(1)}, bf16[128,128]{1,0:T(8,128)(2,1)S(1)}, u32[]{:S(2)}, u32[]{:S(2)}) collective-permute-start(bf16[128,128]{1,0:T(8,128)(2,1)S(1)} %get-tuple-element.28.mine), channel_id=1, source_target_pairs={{0,1},{1,0},{2,3},{3,2},{4,5},{5,4},{6,7},{7,6},{8,9},{9,8},{10,11... | collective-permute-start | bytes 98312 | tf_op jit(solution)/shard_map/ppermute | solution.py:21
  16.1 0.0 collective-permute-start.11
  16.2 1.1 %collective-permute-done.5.theirs = bf16[128,128]{1,0:T(8,128)(2,1)S(1)} collective-permute-done((bf16[128,128]{1,0:T(8,128)(2,1)S(1)}, bf16[128,128]{1,0:T(8,128)(2,1)S(1)}, u32[]{:S(2)}, u32[]{:S(2)}) %collective-permute-start.5) | collective-permute-done | bytes 32800 | tf_op jit(solution)/shard_map/ppermute | solution.py:21
  17.2 0.0 collective-permute-done.4.theirs
  17.3 1.6 %collective-permute-start.6 = (bf16[2,128,256]{2,1,0:T(8,128)(2,1)S(1)}, bf16[2,128,256]{2,1,0:T(8,128)(2,1)S(1)}, u32[]{:S(2)}, u32[]{:S(2)}) collective-permute-start(bf16[2,128,256]{2,1,0:T(8,128)(2,1)S(1)} %get-tuple-element.29.refs_0_), channel_id=1, source_target_pairs={{0,16},{1,25},{2,18},{3,27},{4,20},{5,29},{6,22},{7,31},{8,24},{9,... | collective-permute-start | bytes 393224 | tf_op jit(solution)/shard_map/ppermute | solution.py:32
  18.9 2.0 %collective-permute-start.10 = (bf16[2,128,128]{2,1,0:T(8,128)(2,1)S(1)}, bf16[2,128,128]{2,1,0:T(8,128)(2,1)S(1)}, u32[]{:S(2)}, u32[]{:S(2)}) collective-permute-start(bf16[2,128,128]{2,1,0:T(8,128)(2,1)S(1)} %gradient_pair.1.rest_0_.refs_4_), channel_id=1, source_target_pairs={{0,4},{1,7},{2,6},{3,5},{4,0},{5,3},{6,2},{7,1},{8,12},{9,15},{10,... | collective-permute-start | bytes 196616 | tf_op jit(solution)/shard_map/ppermute | solution.py:32
  20.9 0.7 %collective-permute-done.11.refs_6_ = f32[128,256]{1,0:T(8,128)S(1)} collective-permute-done((f32[128,256]{1,0:T(8,128)S(1)}, f32[128,256]{1,0:T(8,128)S(1)}, u32[]{:S(2)}, u32[]{:S(2)}) %collective-permute-start.11) | collective-permute-done | bytes 131104 | tf_op jit(solution)/shard_map/ppermute | solution.py:32
  21.6 0.0 collective-permute-start.13
  21.6 1.5 %collective-permute-start.7 = (bf16[128,256]{1,0:T(8,128)(2,1)S(1)}, bf16[128,256]{1,0:T(8,128)(2,1)S(1)}, u32[]{:S(2)}, u32[]{:S(2)}) collective-permute-start(bf16[128,256]{1,0:T(8,128)(2,1)S(1)} %get-tuple-element.30), channel_id=1, source_target_pairs={{0,8},{1,9},{2,10},{3,11},{4,12},{5,13},{6,14},{7,15},{8,0},{9,1},... | collective-permute-start | bytes 196616 | tf_op jit(solution)/shard_map/ppermute | solution.py:32
  23.1 0.6 %collective-permute-done.6.refs_1_ = bf16[2,128,256]{2,1,0:T(8,128)(2,1)S(1)} collective-permute-done((bf16[2,128,256]{2,1,0:T(8,128)(2,1)S(1)}, bf16[2,128,256]{2,1,0:T(8,128)(2,1)S(1)}, u32[]{:S(2)}, u32[]{:S(2)}) %collective-permute-start.6) | collective-permute-done | bytes 131104 | tf_op jit(solution)/shard_map/ppermute | solution.py:32
  23.7 0.0 collective-permute-start.8
  23.7 1.7 %collective-permute-done.10.refs_5_ = bf16[2,128,128]{2,1,0:T(8,128)(2,1)S(1)} collective-permute-done((bf16[2,128,128]{2,1,0:T(8,128)(2,1)S(1)}, bf16[2,128,128]{2,1,0:T(8,128)(2,1)S(1)}, u32[]{:S(2)}, u32[]{:S(2)}) %collective-permute-start.10) | collective-permute-done | bytes 65568 | tf_op jit(solution)/shard_map/ppermute | solution.py:32
  25.4 0.0 collective-permute-start.12
  25.4 0.7 %collective-permute-done.7.refs_2_ = bf16[128,256]{1,0:T(8,128)(2,1)S(1)} collective-permute-done((bf16[128,256]{1,0:T(8,128)(2,1)S(1)}, bf16[128,256]{1,0:T(8,128)(2,1)S(1)}, u32[]{:S(2)}, u32[]{:S(2)}) %collective-permute-start.7) | collective-permute-done | bytes 65568 | tf_op jit(solution)/shard_map/ppermute | solution.py:32
  26.1 0.0 collective-permute-start.9
  26.1 0.6 %collective-permute-done.12.refs_7_ = bf16[2,128,128]{2,1,0:T(8,128)(2,1)S(1)} collective-permute-done((bf16[2,128,128]{2,1,0:T(8,128)(2,1)S(1)}, bf16[2,128,128]{2,1,0:T(8,128)(2,1)S(1)}, u32[]{:S(2)}, u32[]{:S(2)}) %collective-permute-start.12) | collective-permute-done | bytes 65568 | tf_op jit(solution)/shard_map/ppermute | solution.py:21
  26.7 0.0 collective-permute-done.13.refs_8_
  26.7 1.2 %backward_blocks.1 = (f32[4,128,128]{2,1,0:T(8,128)S(1)}, bf16[4,128,128]{2,1,0:T(8,128)(2,1)S(1)}, bf16[4,128,128]{2,1,0:T(8,128)(2,1)S(1)}, bf16[4,128,128]{2,1,0:T(8,128)(2,1)S(1)}) custom-call(s32[1,1,32]{2,1,0:T(1,128)S(1)} %get-tuple-element.31.refs_0_, s32[1,1,32]{2,1,0:T(1,128)S(1)} %get-tuple-element.32.refs_1_, s32[1,1]{1,0:T(1,128)S(6)} %copy.13.counts.refs_2_, ...), custom_call_target="tpu_custom_call" | custom-call | bytes 33554432 | tf_op jit(solution)/shard_map/backward_blocks/pallas_call | solution.py:270
  27.9 0.0 collective-permute-done.9.refs_4_
  27.9 0.0 collective-permute-done.8.refs_3_
  27.9 0.1 weight_rows.1
  28.0 1.6 %collective-permute-start.14 = (bf16[2,128,256]{2,1,0:T(8,128)(2,1)S(1)}, bf16[2,128,256]{2,1,0:T(8,128)(2,1)S(1)}, u32[]{:S(2)}, u32[]{:S(2)}) collective-permute-start(bf16[2,128,256]{2,1,0:T(8,128)(2,1)S(1)} %get-tuple-element.36.refs_0_), channel_id=1, source_target_pairs={{0,4},{1,7},{2,6},{3,5},{4,0},{5,3},{6,2},{7,1},{8,12},{9,15},{10,... | collective-permute-start | bytes 393224 | tf_op jit(solution)/shard_map/ppermute | solution.py:32
  29.6 1.5 %collective-permute-start.18 = (bf16[4,128,128]{2,1,0:T(8,128)(2,1)S(1)}, bf16[4,128,128]{2,1,0:T(8,128)(2,1)S(1)}, u32[]{:S(2)}, u32[]{:S(2)}) collective-permute-start(bf16[4,128,128]{2,1,0:T(8,128)(2,1)S(1)} %get-tuple-element.39), channel_id=1, source_target_pairs={{0,8},{8,0},{16,24},{24,16},{1,9},{9,1},{17,25},{25,17},{2,10},{10... | collective-permute-start | bytes 393224 | tf_op jit(solution)/shard_map/ppermute | solution.py:21
  31.1 2.2 %collective-permute-start.19 = (bf16[4,128,128]{2,1,0:T(8,128)(2,1)S(1)}, bf16[4,128,128]{2,1,0:T(8,128)(2,1)S(1)}, u32[]{:S(2)}, u32[]{:S(2)}) collective-permute-start(bf16[4,128,128]{2,1,0:T(8,128)(2,1)S(1)} %get-tuple-element.40), channel_id=1, source_target_pairs={{0,16},{8,24},{16,0},{24,8},{1,17},{9,25},{17,1},{25,9},{2,18},{10... | collective-permute-start | bytes 393224 | tf_op jit(solution)/shard_map/ppermute | solution.py:21
  33.3 0.0 collective-permute-start.20
  33.3 1.4 %collective-permute-start.15 = (bf16[128,256]{1,0:T(8,128)(2,1)S(1)}, bf16[128,256]{1,0:T(8,128)(2,1)S(1)}, u32[]{:S(2)}, u32[]{:S(2)}) collective-permute-start(bf16[128,256]{1,0:T(8,128)(2,1)S(1)} %get-tuple-element.37), channel_id=1, source_target_pairs={{0,2},{1,3},{2,0},{3,1},{4,6},{5,7},{6,4},{7,5},{8,10},{9,11},{10,... | collective-permute-start | bytes 196616 | tf_op jit(solution)/shard_map/ppermute | solution.py:32
  34.7 1.9 %collective-permute-done.14.refs_1_ = bf16[2,128,256]{2,1,0:T(8,128)(2,1)S(1)} collective-permute-done((bf16[2,128,256]{2,1,0:T(8,128)(2,1)S(1)}, bf16[2,128,256]{2,1,0:T(8,128)(2,1)S(1)}, u32[]{:S(2)}, u32[]{:S(2)}) %collective-permute-start.14) | collective-permute-done | bytes 131104 | tf_op jit(solution)/shard_map/ppermute | solution.py:32
  36.6 1.3 %collective-permute-done.15.refs_2_ = bf16[128,256]{1,0:T(8,128)(2,1)S(1)} collective-permute-done((bf16[128,256]{1,0:T(8,128)(2,1)S(1)}, bf16[128,256]{1,0:T(8,128)(2,1)S(1)}, u32[]{:S(2)}, u32[]{:S(2)}) %collective-permute-start.15) | collective-permute-done | bytes 65568 | tf_op jit(solution)/shard_map/ppermute | solution.py:32
  37.9 0.0 collective-permute-start.17
  37.9 0.0 collective-permute-done.18.refs_7_
  37.9 1.3 %collective-permute-done.19.refs_8_ = bf16[4,128,128]{2,1,0:T(8,128)(2,1)S(1)} collective-permute-done((bf16[4,128,128]{2,1,0:T(8,128)(2,1)S(1)}, bf16[4,128,128]{2,1,0:T(8,128)(2,1)S(1)}, u32[]{:S(2)}, u32[]{:S(2)}) %collective-permute-start.19) | collective-permute-done | bytes 131104 | tf_op jit(solution)/shard_map/ppermute | solution.py:21
  39.2 0.0 collective-permute-done.20.refs_9_
  39.2 0.0 collective-permute-done.17.refs_4_
  39.2 0.0 collective-permute-done.16.refs_3_
  39.2 0.9 %join_outputs.1 = (bf16[128,256]{1,0:T(8,128)(2,1)}, f32[128,256]{1,0:T(8,128)}, f32[128,256]{1,0:T(8,128)}, f32[512,128]{1,0:T(8,128)}) custom-call(bf16[2,128,256]{2,1,0:T(8,128)(2,1)S(1)} %get-tuple-element.36.refs_0_, bf16[2,128,256]{2,1,0:T(8,128)(2,1)S(1)} %collective-permute-done.14.refs_1_, bf16[128,256]{1,0:T(8,128)(2,1)S(1)} %collective-permute-done.15.refs_2_, ...), custom_call_target="tpu_custom_call" | custom-call | tf_op jit(solution)/shard_map/join_outputs/pallas_call | solution.py:297
  (12 shorter events, 0.1 us)
Async XLA Ops:
  3.5 1.7 %collective-permute-start = (f32[4,128,128]{2,1,0:T(8,128)S(1)}, f32[4,128,128]{2,1,0:T(8,128)S(1)}, u32[]{:S(2)}, u32[]{:S(2)}) collective-permute-start(f32[4,128,128]{2,1,0:T(8,128)S(1)} %get-tuple-element.26), channel_id=1, source_target_pairs={{0,1},{1,0},{2,3},{3,2},{4,5},{5,4},{6,7},{7,6},{8,9},{9,8},{10,11... | collective-permute-start | bytes 786440 | tf_op jit(solution)/shard_map/ppermute | solution.py:21
  5.2 9.9 %copy-start.2 = (bf16[128,256]{1,0:T(8,128)(2,1)S(1)}, bf16[128,256]{1,0:T(8,128)(2,1)}, u32[]{:S(2)}) copy-start(bf16[128,256]{1,0:T(8,128)(2,1)} %refs_7_.1) | copy-start | bytes 196612
  5.2 9.9 %copy-start.3 = (bf16[128,128]{1,0:T(8,128)(2,1)S(1)}, bf16[128,128]{1,0:T(8,128)(2,1)}, u32[]{:S(2)}) copy-start(bf16[128,128]{1,0:T(8,128)(2,1)} %refs_4_.1) | copy-start | bytes 98308
  5.3 7.0 %collective-permute-start.3 = (bf16[128,128]{1,0:T(8,128)(2,1)S(1)}, bf16[128,128]{1,0:T(8,128)(2,1)S(1)}, u32[]{:S(2)}, u32[]{:S(2)}) collective-permute-start(bf16[128,128]{1,0:T(8,128)(2,1)S(1)} %get-tuple-element.48), channel_id=1, source_target_pairs={{0,6},{1,7},{2,4},{3,5},{4,2},{5,3},{6,0},{7,1},{8,14},{9,15},{10,... | collective-permute-start | bytes 98312 | tf_op jit(solution)/shard_map/ppermute | solution.py:21
  10.3 4.8 %collective-permute-start.2 = (bf16[128,128]{1,0:T(8,128)(2,1)S(1)}, bf16[128,128]{1,0:T(8,128)(2,1)S(1)}, u32[]{:S(2)}, u32[]{:S(2)}) collective-permute-start(bf16[128,128]{1,0:T(8,128)(2,1)S(1)} %get-tuple-element.49), channel_id=1, source_target_pairs={{0,4},{1,5},{2,6},{3,7},{4,0},{5,1},{6,2},{7,3},{8,12},{9,13},{10,... | collective-permute-start | bytes 98312 | tf_op jit(solution)/shard_map/ppermute | solution.py:21
  10.3 4.8 %collective-permute-start.1 = (bf16[128,128]{1,0:T(8,128)(2,1)S(1)}, bf16[128,128]{1,0:T(8,128)(2,1)S(1)}, u32[]{:S(2)}, u32[]{:S(2)}) collective-permute-start(bf16[128,128]{1,0:T(8,128)(2,1)S(1)} %get-tuple-element.50), channel_id=1, source_target_pairs={{0,2},{1,3},{2,0},{3,1},{4,6},{5,7},{6,4},{7,5},{8,10},{9,11},{10,... | collective-permute-start | bytes 98312 | tf_op jit(solution)/shard_map/ppermute | solution.py:21
  10.9 4.2 %copy-start = (bf16[128,256]{1,0:T(8,128)(2,1)S(1)}, bf16[128,256]{1,0:T(8,128)(2,1)}, u32[]{:S(2)}) copy-start(bf16[128,256]{1,0:T(8,128)(2,1)} %refs_5_.1) | copy-start | bytes 196612
  10.9 4.2 %copy-start.1 = (bf16[128,256]{1,0:T(8,128)(2,1)S(1)}, bf16[128,256]{1,0:T(8,128)(2,1)}, u32[]{:S(2)}) copy-start(bf16[128,256]{1,0:T(8,128)(2,1)} %refs_6_.1) | copy-start | bytes 196612
  15.6 1.7 %collective-permute-start.4 = (f32[2,128,256]{2,1,0:T(8,128)S(1)}, f32[2,128,256]{2,1,0:T(8,128)S(1)}, u32[]{:S(2)}, u32[]{:S(2)}) collective-permute-start(f32[2,128,256]{2,1,0:T(8,128)S(1)} %get-tuple-element.27.mine), channel_id=1, source_target_pairs={{0,1},{1,0},{2,3},{3,2},{4,5},{5,4},{6,7},{7,6},{8,9},{9,8},{10,11... | collective-permute-start | bytes 786440 | tf_op jit(solution)/shard_map/ppermute | solution.py:21
  15.6 1.6 %collective-permute-start.5 = (bf16[128,128]{1,0:T(8,128)(2,1)S(1)}, bf16[128,128]{1,0:T(8,128)(2,1)S(1)}, u32[]{:S(2)}, u32[]{:S(2)}) collective-permute-start(bf16[128,128]{1,0:T(8,128)(2,1)S(1)} %get-tuple-element.28.mine), channel_id=1, source_target_pairs={{0,1},{1,0},{2,3},{3,2},{4,5},{5,4},{6,7},{7,6},{8,9},{9,8},{10,11... | collective-permute-start | bytes 98312 | tf_op jit(solution)/shard_map/ppermute | solution.py:21
  16.1 5.5 %collective-permute-start.11 = (f32[128,256]{1,0:T(8,128)S(1)}, f32[128,256]{1,0:T(8,128)S(1)}, u32[]{:S(2)}, u32[]{:S(2)}) collective-permute-start(f32[128,256]{1,0:T(8,128)S(1)} %get-tuple-element.34), channel_id=1, source_target_pairs={{0,2},{1,3},{2,0},{3,1},{4,6},{5,7},{6,4},{7,5},{8,10},{9,11},{10,... | collective-permute-start | bytes 393224 | tf_op jit(solution)/shard_map/ppermute | solution.py:32
  17.3 6.4 %collective-permute-start.6 = (bf16[2,128,256]{2,1,0:T(8,128)(2,1)S(1)}, bf16[2,128,256]{2,1,0:T(8,128)(2,1)S(1)}, u32[]{:S(2)}, u32[]{:S(2)}) collective-permute-start(bf16[2,128,256]{2,1,0:T(8,128)(2,1)S(1)} %get-tuple-element.29.refs_0_), channel_id=1, source_target_pairs={{0,16},{1,25},{2,18},{3,27},{4,20},{5,29},{6,22},{7,31},{8,24},{9,... | collective-permute-start | bytes 393224 | tf_op jit(solution)/shard_map/ppermute | solution.py:32
  18.9 6.6 %collective-permute-start.10 = (bf16[2,128,128]{2,1,0:T(8,128)(2,1)S(1)}, bf16[2,128,128]{2,1,0:T(8,128)(2,1)S(1)}, u32[]{:S(2)}, u32[]{:S(2)}) collective-permute-start(bf16[2,128,128]{2,1,0:T(8,128)(2,1)S(1)} %gradient_pair.1.rest_0_.refs_4_), channel_id=1, source_target_pairs={{0,4},{1,7},{2,6},{3,5},{4,0},{5,3},{6,2},{7,1},{8,12},{9,15},{10,... | collective-permute-start | bytes 196616 | tf_op jit(solution)/shard_map/ppermute | solution.py:32
  21.6 5.1 %collective-permute-start.13 = (f32[128,256]{1,0:T(8,128)S(1)}, f32[128,256]{1,0:T(8,128)S(1)}, u32[]{:S(2)}, u32[]{:S(2)}) collective-permute-start(f32[128,256]{1,0:T(8,128)S(1)} %collective-permute-done.11.refs_6_), channel_id=1, source_target_pairs={{0,1},{1,0},{2,3},{3,2},{4,5},{5,4},{6,7},{7,6},{8,9},{9,8},{10,11... | collective-permute-start | bytes 393224 | tf_op jit(solution)/shard_map/ppermute | solution.py:21
  21.6 4.5 %collective-permute-start.7 = (bf16[128,256]{1,0:T(8,128)(2,1)S(1)}, bf16[128,256]{1,0:T(8,128)(2,1)S(1)}, u32[]{:S(2)}, u32[]{:S(2)}) collective-permute-start(bf16[128,256]{1,0:T(8,128)(2,1)S(1)} %get-tuple-element.30), channel_id=1, source_target_pairs={{0,8},{1,9},{2,10},{3,11},{4,12},{5,13},{6,14},{7,15},{8,0},{9,1},... | collective-permute-start | bytes 196616 | tf_op jit(solution)/shard_map/ppermute | solution.py:32
  23.7 4.2 %collective-permute-start.8 = (bf16[2,128,256]{2,1,0:T(8,128)(2,1)S(1)}, bf16[2,128,256]{2,1,0:T(8,128)(2,1)S(1)}, u32[]{:S(2)}, u32[]{:S(2)}) collective-permute-start(bf16[2,128,256]{2,1,0:T(8,128)(2,1)S(1)} %collective-permute-done.6.refs_1_), channel_id=1, source_target_pairs={{0,1},{1,0},{2,3},{3,2},{4,5},{5,4},{6,7},{7,6},{8,9},{9,8},{10,11... | collective-permute-start | bytes 393224 | tf_op jit(solution)/shard_map/ppermute | solution.py:21
  25.4 1.3 %collective-permute-start.12 = (bf16[2,128,128]{2,1,0:T(8,128)(2,1)S(1)}, bf16[2,128,128]{2,1,0:T(8,128)(2,1)S(1)}, u32[]{:S(2)}, u32[]{:S(2)}) collective-permute-start(bf16[2,128,128]{2,1,0:T(8,128)(2,1)S(1)} %collective-permute-done.10.refs_5_), channel_id=1, source_target_pairs={{0,1},{1,0},{2,3},{3,2},{4,5},{5,4},{6,7},{7,6},{8,9},{9,8},{10,11... | collective-permute-start | bytes 196616 | tf_op jit(solution)/shard_map/ppermute | solution.py:21
  26.1 1.8 %collective-permute-start.9 = (bf16[128,256]{1,0:T(8,128)(2,1)S(1)}, bf16[128,256]{1,0:T(8,128)(2,1)S(1)}, u32[]{:S(2)}, u32[]{:S(2)}) collective-permute-start(bf16[128,256]{1,0:T(8,128)(2,1)S(1)} %collective-permute-done.7.refs_2_), channel_id=1, source_target_pairs={{0,1},{1,0},{2,3},{3,2},{4,5},{5,4},{6,7},{7,6},{8,9},{9,8},{10,11... | collective-permute-start | bytes 196616 | tf_op jit(solution)/shard_map/ppermute | solution.py:21
  28.0 8.6 %collective-permute-start.14 = (bf16[2,128,256]{2,1,0:T(8,128)(2,1)S(1)}, bf16[2,128,256]{2,1,0:T(8,128)(2,1)S(1)}, u32[]{:S(2)}, u32[]{:S(2)}) collective-permute-start(bf16[2,128,256]{2,1,0:T(8,128)(2,1)S(1)} %get-tuple-element.36.refs_0_), channel_id=1, source_target_pairs={{0,4},{1,7},{2,6},{3,5},{4,0},{5,3},{6,2},{7,1},{8,12},{9,15},{10,... | collective-permute-start | bytes 393224 | tf_op jit(solution)/shard_map/ppermute | solution.py:32
  29.6 8.4 %collective-permute-start.18 = (bf16[4,128,128]{2,1,0:T(8,128)(2,1)S(1)}, bf16[4,128,128]{2,1,0:T(8,128)(2,1)S(1)}, u32[]{:S(2)}, u32[]{:S(2)}) collective-permute-start(bf16[4,128,128]{2,1,0:T(8,128)(2,1)S(1)} %get-tuple-element.39), channel_id=1, source_target_pairs={{0,8},{8,0},{16,24},{24,16},{1,9},{9,1},{17,25},{25,17},{2,10},{10... | collective-permute-start | bytes 393224 | tf_op jit(solution)/shard_map/ppermute | solution.py:21
  31.1 8.1 %collective-permute-start.19 = (bf16[4,128,128]{2,1,0:T(8,128)(2,1)S(1)}, bf16[4,128,128]{2,1,0:T(8,128)(2,1)S(1)}, u32[]{:S(2)}, u32[]{:S(2)}) collective-permute-start(bf16[4,128,128]{2,1,0:T(8,128)(2,1)S(1)} %get-tuple-element.40), channel_id=1, source_target_pairs={{0,16},{8,24},{16,0},{24,8},{1,17},{9,25},{17,1},{25,9},{2,18},{10... | collective-permute-start | bytes 393224 | tf_op jit(solution)/shard_map/ppermute | solution.py:21
  33.3 5.9 %collective-permute-start.20 = (bf16[4,128,128]{2,1,0:T(8,128)(2,1)S(1)}, bf16[4,128,128]{2,1,0:T(8,128)(2,1)S(1)}, u32[]{:S(2)}, u32[]{:S(2)}) collective-permute-start(bf16[4,128,128]{2,1,0:T(8,128)(2,1)S(1)} %get-tuple-element.41), channel_id=1, source_target_pairs={{0,24},{8,16},{16,8},{24,0},{1,25},{9,17},{17,9},{25,1},{2,26},{10... | collective-permute-start | bytes 393224 | tf_op jit(solution)/shard_map/ppermute | solution.py:21
  33.3 4.6 %collective-permute-start.15 = (bf16[128,256]{1,0:T(8,128)(2,1)S(1)}, bf16[128,256]{1,0:T(8,128)(2,1)S(1)}, u32[]{:S(2)}, u32[]{:S(2)}) collective-permute-start(bf16[128,256]{1,0:T(8,128)(2,1)S(1)} %get-tuple-element.37), channel_id=1, source_target_pairs={{0,2},{1,3},{2,0},{3,1},{4,6},{5,7},{6,4},{7,5},{8,10},{9,11},{10,... | collective-permute-start | bytes 196616 | tf_op jit(solution)/shard_map/ppermute | solution.py:32
  36.6 2.6 %collective-permute-start.16 = (bf16[2,128,256]{2,1,0:T(8,128)(2,1)S(1)}, bf16[2,128,256]{2,1,0:T(8,128)(2,1)S(1)}, u32[]{:S(2)}, u32[]{:S(2)}) collective-permute-start(bf16[2,128,256]{2,1,0:T(8,128)(2,1)S(1)} %collective-permute-done.14.refs_1_), channel_id=1, source_target_pairs={{0,1},{1,0},{2,3},{3,2},{4,5},{5,4},{6,7},{7,6},{8,9},{9,8},{10,11... | collective-permute-start | bytes 393224 | tf_op jit(solution)/shard_map/ppermute | solution.py:21
  37.9 1.3 %collective-permute-start.17 = (bf16[128,256]{1,0:T(8,128)(2,1)S(1)}, bf16[128,256]{1,0:T(8,128)(2,1)S(1)}, u32[]{:S(2)}, u32[]{:S(2)}) collective-permute-start(bf16[128,256]{1,0:T(8,128)(2,1)S(1)} %collective-permute-done.15.refs_2_), channel_id=1, source_target_pairs={{0,1},{1,0},{2,3},{3,2},{4,5},{5,4},{6,7},{7,6},{8,9},{9,8},{10,11... | collective-permute-start | bytes 196616 | tf_op jit(solution)/shard_map/ppermute | solution.py:21
